TPU v7x, 32 devices: a whole 2x2x4 slice. The times are simulated.
32 devices in a mesh: shot: 2 (over y), slab: 4 (over z), rep: 2 (over x), sub: 2 (over core).
Axes of the slice: x: 2, y: 2, z: 4, core: 2. Of those that a mesh axis runs over, the one named last changes fastest.
Arguments:
- courant: float32 [16, 32, 256], P('slab', 'sub'), may hold values from 0.2 to 0.42
- incident_prev: float32 [32, 32, 256], P(('shot', 'slab'), 'sub', 'rep'), parts along dimension 0, may hold values from -6 to 6
- incident_now: float32 [32, 32, 256], P(('shot', 'slab'), 'sub', 'rep'), parts along dimension 0, may hold values from -6 to 6
- wavelet: float32 [4, 8], replicated, may hold values from -6 to 6
- source_z: int32 [16], P('shot'), parts along dimension 0, may hold values from 0 to 15
- source_y: int32 [16], P('shot'), parts along dimension 0, may hold values from 0 to 31
- source_x: int32 [16], P('shot'), parts along dimension 0, may hold values from 0 to 255
- replica_seeds: int32 [4], P('rep'), may hold values from 0 to 999999
- receiver_z: int32 [32], replicated, may hold values from 0 to 15, as said below
- receiver_y: int32 [32], replicated, may hold values from 0 to 31, as said below
- receiver_x: int32 [32], replicated, may hold values from 0 to 255, as said below
Outputs:
- incident_final: float32 [32, 32, 256], P(('shot', 'slab'), 'sub', 'rep'), parts along dimension 0
- scattered_final: float32 [4, 32, 32, 256], P('rep', ('shot', 'slab'), 'sub'), parts along dimension 1
- traces: float32 [8, 4, 32], P('shot', 'rep'), parts along dimension 0
There are 2 independent parts, one for each index of `shot`. A program takes and returns all parts, laid end to end along the dimension named above; an argument that names none is the same for every part. Nothing has to cross between parts.
Inputs may be any that keep to these rules, and one draw needn't show every extreme that they name: `receiver_z`: receiver j lies at a depth from (j // 8) * 4 to that plus 4 - 1; the first receiver is at depth 0 and the last at depth 16 - 1. `receiver_y`: receiver j lies at a second coordinate from ((j // 4) % 2) * 16 to that plus 16 - 1; the first receiver is at 0 and the last at 31. `receiver_x`: the first receiver is at 0 and the last at 255.
All inputs are finite; a program needn't handle non-finite values.
Results may differ from a plain program's by a relative error of at most 0.00002.
Values sent between devices are 32-bit elements; how exact they have to be, the bound alone decides.
No kernel may reach another device: no remote copies, remote signals or barrier semaphores. Data moves between devices by JAX's collectives and lax.ppermute only.
A program may use at most 64 MiB of HBM per device.

v0:
```python
import jax
import jax.numpy as jnp
from jax import lax
from jax.sharding import PartitionSpec as P

STEPS = 4


stencil_coeffs = (-205.0 / 72.0, 8.0 / 5.0, -1.0 / 5.0, 8.0 / 315.0, -1.0 / 560.0)
pert_scale = 0.2


def padded_2(array, sides, width):
    for axis, dim in sides:
        size, length = (lax.axis_size(axis), array.shape[dim])
        up = [(i, (i + 1) % size) for i in range(size - 1)]
        down = [(j, i) for i, j in up]
        last = lax.slice_in_dim(array, length - width, length, axis=dim)
        first = lax.slice_in_dim(array, 0, width, axis=dim)
        before = lax.ppermute(last, axis, up)
        after = lax.ppermute(first, axis, down)
        array = jnp.concatenate([before, array, after], axis=dim)
    return array


def laplace(padded):
    deep_count = padded.shape[-3] - 8
    tall_count = padded.shape[-2] - 8
    wide_count = padded.shape[-1] - 8

    def window(shift_z, shift_y, shift_x):
        return padded[
            ...,
            4 + shift_z : 4 + shift_z + deep_count,
            4 + shift_y : 4 + shift_y + tall_count,
            4 + shift_x : 4 + shift_x + wide_count,
        ]

    summed = 3.0 * stencil_coeffs[0] * window(0, 0, 0)
    for offset in range(1, 5):
        couple = (
            window(offset, 0, 0)
            + window(-offset, 0, 0)
            + window(0, offset, 0)
            + window(0, -offset, 0)
            + window(0, 0, offset)
            + window(0, 0, -offset)
        )
        summed = summed + stencil_coeffs[offset] * couple
    return summed


def perturbation(seed_values, depth_coord, height_coord, width_coord):
    hashed = (
        seed_values[:, None, None, None] * 668265263
        + depth_coord[None, :, None, None] * 73856093
        + height_coord[None, None, :, None] * 19349663
        + width_coord[None, None, None, :] * 83492791
    )
    hashed = jnp.bitwise_xor(hashed, jnp.right_shift(hashed, 15))
    hashed = hashed * 1274126177
    hashed = jnp.bitwise_xor(hashed, jnp.right_shift(hashed, 13))
    fraction = jnp.bitwise_and(hashed, 65535).astype(jnp.float32) / 65535.0
    return pert_scale * (2.0 * fraction - 1.0)


def inject(field, amounts, where_z, where_y, where_x, start_z, start_y, start_x):
    local_z = where_z - start_z
    local_y = where_y - start_y
    local_x = where_x - start_x
    inside = (
        (local_z >= 0)
        & (local_z < field.shape[0])
        & (local_y >= 0)
        & (local_y < field.shape[1])
        & (local_x >= 0)
        & (local_x < field.shape[2])
    )
    clip_z = jnp.clip(local_z, 0, field.shape[0] - 1)
    clip_y = jnp.clip(local_y, 0, field.shape[1] - 1)
    clip_x = jnp.clip(local_x, 0, field.shape[2] - 1)
    return field.at[clip_z, clip_y, clip_x].add(jnp.where(inside, amounts, jnp.zeros_like(amounts)))


def sample(field, where_z, where_y, where_x, start_z, start_y):
    local_z = where_z - start_z
    local_y = where_y - start_y
    inside = (
        (local_z >= 0) & (local_z < field.shape[1]) & (local_y >= 0) & (local_y < field.shape[2])
    )
    clip_z = jnp.clip(local_z, 0, field.shape[1] - 1)
    clip_y = jnp.clip(local_y, 0, field.shape[2] - 1)
    picked = field[:, clip_z, clip_y, where_x]
    return jnp.where(inside[None, :], picked, jnp.zeros_like(picked))


def shards(
    courant,
    incident_prev,
    incident_now,
    wavelet,
    source_z,
    source_y,
    source_x,
    replica_seeds,
    receiver_z,
    receiver_y,
    receiver_x,
):
    deep_count, tall_count, part_width = incident_now.shape
    full_width = courant.shape[2]
    start_z = lax.axis_index("slab") * deep_count
    start_y = lax.axis_index("sub") * tall_count
    start_x = lax.axis_index("rep") * part_width
    speed_square = courant * courant
    depth_coord = start_z + jnp.arange(deep_count, dtype=jnp.int32)
    height_coord = start_y + jnp.arange(tall_count, dtype=jnp.int32)
    width_coord = jnp.arange(full_width, dtype=jnp.int32)
    contrast = perturbation(replica_seeds, depth_coord, height_coord, width_coord)
    whole_prev, whole_now = (
        lax.all_gather(incident_prev, "rep", axis=2, tiled=True),
        lax.all_gather(incident_now, "rep", axis=2, tiled=True),
    )
    wave_prev = jnp.zeros(contrast.shape, jnp.float32)
    wave_now = jnp.zeros(contrast.shape, jnp.float32)
    recorded = []
    for step_index in range(STEPS):
        padded = padded_2(whole_now, (("slab", 0), ("sub", 1)), 4)
        padded = jnp.pad(padded, ((0, 0), (0, 0), (4, 4)))
        whole_next = 2.0 * whole_now - whole_prev + speed_square * laplace(padded)
        whole_next = inject(
            whole_next, wavelet[step_index], source_z, source_y, source_x, start_z, start_y, 0
        )
        wave_padded = padded_2(wave_now, (("slab", 1), ("sub", 2)), 4)
        wave_padded = jnp.pad(wave_padded, ((0, 0), (0, 0), (0, 0), (4, 4)))
        source_term = 2.0 * contrast * (whole_next - 2.0 * whole_now + whole_prev)
        whole_prev, whole_now = (whole_now, whole_next)
        wave_next = 2.0 * wave_now - wave_prev + speed_square * laplace(wave_padded) + source_term
        picked = sample(wave_next, receiver_z, receiver_y, receiver_x, start_z, start_y)
        picked = lax.psum(picked, ("slab", "sub"))
        recorded.append(picked)
        wave_prev, wave_now = (wave_now, wave_next)
    traces = jnp.stack(recorded)
    incident_final = lax.dynamic_slice_in_dim(whole_now, start_x, part_width, 2)
    return (incident_final, wave_now, traces)


def solution(mesh):
    return jax.shard_map(
        shards,
        mesh=mesh,
        in_specs=(
            P("slab", "sub", None),
            P(("shot", "slab"), "sub", "rep"),
            P(("shot", "slab"), "sub", "rep"),
            P(),
            P("shot"),
            P("shot"),
            P("shot"),
            P("rep"),
            P(),
            P(),
            P(),
        ),
        out_specs=(
            P(("shot", "slab"), "sub", "rep"),
            P("rep", ("shot", "slab"), "sub", None),
            P("shot", "rep", None),
        ),
        check_vma=False,
    )
```

profile of v0, /device:TPU:0, one launch (start us, length us, event | category | flops | bytes accessed | tf_op | source)
XLA Modules:
  0.0 163.0 jit_solution(7642810173162248113)
XLA Ops:
  0.6 5.9 %all_gather.6 = f32[4,16,256]{2,1,0:T(8,128)S(1)} all-gather(f32[4,16,128]{2,1,0:T(8,128)} %param.13), channel_id=1, replica_groups=mesh['shot'=2,'slab'=4,'rep'=2,'sub'=2] {'rep'}, dimensions={2}, use_global_device_ids=true | all-gather | bytes 98304 | tf_op jit(solution)/shard_map/all_gather | solution.py:122
  6.5 4.0 %collective-permute-start.1 = (f32[4,16,256]{2,1,0:T(8,128)S(1)}, f32[4,16,256]{2,1,0:T(8,128)S(1)}, u32[]{:S(2)}, u32[]{:S(2)}) collective-permute-start(f32[4,16,256]{2,1,0:T(8,128)S(1)} %all_gather.6), channel_id=1, source_target_pairs={{0,4},{4,8},{8,12},{1,5},{5,9},{9,13},{2,6},{6,10},{10,14},{3,7},{... | collective-permute-start | bytes 196616 | tf_op jit(solution)/shard_map/ppermute | solution.py:20
  10.5 1.3 collective-permute-start
  11.8 4.6 %collective-permute-start.17 = (f32[2,4,16,256]{3,2,1,0:T(8,128)S(1)}, f32[2,4,16,256]{3,2,1,0:T(8,128)S(1)}, u32[]{:S(2)}, u32[]{:S(2)}) collective-permute-start(f32[2,4,16,256]{3,2,1,0:T(8,128)S(1)} %broadcast_in_dim.34), channel_id=1, source_target_pairs={{0,4},{4,8},{8,12},{1,5},{5,9},{9,13},{2,6},{6,10},{10,14},{3,7},{... | collective-permute-start | bytes 393224 | tf_op jit(solution)/shard_map/ppermute | solution.py:20
  16.4 1.3 collective-permute-start.16
  17.7 0.7 fusion.179
  18.4 0.7 bitcast_select_fusion
  19.1 0.8 bitcast_select_fusion.1
  20.7 1.3 collective-permute-start.3
  22.0 1.3 collective-permute-start.2
  23.3 5.0 %all_gather.7 = f32[4,16,256]{2,1,0:T(8,128)S(1)} all-gather(f32[4,16,128]{2,1,0:T(8,128)} %param.12), channel_id=1, replica_groups=mesh['shot'=2,'slab'=4,'rep'=2,'sub'=2] {'rep'}, dimensions={2}, use_global_device_ids=true | all-gather | bytes 98304 | tf_op jit(solution)/shard_map/all_gather | solution.py:121
  28.6 1.0 fusion.157
  29.6 0.9 scatter_fusion
  30.5 4.5 %collective-permute-start.5 = (f32[4,16,256]{2,1,0:T(8,128)S(1)}, f32[4,16,256]{2,1,0:T(8,128)S(1)}, u32[]{:S(2)}, u32[]{:S(2)}) collective-permute-start(f32[4,16,256]{2,1,0:T(8,128)S(1)} %scatter_fusion), channel_id=1, source_target_pairs={{0,4},{4,8},{8,12},{1,5},{5,9},{9,13},{2,6},{6,10},{10,14},{3,7},{... | collective-permute-start | bytes 196616 | tf_op jit(solution)/shard_map/ppermute | solution.py:20
  35.2 1.3 collective-permute-start.4
  37.0 4.3 %collective-permute-done.4 = f32[4,16,256]{2,1,0:T(8,128)S(1)} collective-permute-done((f32[4,16,256]{2,1,0:T(8,128)S(1)}, f32[4,16,256]{2,1,0:T(8,128)S(1)}, u32[]{:S(2)}, u32[]{:S(2)}) %collective-permute-start.4) | collective-permute-done | bytes 65568 | tf_op jit(solution)/shard_map/ppermute | solution.py:21
  41.4 1.3 collective-permute-start.7
  42.7 1.3 collective-permute-start.6
  44.0 1.8 %collective-permute-done.6 = f32[12,4,256]{2,1,0:T(4,128)S(1)} collective-permute-done((f32[12,4,256]{2,1,0:T(4,128)S(1)}, f32[12,4,256]{2,1,0:T(4,128)S(1)}, u32[]{:S(2)}, u32[]{:S(2)}) %collective-permute-start.6) | collective-permute-done | bytes 49184 | tf_op jit(solution)/shard_map/ppermute | solution.py:21
  46.0 1.0 fusion.145
  47.1 0.9 scatter_fusion.1
  48.0 3.5 %collective-permute-start.9 = (f32[4,16,256]{2,1,0:T(8,128)S(1)}, f32[4,16,256]{2,1,0:T(8,128)S(1)}, u32[]{:S(2)}, u32[]{:S(2)}) collective-permute-start(f32[4,16,256]{2,1,0:T(8,128)S(1)} %scatter_fusion.1), channel_id=1, source_target_pairs={{0,4},{4,8},{8,12},{1,5},{5,9},{9,13},{2,6},{6,10},{10,14},{3,7},{... | collective-permute-start | bytes 196616 | tf_op jit(solution)/shard_map/ppermute | solution.py:20
  51.6 1.3 collective-permute-start.8
  53.4 4.3 %collective-permute-done.8 = f32[4,16,256]{2,1,0:T(8,128)S(1)} collective-permute-done((f32[4,16,256]{2,1,0:T(8,128)S(1)}, f32[4,16,256]{2,1,0:T(8,128)S(1)}, u32[]{:S(2)}, u32[]{:S(2)}) %collective-permute-start.8) | collective-permute-done | bytes 65568 | tf_op jit(solution)/shard_map/ppermute | solution.py:21
  57.8 1.3 collective-permute-start.11
  59.1 1.3 collective-permute-start.10
  60.5 1.7 %collective-permute-done.10 = f32[12,4,256]{2,1,0:T(4,128)S(1)} collective-permute-done((f32[12,4,256]{2,1,0:T(4,128)S(1)}, f32[12,4,256]{2,1,0:T(4,128)S(1)}, u32[]{:S(2)}, u32[]{:S(2)}) %collective-permute-start.10) | collective-permute-done | bytes 49184 | tf_op jit(solution)/shard_map/ppermute | solution.py:21
  62.7 0.9 scatter_fusion.2
  63.6 3.5 %collective-permute-start.13 = (f32[4,16,256]{2,1,0:T(8,128)S(1)}, f32[4,16,256]{2,1,0:T(8,128)S(1)}, u32[]{:S(2)}, u32[]{:S(2)}) collective-permute-start(f32[4,16,256]{2,1,0:T(8,128)S(1)} %scatter_fusion.2), channel_id=1, source_target_pairs={{0,4},{4,8},{8,12},{1,5},{5,9},{9,13},{2,6},{6,10},{10,14},{3,7},{... | collective-permute-start | bytes 196616 | tf_op jit(solution)/shard_map/ppermute | solution.py:20
  67.2 1.8 %collective-permute-start.19 = (f32[2,12,4,256]{3,2,1,0:T(4,128)S(1)}, f32[2,12,4,256]{3,2,1,0:T(4,128)S(1)}, u32[]{:S(2)}, u32[]{:S(2)}) collective-permute-start(f32[2,12,4,256]{3,2,1,0:T(4,128)S(1)} %get-tuple-element.21), channel_id=1, source_target_pairs={{0,1},{2,3},{4,5},{6,7},{8,9},{10,11},{12,13},{14,15},{16,17},{18,... | collective-permute-start | bytes 294920 | tf_op jit(solution)/shard_map/ppermute | solution.py:20
  69.0 1.3 collective-permute-start.18
  70.3 1.3 collective-permute-start.12
  71.6 5.3 %collective-permute-done.12 = f32[4,16,256]{2,1,0:T(8,128)S(1)} collective-permute-done((f32[4,16,256]{2,1,0:T(8,128)S(1)}, f32[4,16,256]{2,1,0:T(8,128)S(1)}, u32[]{:S(2)}, u32[]{:S(2)}) %collective-permute-start.12) | collective-permute-done | bytes 65568 | tf_op jit(solution)/shard_map/ppermute | solution.py:21
  77.0 2.0 %collective-permute-start.15 = (f32[12,4,256]{2,1,0:T(4,128)S(1)}, f32[12,4,256]{2,1,0:T(4,128)S(1)}, u32[]{:S(2)}, u32[]{:S(2)}) collective-permute-start(f32[12,4,256]{2,1,0:T(4,128)S(1)} %get-tuple-element.23), channel_id=1, source_target_pairs={{0,1},{2,3},{4,5},{6,7},{8,9},{10,11},{12,13},{14,15},{16,17},{18,... | collective-permute-start | bytes 147464 | tf_op jit(solution)/shard_map/ppermute | solution.py:20
  79.1 1.3 collective-permute-start.14
  80.9 1.3 collective-permute-done.14
  82.7 0.9 scatter_fusion.3
  84.0 2.2 %collective-permute-start.21 = (f32[2,4,16,256]{3,2,1,0:T(8,128)S(1)}, f32[2,4,16,256]{3,2,1,0:T(8,128)S(1)}, u32[]{:S(2)}, u32[]{:S(2)}) collective-permute-start(f32[2,4,16,256]{3,2,1,0:T(8,128)S(1)} %fusion.87), channel_id=1, source_target_pairs={{0,4},{4,8},{8,12},{1,5},{5,9},{9,13},{2,6},{6,10},{10,14},{3,7},{... | collective-permute-start | bytes 393224 | tf_op jit(solution)/shard_map/ppermute | solution.py:20
  86.2 1.3 collective-permute-start.20
  87.5 1.8 %collective-permute-done.21 = f32[2,4,16,256]{3,2,1,0:T(8,128)S(1)} collective-permute-done((f32[2,4,16,256]{3,2,1,0:T(8,128)S(1)}, f32[2,4,16,256]{3,2,1,0:T(8,128)S(1)}, u32[]{:S(2)}, u32[]{:S(2)}) %collective-permute-start.21) | collective-permute-done | bytes 131104 | tf_op jit(solution)/shard_map/ppermute | solution.py:20
  89.3 4.1 %collective-permute-done.20 = f32[2,4,16,256]{3,2,1,0:T(8,128)S(1)} collective-permute-done((f32[2,4,16,256]{3,2,1,0:T(8,128)S(1)}, f32[2,4,16,256]{3,2,1,0:T(8,128)S(1)}, u32[]{:S(2)}, u32[]{:S(2)}) %collective-permute-start.20) | collective-permute-done | bytes 131104 | tf_op jit(solution)/shard_map/ppermute | solution.py:21
  93.4 1.3 collective-permute-start.23
  94.7 1.3 collective-permute-start.22
  96.1 1.9 %collective-permute-done.22 = f32[2,12,4,256]{3,2,1,0:T(4,128)S(1)} collective-permute-done((f32[2,12,4,256]{3,2,1,0:T(4,128)S(1)}, f32[2,12,4,256]{3,2,1,0:T(4,128)S(1)}, u32[]{:S(2)}, u32[]{:S(2)}) %collective-permute-start.22) | collective-permute-done | bytes 98336 | tf_op jit(solution)/shard_map/ppermute | solution.py:21
  98.8 2.2 %collective-permute-start.25 = (f32[2,4,16,256]{3,2,1,0:T(8,128)S(1)}, f32[2,4,16,256]{3,2,1,0:T(8,128)S(1)}, u32[]{:S(2)}, u32[]{:S(2)}) collective-permute-start(f32[2,4,16,256]{3,2,1,0:T(8,128)S(1)} %fusion.65), channel_id=1, source_target_pairs={{0,4},{4,8},{8,12},{1,5},{5,9},{9,13},{2,6},{6,10},{10,14},{3,7},{... | collective-permute-start | bytes 393224 | tf_op jit(solution)/shard_map/ppermute | solution.py:20
  101.0 1.3 collective-permute-start.24
  102.3 1.7 %collective-permute-done.25 = f32[2,4,16,256]{3,2,1,0:T(8,128)S(1)} collective-permute-done((f32[2,4,16,256]{3,2,1,0:T(8,128)S(1)}, f32[2,4,16,256]{3,2,1,0:T(8,128)S(1)}, u32[]{:S(2)}, u32[]{:S(2)}) %collective-permute-start.25) | collective-permute-done | bytes 131104 | tf_op jit(solution)/shard_map/ppermute | solution.py:20
  104.1 4.1 %collective-permute-done.24 = f32[2,4,16,256]{3,2,1,0:T(8,128)S(1)} collective-permute-done((f32[2,4,16,256]{3,2,1,0:T(8,128)S(1)}, f32[2,4,16,256]{3,2,1,0:T(8,128)S(1)}, u32[]{:S(2)}, u32[]{:S(2)}) %collective-permute-start.24) | collective-permute-done | bytes 131104 | tf_op jit(solution)/shard_map/ppermute | solution.py:21
  108.2 1.3 collective-permute-start.27
  109.5 1.3 collective-permute-start.26
  110.9 1.8 %collective-permute-done.26 = f32[2,12,4,256]{3,2,1,0:T(4,128)S(1)} collective-permute-done((f32[2,12,4,256]{3,2,1,0:T(4,128)S(1)}, f32[2,12,4,256]{3,2,1,0:T(4,128)S(1)}, u32[]{:S(2)}, u32[]{:S(2)}) %collective-permute-start.26) | collective-permute-done | bytes 98336 | tf_op jit(solution)/shard_map/ppermute | solution.py:21
  113.6 2.2 %collective-permute-start.29 = (f32[2,4,16,256]{3,2,1,0:T(8,128)S(1)}, f32[2,4,16,256]{3,2,1,0:T(8,128)S(1)}, u32[]{:S(2)}, u32[]{:S(2)}) collective-permute-start(f32[2,4,16,256]{3,2,1,0:T(8,128)S(1)} %fusion.42), channel_id=1, source_target_pairs={{0,4},{4,8},{8,12},{1,5},{5,9},{9,13},{2,6},{6,10},{10,14},{3,7},{... | collective-permute-start | bytes 393224 | tf_op jit(solution)/shard_map/ppermute | solution.py:20
  115.8 1.3 collective-permute-start.28
  117.1 4.7 %copy.188 = f32[2,4,16,256]{0,3,2,1:T(8,128)} copy(f32[2,4,16,256]{3,2,1,0:T(8,128)S(1)} %fusion.87) | data formatting | bytes 262144 | tf_op jit(solution)/shard_map/add | solution.py:138
  121.8 1.4 gather_fusion
  123.2 1.8 %collective-permute-start.31 = (f32[2,12,4,256]{3,2,1,0:T(4,128)S(1)}, f32[2,12,4,256]{3,2,1,0:T(4,128)S(1)}, u32[]{:S(2)}, u32[]{:S(2)}) collective-permute-start(f32[2,12,4,256]{3,2,1,0:T(4,128)S(1)} %get-tuple-element.15), channel_id=1, source_target_pairs={{0,1},{2,3},{4,5},{6,7},{8,9},{10,11},{12,13},{14,15},{16,17},{18,... | collective-permute-start | bytes 294920 | tf_op jit(solution)/shard_map/ppermute | solution.py:20
  125.0 1.5 collective-permute-start.30
  127.1 4.7 %copy.190 = f32[2,4,16,256]{0,3,2,1:T(8,128)} copy(f32[2,4,16,256]{3,2,1,0:T(8,128)S(1)} %fusion.65) | data formatting | bytes 262144 | tf_op jit(solution)/shard_map/add | solution.py:138
  131.8 1.4 gather_fusion.1
  133.2 4.7 %copy.192 = f32[2,4,16,256]{0,3,2,1:T(8,128)} copy(f32[2,4,16,256]{3,2,1,0:T(8,128)S(1)} %fusion.42) | data formatting | bytes 262144 | tf_op jit(solution)/shard_map/add | solution.py:138
  137.8 1.4 gather_fusion.2
  140.1 4.7 %copy.194 = f32[2,4,16,256]{0,3,2,1:T(8,128)} copy(f32[2,4,16,256]{3,2,1,0:T(8,128)S(1)} %fusion.19) | data formatting | bytes 262144 | tf_op jit(solution)/shard_map/add | solution.py:138
  144.8 1.4 gather_fusion.3
  146.6 15.9 %all-reduce.10 = (f32[1,2,32]{2,1,0:T(2,128)S(1)}, f32[1,2,32]{2,1,0:T(2,128)S(1)}, f32[1,2,32]{2,1,0:T(2,128)S(1)}, f32[1,2,32]{2,1,0:T(2,128)S(1)}) all-reduce(f32[1,2,32]{2,1,0:T(2,128)S(1)} %bitcast.43, f32[1,2,32]{2,1,0:T(2,128)S(1)} %bitcast.42, ...), channel_id=1, replica_groups=mesh['shot'=2,'slab'=4,'rep'=2,'sub'=2] {'slab','sub'}, use_global_device_ids=true, to_apply=%region_7.8 | all-reduce | flops 256 | bytes 2048 | tf_op jit(solution)/shard_map/psum | solution.py:140
  (82 shorter events, 8.9 us)
Async XLA Ops:
  0.6 59.8 %copy-start = (f32[4,16,256]{2,1,0:T(8,128)S(1)}, f32[4,16,256]{2,1,0:T(8,128)}, u32[]{:S(2)}) copy-start(f32[4,16,256]{2,1,0:T(8,128)} %param.11) | copy-start | bytes 196612
  6.5 14.0 %collective-permute-start.1 = (f32[4,16,256]{2,1,0:T(8,128)S(1)}, f32[4,16,256]{2,1,0:T(8,128)S(1)}, u32[]{:S(2)}, u32[]{:S(2)}) collective-permute-start(f32[4,16,256]{2,1,0:T(8,128)S(1)} %all_gather.6), channel_id=1, source_target_pairs={{0,4},{4,8},{8,12},{1,5},{5,9},{9,13},{2,6},{6,10},{10,14},{3,7},{... | collective-permute-start | bytes 196616 | tf_op jit(solution)/shard_map/ppermute | solution.py:20
  10.5 10.1 %collective-permute-start = (f32[4,16,256]{2,1,0:T(8,128)S(1)}, f32[4,16,256]{2,1,0:T(8,128)S(1)}, u32[]{:S(2)}, u32[]{:S(2)}) collective-permute-start(f32[4,16,256]{2,1,0:T(8,128)S(1)} %all_gather.6), channel_id=1, source_target_pairs={{4,0},{8,4},{12,8},{5,1},{9,5},{13,9},{6,2},{10,6},{14,10},{7,3},{... | collective-permute-start | bytes 196616 | tf_op jit(solution)/shard_map/ppermute | solution.py:21
  11.8 55.3 %collective-permute-start.17 = (f32[2,4,16,256]{3,2,1,0:T(8,128)S(1)}, f32[2,4,16,256]{3,2,1,0:T(8,128)S(1)}, u32[]{:S(2)}, u32[]{:S(2)}) collective-permute-start(f32[2,4,16,256]{3,2,1,0:T(8,128)S(1)} %broadcast_in_dim.34), channel_id=1, source_target_pairs={{0,4},{4,8},{8,12},{1,5},{5,9},{9,13},{2,6},{6,10},{10,14},{3,7},{... | collective-permute-start | bytes 393224 | tf_op jit(solution)/shard_map/ppermute | solution.py:20
  16.4 50.7 %collective-permute-start.16 = (f32[2,4,16,256]{3,2,1,0:T(8,128)S(1)}, f32[2,4,16,256]{3,2,1,0:T(8,128)S(1)}, u32[]{:S(2)}, u32[]{:S(2)}) collective-permute-start(f32[2,4,16,256]{3,2,1,0:T(8,128)S(1)} %broadcast_in_dim.34), channel_id=1, source_target_pairs={{4,0},{8,4},{12,8},{5,1},{9,5},{13,9},{6,2},{10,6},{14,10},{7,3},{... | collective-permute-start | bytes 393224 | tf_op jit(solution)/shard_map/ppermute | solution.py:21
  20.7 7.6 %collective-permute-start.3 = (f32[12,4,256]{2,1,0:T(4,128)S(1)}, f32[12,4,256]{2,1,0:T(4,128)S(1)}, u32[]{:S(2)}, u32[]{:S(2)}) collective-permute-start(f32[12,4,256]{2,1,0:T(4,128)S(1)} %get-tuple-element.29), channel_id=1, source_target_pairs={{0,1},{2,3},{4,5},{6,7},{8,9},{10,11},{12,13},{14,15},{16,17},{18,... | collective-permute-start | bytes 147464 | tf_op jit(solution)/shard_map/ppermute | solution.py:20
  22.0 6.3 %collective-permute-start.2 = (f32[12,4,256]{2,1,0:T(4,128)S(1)}, f32[12,4,256]{2,1,0:T(4,128)S(1)}, u32[]{:S(2)}, u32[]{:S(2)}) collective-permute-start(f32[12,4,256]{2,1,0:T(4,128)S(1)} %get-tuple-element.30), channel_id=1, source_target_pairs={{1,0},{3,2},{5,4},{7,6},{9,8},{11,10},{13,12},{15,14},{17,16},{19,... | collective-permute-start | bytes 147464 | tf_op jit(solution)/shard_map/ppermute | solution.py:21
  30.5 6.4 %collective-permute-start.5 = (f32[4,16,256]{2,1,0:T(8,128)S(1)}, f32[4,16,256]{2,1,0:T(8,128)S(1)}, u32[]{:S(2)}, u32[]{:S(2)}) collective-permute-start(f32[4,16,256]{2,1,0:T(8,128)S(1)} %scatter_fusion), channel_id=1, source_target_pairs={{0,4},{4,8},{8,12},{1,5},{5,9},{9,13},{2,6},{6,10},{10,14},{3,7},{... | collective-permute-start | bytes 196616 | tf_op jit(solution)/shard_map/ppermute | solution.py:20
  35.2 6.1 %collective-permute-start.4 = (f32[4,16,256]{2,1,0:T(8,128)S(1)}, f32[4,16,256]{2,1,0:T(8,128)S(1)}, u32[]{:S(2)}, u32[]{:S(2)}) collective-permute-start(f32[4,16,256]{2,1,0:T(8,128)S(1)} %scatter_fusion), channel_id=1, source_target_pairs={{4,0},{8,4},{12,8},{5,1},{9,5},{13,9},{6,2},{10,6},{14,10},{7,3},{... | collective-permute-start | bytes 196616 | tf_op jit(solution)/shard_map/ppermute | solution.py:21
  41.4 2.6 %collective-permute-start.7 = (f32[12,4,256]{2,1,0:T(4,128)S(1)}, f32[12,4,256]{2,1,0:T(4,128)S(1)}, u32[]{:S(2)}, u32[]{:S(2)}) collective-permute-start(f32[12,4,256]{2,1,0:T(4,128)S(1)} %get-tuple-element.27), channel_id=1, source_target_pairs={{0,1},{2,3},{4,5},{6,7},{8,9},{10,11},{12,13},{14,15},{16,17},{18,... | collective-permute-start | bytes 147464 | tf_op jit(solution)/shard_map/ppermute | solution.py:20
  42.7 3.1 %collective-permute-start.6 = (f32[12,4,256]{2,1,0:T(4,128)S(1)}, f32[12,4,256]{2,1,0:T(4,128)S(1)}, u32[]{:S(2)}, u32[]{:S(2)}) collective-permute-start(f32[12,4,256]{2,1,0:T(4,128)S(1)} %get-tuple-element.28), channel_id=1, source_target_pairs={{1,0},{3,2},{5,4},{7,6},{9,8},{11,10},{13,12},{15,14},{17,16},{19,... | collective-permute-start | bytes 147464 | tf_op jit(solution)/shard_map/ppermute | solution.py:21
  48.0 5.4 %collective-permute-start.9 = (f32[4,16,256]{2,1,0:T(8,128)S(1)}, f32[4,16,256]{2,1,0:T(8,128)S(1)}, u32[]{:S(2)}, u32[]{:S(2)}) collective-permute-start(f32[4,16,256]{2,1,0:T(8,128)S(1)} %scatter_fusion.1), channel_id=1, source_target_pairs={{0,4},{4,8},{8,12},{1,5},{5,9},{9,13},{2,6},{6,10},{10,14},{3,7},{... | collective-permute-start | bytes 196616 | tf_op jit(solution)/shard_map/ppermute | solution.py:20
  51.6 6.1 %collective-permute-start.8 = (f32[4,16,256]{2,1,0:T(8,128)S(1)}, f32[4,16,256]{2,1,0:T(8,128)S(1)}, u32[]{:S(2)}, u32[]{:S(2)}) collective-permute-start(f32[4,16,256]{2,1,0:T(8,128)S(1)} %scatter_fusion.1), channel_id=1, source_target_pairs={{4,0},{8,4},{12,8},{5,1},{9,5},{13,9},{6,2},{10,6},{14,10},{7,3},{... | collective-permute-start | bytes 196616 | tf_op jit(solution)/shard_map/ppermute | solution.py:21
  57.8 2.7 %collective-permute-start.11 = (f32[12,4,256]{2,1,0:T(4,128)S(1)}, f32[12,4,256]{2,1,0:T(4,128)S(1)}, u32[]{:S(2)}, u32[]{:S(2)}) collective-permute-start(f32[12,4,256]{2,1,0:T(4,128)S(1)} %get-tuple-element.25), channel_id=1, source_target_pairs={{0,1},{2,3},{4,5},{6,7},{8,9},{10,11},{12,13},{14,15},{16,17},{18,... | collective-permute-start | bytes 147464 | tf_op jit(solution)/shard_map/ppermute | solution.py:20
  59.1 3.1 %collective-permute-start.10 = (f32[12,4,256]{2,1,0:T(4,128)S(1)}, f32[12,4,256]{2,1,0:T(4,128)S(1)}, u32[]{:S(2)}, u32[]{:S(2)}) collective-permute-start(f32[12,4,256]{2,1,0:T(4,128)S(1)} %get-tuple-element.26), channel_id=1, source_target_pairs={{1,0},{3,2},{5,4},{7,6},{9,8},{11,10},{13,12},{15,14},{17,16},{19,... | collective-permute-start | bytes 147464 | tf_op jit(solution)/shard_map/ppermute | solution.py:21
  60.4 50.4 %copy-start.2 = (s32[32]{0:T(128)S(1)}, s32[32]{0:T(128)}, u32[]{:S(2)}) copy-start(s32[32]{0:T(128)} %param.20) | copy-start | bytes 388
  60.4 50.4 %copy-start.3 = (s32[32]{0:T(128)S(1)}, s32[32]{0:T(128)}, u32[]{:S(2)}) copy-start(s32[32]{0:T(128)} %param.19) | copy-start | bytes 388
  60.4 50.4 %copy-start.4 = (s32[32]{0:T(128)S(1)}, s32[32]{0:T(128)}, u32[]{:S(2)}) copy-start(s32[32]{0:T(128)} %param.21) | copy-start | bytes 388
  63.6 8.0 %collective-permute-start.13 = (f32[4,16,256]{2,1,0:T(8,128)S(1)}, f32[4,16,256]{2,1,0:T(8,128)S(1)}, u32[]{:S(2)}, u32[]{:S(2)}) collective-permute-start(f32[4,16,256]{2,1,0:T(8,128)S(1)} %scatter_fusion.2), channel_id=1, source_target_pairs={{0,4},{4,8},{8,12},{1,5},{5,9},{9,13},{2,6},{6,10},{10,14},{3,7},{... | collective-permute-start | bytes 196616 | tf_op jit(solution)/shard_map/ppermute | solution.py:20
  67.2 13.2 %collective-permute-start.19 = (f32[2,12,4,256]{3,2,1,0:T(4,128)S(1)}, f32[2,12,4,256]{3,2,1,0:T(4,128)S(1)}, u32[]{:S(2)}, u32[]{:S(2)}) collective-permute-start(f32[2,12,4,256]{3,2,1,0:T(4,128)S(1)} %get-tuple-element.21), channel_id=1, source_target_pairs={{0,1},{2,3},{4,5},{6,7},{8,9},{10,11},{12,13},{14,15},{16,17},{18,... | collective-permute-start | bytes 294920 | tf_op jit(solution)/shard_map/ppermute | solution.py:20
  69.0 11.4 %collective-permute-start.18 = (f32[2,12,4,256]{3,2,1,0:T(4,128)S(1)}, f32[2,12,4,256]{3,2,1,0:T(4,128)S(1)}, u32[]{:S(2)}, u32[]{:S(2)}) collective-permute-start(f32[2,12,4,256]{3,2,1,0:T(4,128)S(1)} %get-tuple-element.22), channel_id=1, source_target_pairs={{1,0},{3,2},{5,4},{7,6},{9,8},{11,10},{13,12},{15,14},{17,16},{19,... | collective-permute-start | bytes 294920 | tf_op jit(solution)/shard_map/ppermute | solution.py:21
  70.3 6.7 %collective-permute-start.12 = (f32[4,16,256]{2,1,0:T(8,128)S(1)}, f32[4,16,256]{2,1,0:T(8,128)S(1)}, u32[]{:S(2)}, u32[]{:S(2)}) collective-permute-start(f32[4,16,256]{2,1,0:T(8,128)S(1)} %scatter_fusion.2), channel_id=1, source_target_pairs={{4,0},{8,4},{12,8},{5,1},{9,5},{13,9},{6,2},{10,6},{14,10},{7,3},{... | collective-permute-start | bytes 196616 | tf_op jit(solution)/shard_map/ppermute | solution.py:21
  77.0 3.8 %collective-permute-start.15 = (f32[12,4,256]{2,1,0:T(4,128)S(1)}, f32[12,4,256]{2,1,0:T(4,128)S(1)}, u32[]{:S(2)}, u32[]{:S(2)}) collective-permute-start(f32[12,4,256]{2,1,0:T(4,128)S(1)} %get-tuple-element.23), channel_id=1, source_target_pairs={{0,1},{2,3},{4,5},{6,7},{8,9},{10,11},{12,13},{14,15},{16,17},{18,... | collective-permute-start | bytes 147464 | tf_op jit(solution)/shard_map/ppermute | solution.py:20
  79.1 3.1 %collective-permute-start.14 = (f32[12,4,256]{2,1,0:T(4,128)S(1)}, f32[12,4,256]{2,1,0:T(4,128)S(1)}, u32[]{:S(2)}, u32[]{:S(2)}) collective-permute-start(f32[12,4,256]{2,1,0:T(4,128)S(1)} %get-tuple-element.24), channel_id=1, source_target_pairs={{1,0},{3,2},{5,4},{7,6},{9,8},{11,10},{13,12},{15,14},{17,16},{19,... | collective-permute-start | bytes 147464 | tf_op jit(solution)/shard_map/ppermute | solution.py:21
  84.0 5.3 %collective-permute-start.21 = (f32[2,4,16,256]{3,2,1,0:T(8,128)S(1)}, f32[2,4,16,256]{3,2,1,0:T(8,128)S(1)}, u32[]{:S(2)}, u32[]{:S(2)}) collective-permute-start(f32[2,4,16,256]{3,2,1,0:T(8,128)S(1)} %fusion.87), channel_id=1, source_target_pairs={{0,4},{4,8},{8,12},{1,5},{5,9},{9,13},{2,6},{6,10},{10,14},{3,7},{... | collective-permute-start | bytes 393224 | tf_op jit(solution)/shard_map/ppermute | solution.py:20
  86.2 7.2 %collective-permute-start.20 = (f32[2,4,16,256]{3,2,1,0:T(8,128)S(1)}, f32[2,4,16,256]{3,2,1,0:T(8,128)S(1)}, u32[]{:S(2)}, u32[]{:S(2)}) collective-permute-start(f32[2,4,16,256]{3,2,1,0:T(8,128)S(1)} %fusion.87), channel_id=1, source_target_pairs={{4,0},{8,4},{12,8},{5,1},{9,5},{13,9},{6,2},{10,6},{14,10},{7,3},{... | collective-permute-start | bytes 393224 | tf_op jit(solution)/shard_map/ppermute | solution.py:21
  93.4 2.6 %collective-permute-start.23 = (f32[2,12,4,256]{3,2,1,0:T(4,128)S(1)}, f32[2,12,4,256]{3,2,1,0:T(4,128)S(1)}, u32[]{:S(2)}, u32[]{:S(2)}) collective-permute-start(f32[2,12,4,256]{3,2,1,0:T(4,128)S(1)} %get-tuple-element.19), channel_id=1, source_target_pairs={{0,1},{2,3},{4,5},{6,7},{8,9},{10,11},{12,13},{14,15},{16,17},{18,... | collective-permute-start | bytes 294920 | tf_op jit(solution)/shard_map/ppermute | solution.py:20
  94.7 3.2 %collective-permute-start.22 = (f32[2,12,4,256]{3,2,1,0:T(4,128)S(1)}, f32[2,12,4,256]{3,2,1,0:T(4,128)S(1)}, u32[]{:S(2)}, u32[]{:S(2)}) collective-permute-start(f32[2,12,4,256]{3,2,1,0:T(4,128)S(1)} %get-tuple-element.20), channel_id=1, source_target_pairs={{1,0},{3,2},{5,4},{7,6},{9,8},{11,10},{13,12},{15,14},{17,16},{19,... | collective-permute-start | bytes 294920 | tf_op jit(solution)/shard_map/ppermute | solution.py:21
  98.8 5.3 %collective-permute-start.25 = (f32[2,4,16,256]{3,2,1,0:T(8,128)S(1)}, f32[2,4,16,256]{3,2,1,0:T(8,128)S(1)}, u32[]{:S(2)}, u32[]{:S(2)}) collective-permute-start(f32[2,4,16,256]{3,2,1,0:T(8,128)S(1)} %fusion.65), channel_id=1, source_target_pairs={{0,4},{4,8},{8,12},{1,5},{5,9},{9,13},{2,6},{6,10},{10,14},{3,7},{... | collective-permute-start | bytes 393224 | tf_op jit(solution)/shard_map/ppermute | solution.py:20
  101.0 7.2 %collective-permute-start.24 = (f32[2,4,16,256]{3,2,1,0:T(8,128)S(1)}, f32[2,4,16,256]{3,2,1,0:T(8,128)S(1)}, u32[]{:S(2)}, u32[]{:S(2)}) collective-permute-start(f32[2,4,16,256]{3,2,1,0:T(8,128)S(1)} %fusion.65), channel_id=1, source_target_pairs={{4,0},{8,4},{12,8},{5,1},{9,5},{13,9},{6,2},{10,6},{14,10},{7,3},{... | collective-permute-start | bytes 393224 | tf_op jit(solution)/shard_map/ppermute | solution.py:21
  108.2 2.7 %collective-permute-start.27 = (f32[2,12,4,256]{3,2,1,0:T(4,128)S(1)}, f32[2,12,4,256]{3,2,1,0:T(4,128)S(1)}, u32[]{:S(2)}, u32[]{:S(2)}) collective-permute-start(f32[2,12,4,256]{3,2,1,0:T(4,128)S(1)} %get-tuple-element.17), channel_id=1, source_target_pairs={{0,1},{2,3},{4,5},{6,7},{8,9},{10,11},{12,13},{14,15},{16,17},{18,... | collective-permute-start | bytes 294920 | tf_op jit(solution)/shard_map/ppermute | solution.py:20
  109.5 3.2 %collective-permute-start.26 = (f32[2,12,4,256]{3,2,1,0:T(4,128)S(1)}, f32[2,12,4,256]{3,2,1,0:T(4,128)S(1)}, u32[]{:S(2)}, u32[]{:S(2)}) collective-permute-start(f32[2,12,4,256]{3,2,1,0:T(4,128)S(1)} %get-tuple-element.18), channel_id=1, source_target_pairs={{1,0},{3,2},{5,4},{7,6},{9,8},{11,10},{13,12},{15,14},{17,16},{19,... | collective-permute-start | bytes 294920 | tf_op jit(solution)/shard_map/ppermute | solution.py:21
  113.6 9.6 %collective-permute-start.29 = (f32[2,4,16,256]{3,2,1,0:T(8,128)S(1)}, f32[2,4,16,256]{3,2,1,0:T(8,128)S(1)}, u32[]{:S(2)}, u32[]{:S(2)}) collective-permute-start(f32[2,4,16,256]{3,2,1,0:T(8,128)S(1)} %fusion.42), channel_id=1, source_target_pairs={{0,4},{4,8},{8,12},{1,5},{5,9},{9,13},{2,6},{6,10},{10,14},{3,7},{... | collective-permute-start | bytes 393224 | tf_op jit(solution)/shard_map/ppermute | solution.py:20
  115.8 7.4 %collective-permute-start.28 = (f32[2,4,16,256]{3,2,1,0:T(8,128)S(1)}, f32[2,4,16,256]{3,2,1,0:T(8,128)S(1)}, u32[]{:S(2)}, u32[]{:S(2)}) collective-permute-start(f32[2,4,16,256]{3,2,1,0:T(8,128)S(1)} %fusion.42), channel_id=1, source_target_pairs={{4,0},{8,4},{12,8},{5,1},{9,5},{13,9},{6,2},{10,6},{14,10},{7,3},{... | collective-permute-start | bytes 393224 | tf_op jit(solution)/shard_map/ppermute | solution.py:21
  123.2 16.0 %collective-permute-start.31 = (f32[2,12,4,256]{3,2,1,0:T(4,128)S(1)}, f32[2,12,4,256]{3,2,1,0:T(4,128)S(1)}, u32[]{:S(2)}, u32[]{:S(2)}) collective-permute-start(f32[2,12,4,256]{3,2,1,0:T(4,128)S(1)} %get-tuple-element.15), channel_id=1, source_target_pairs={{0,1},{2,3},{4,5},{6,7},{8,9},{10,11},{12,13},{14,15},{16,17},{18,... | collective-permute-start | bytes 294920 | tf_op jit(solution)/shard_map/ppermute | solution.py:20
  125.0 14.2 %collective-permute-start.30 = (f32[2,12,4,256]{3,2,1,0:T(4,128)S(1)}, f32[2,12,4,256]{3,2,1,0:T(4,128)S(1)}, u32[]{:S(2)}, u32[]{:S(2)}) collective-permute-start(f32[2,12,4,256]{3,2,1,0:T(4,128)S(1)} %get-tuple-element.16), channel_id=1, source_target_pairs={{1,0},{3,2},{5,4},{7,6},{9,8},{11,10},{13,12},{15,14},{17,16},{19,... | collective-permute-start | bytes 294920 | tf_op jit(solution)/shard_map/ppermute | solution.py:21
  140.1 22.9 %copy-start.1 = (f32[2,4,16,256]{3,2,1,0:T(8,128)}, f32[2,4,16,256]{3,2,1,0:T(8,128)S(1)}, u32[]{:S(2)}) copy-start(f32[2,4,16,256]{3,2,1,0:T(8,128)S(1)} %fusion.19) | copy-start | bytes 393220
where the time goes:
time: 164 us; the launch traced here: 163 us
  starting transfers between devices  59.5 us (36%)
  waiting for transfers between devices  35.4 us (22%)
  blocking collectives  26.8 us (16%)
  local copies, waits for them, and re-layouts  25.4 us (15%)
  other arithmetic  14.7 us (9%)
    ppermute x16, starting transfers between devices, padded_2(): before = lax.ppermute(last, axis, up)  38.7 us
    ppermute x16, waiting for transfers between devices, padded_2(): after = lax.ppermute(first, axis, down)  30.8 us
    ppermute x16, starting transfers between devices, padded_2(): after = lax.ppermute(first, axis, down)  20.8 us
    add x4, local copies, waits for them, and re-layouts, shards(): 2.0 * wave_now - wave_prev + speed_square * laplace(wave_padded)  18.7 us
    psum x1, blocking collectives, shards(): picked = lax.psum(picked, ('slab', 'sub'))  15.9 us
    all_gather x1, blocking collectives, shards(): lax.all_gather(incident_now, 'rep', axis=2, tiled=True)  5.89 us
    gather x4, local copies, waits for them, and re-layouts, sample(): picked = field[:, clip_z, clip_y, where_x]  5.42 us
    all_gather x1, blocking collectives, shards(): lax.all_gather(incident_prev, 'rep', axis=2, tiled=True)  4.99 us
  transfers between devices with their start and end apart: 32, of which 14 were waited for; matrix products, arithmetic and copies ran while one was open for 17% of the time, Pallas kernels for 0%

commit v1 on v0

--- a/solution.py
+++ b/solution.py
@@ -1,13 +1,19 @@
 import jax
 import jax.numpy as jnp
+import numpy as np
 from jax import lax
+from jax.experimental import pallas as pl
+from jax.experimental.pallas import tpu as pltpu
 from jax.sharding import PartitionSpec as P
 
 STEPS = 4
+GRID_ROWS = 512
 
 
 stencil_coeffs = (-205.0 / 72.0, 8.0 / 5.0, -1.0 / 5.0, 8.0 / 315.0, -1.0 / 560.0)
 pert_scale = 0.2
+whole_coeffs = (-14350, 8064, -1008, 128, -9)
+coeff_scale = 5040.0
 
 
 def padded_2(array, sides, width):
@@ -94,7 +100,7 @@
     return jnp.where(inside[None, :], picked, jnp.zeros_like(picked))
 
 
-def shards(
+def halo_shards(
     courant,
     incident_prev,
     incident_now,
@@ -145,27 +151,225 @@
     return (incident_final, wave_now, traces)
 
 
+def band(size):
+    apart = np.abs(np.arange(size)[:, None] - np.arange(size)[None, :])
+    return sum(whole_coeffs[k] * (apart == k) for k in range(1, 5))
+
+
+def operators(deep, tall, wide):
+    rows = np.kron(band(deep), np.eye(tall)) + np.kron(np.eye(deep), band(tall))
+    return rows.astype(jnp.bfloat16), band(wide).astype(jnp.bfloat16)
+
+
+def split3(value):
+    high = value.astype(jnp.bfloat16)
+    rest = value - high.astype(jnp.float32)
+    middle = rest.astype(jnp.bfloat16)
+    low = (rest - middle.astype(jnp.float32)).astype(jnp.bfloat16)
+    return high, middle, low
+
+
+def swapped(array, axis, distance):
+    size = lax.axis_size(axis)
+    return lax.ppermute(array, axis, [(i, i ^ distance) for i in range(size)])
+
+
+def whole_kernel(
+    place_ref,
+    wavelet_ref,
+    source_ref,
+    seeds_ref,
+    receiver_ref,
+    rows_op_ref,
+    wide_op_ref,
+    blocks_ref,
+    incident_ref,
+    scattered_ref,
+    traces_ref,
+    field_ref,
+    speed_ref,
+    contrast_ref,
+    force_ref,
+    drive_ref,
+    wave_ref,
+    taken_ref,
+):
+    slab, sub, rep = place_ref[0], place_ref[1], place_ref[2]
+    wide_parts, tall_parts, deep_parts, layers, tall_count, part_width = blocks_ref.shape
+    deep_count = layers // 3
+    deep, tall, wide = deep_parts * deep_count, tall_parts * tall_count, wide_parts * part_width
+    rows = deep * tall
+    replicas = seeds_ref.shape[0]
+    sources = source_ref.shape[1]
+    receivers = receiver_ref.shape[1]
+
+    for x in range(wide_parts):
+        for y in range(tall_parts):
+            for z in range(deep_parts):
+                at_z = pl.multiple_of((slab ^ z) * deep_count, deep_count)
+                at_y = pl.multiple_of((sub ^ y) * tall_count, tall_count)
+                at_x = pl.multiple_of((rep ^ x) * part_width, part_width)
+                there = (pl.ds(at_z, deep_count), pl.ds(at_y, tall_count), pl.ds(at_x, part_width))
+                block = blocks_ref[x, y, z]
+                field_ref[(1,) + there] = block[:deep_count]
+                field_ref[(0,) + there] = block[deep_count : 2 * deep_count]
+                courant = block[2 * deep_count :]
+                speed_ref[there] = courant * courant * (1.0 / coeff_scale)
+
+    z_of = lax.broadcasted_iota(jnp.int32, (deep, tall, wide), 0)
+    y_of = lax.broadcasted_iota(jnp.int32, (deep, tall, wide), 1)
+    x_of = lax.broadcasted_iota(jnp.int32, (deep, tall, wide), 2)
+    cell = z_of * 73856093 + y_of * 19349663 + x_of * 83492791
+    for r in range(replicas):
+        hashed = cell + seeds_ref[r] * 668265263
+        hashed = hashed ^ (hashed >> 15)
+        hashed = hashed * 1274126177
+        hashed = hashed ^ (hashed >> 13)
+        fraction = (hashed & 65535).astype(jnp.float32) / 65535.0
+        contrast_ref[r] = 2.0 * (pert_scale * (2.0 * fraction - 1.0))
+
+    lane = lax.broadcasted_iota(jnp.int32, (1, wide), 1)
+
+    force_ref[...] = jnp.zeros_like(force_ref)
+    for n in range(STEPS):
+        for k in range(sources):
+            at = (n, source_ref[0, k], pl.ds(source_ref[1, k], 1), slice(None))
+            force_ref[at] += jnp.where(lane == source_ref[2, k], wavelet_ref[n, k], 0.0)
+
+    def applied(value):
+        parts = split3(value)
+        total = (3.0 * whole_coeffs[0]) * value
+        for part in parts:
+            total += jnp.dot(rows_op_ref[...], part, preferred_element_type=jnp.float32)
+        for part in parts:
+            total += jnp.dot(part, wide_op_ref[...], preferred_element_type=jnp.float32)
+        return total
+
+    shape = (rows, wide)
+    column = lax.broadcasted_iota(jnp.int32, (receivers, 128), 1)
+    gathered = jnp.zeros((receivers, 128), jnp.float32)
+    speed = speed_ref[...].reshape(shape)
+    for n in range(STEPS):
+        older, newer = n % 2, (n + 1) % 2
+        now = field_ref[newer].reshape(shape)
+        drive = speed * applied(now) + force_ref[n].reshape(shape)
+        drive_ref[...] = drive
+        field_ref[older] = (2.0 * now - field_ref[older].reshape(shape) + drive).reshape(deep, tall, wide)
+        for r in range(replicas):
+            following = contrast_ref[r].reshape(shape) * drive_ref[...]
+            if n > 0:
+                wave = wave_ref[newer, r].reshape(shape)
+                following += speed * applied(wave) + 2.0 * wave
+            if n > 1:
+                following -= wave_ref[older, r].reshape(shape)
+            wave_ref[older, r] = following.reshape(deep, tall, wide)
+            for j in range(receivers):
+                row = wave_ref[older, r, receiver_ref[0, j], pl.ds(receiver_ref[1, j], 1), :]
+                taken_ref[pl.ds(j, 1), :] = jnp.where(lane == receiver_ref[2, j], row, 0.0)
+            summed = jnp.sum(taken_ref[...], axis=1, keepdims=True)
+            gathered += jnp.where(column == n * replicas + r, summed, 0.0)
+    at_z = pl.multiple_of(slab * deep_count, deep_count)
+    at_y = pl.multiple_of(sub * tall_count, tall_count)
+    at_x = pl.multiple_of(rep * part_width, part_width)
+    own = (pl.ds(at_z, deep_count), pl.ds(at_y, tall_count))
+    last = (STEPS - 1) % 2
+    incident_ref[...] = field_ref[(last,) + own + (pl.ds(at_x, part_width),)]
+    for r in range(replicas):
+        scattered_ref[r] = wave_ref[(last, r) + own]
+    traces_ref[...] = jnp.transpose(gathered)[: STEPS * replicas, :]
+
+
+def whole_shards(
+    courant,
+    incident_prev,
+    incident_now,
+    wavelet,
+    source_z,
+    source_y,
+    source_x,
+    replica_seeds,
+    receiver_z,
+    receiver_y,
+    receiver_x,
+):
+    deep_count, tall_count, part_width = incident_now.shape
+    wide = courant.shape[2]
+    slab, sub, rep = (lax.axis_index(axis) for axis in ("slab", "sub", "rep"))
+    slabs, subs, reps = (lax.axis_size(axis) for axis in ("slab", "sub", "rep"))
+    deep, tall = slabs * deep_count, subs * tall_count
+    replicas, receivers = replica_seeds.shape[0], receiver_z.shape[0]
+    part = lax.dynamic_slice_in_dim(courant, rep * part_width, part_width, 2)
+    own = jnp.concatenate([incident_now, incident_prev, part], axis=0)
+    along = {m: swapped(own, "slab", m) for m in sorted(range(1, slabs), key=lambda m: m == 1)}
+    blocks = jnp.stack([own] + [along[m] for m in range(1, slabs)])
+    blocks = jnp.stack([blocks] + [swapped(blocks, "rep", m) for m in range(1, reps)])
+    blocks = jnp.stack([blocks] + [swapped(blocks, "sub", m) for m in range(1, subs)], axis=1)
+    rows_op, wide_op = operators(deep, tall, wide)
+    smem = pl.BlockSpec(memory_space=pltpu.SMEM)
+    vmem = pl.BlockSpec(memory_space=pltpu.VMEM)
+    grid = (deep, tall, wide)
+    incident_final, scattered_final, traces = pl.pallas_call(
+        whole_kernel,
+        out_shape=(
+            jax.ShapeDtypeStruct((deep_count, tall_count, part_width), jnp.float32),
+            jax.ShapeDtypeStruct((replicas, deep_count, tall_count, wide), jnp.float32),
+            jax.ShapeDtypeStruct((STEPS * replicas, receivers), jnp.float32),
+        ),
+        in_specs=[smem] * 5 + [vmem] * 3,
+        out_specs=(vmem, vmem, vmem),
+        scratch_shapes=[
+            pltpu.VMEM((2,) + grid, jnp.float32),
+            pltpu.VMEM(grid, jnp.float32),
+            pltpu.VMEM((replicas,) + grid, jnp.float32),
+            pltpu.VMEM((STEPS,) + grid, jnp.float32),
+            pltpu.VMEM((deep * tall, wide), jnp.float32),
+            pltpu.VMEM((2, replicas) + grid, jnp.float32),
+            pltpu.VMEM((receivers, wide), jnp.float32),
+        ],
+        compiler_params=pltpu.CompilerParams(vmem_limit_bytes=48 * 2**20),
+    )(
+        jnp.stack([slab, sub, rep]).astype(jnp.int32),
+        wavelet,
+        jnp.stack([source_z, source_y, source_x]),
+        replica_seeds,
+        jnp.stack([receiver_z, receiver_y, receiver_x]),
+        jnp.asarray(rows_op),
+        jnp.asarray(wide_op),
+        blocks,
+    )
+    return incident_final, scattered_final, traces.reshape(STEPS, replicas, receivers)
+
+
 def solution(mesh):
-    return jax.shard_map(
-        shards,
-        mesh=mesh,
-        in_specs=(
-            P("slab", "sub", None),
-            P(("shot", "slab"), "sub", "rep"),
-            P(("shot", "slab"), "sub", "rep"),
-            P(),
-            P("shot"),
-            P("shot"),
-            P("shot"),
-            P("rep"),
-            P(),
-            P(),
-            P(),
-        ),
-        out_specs=(
-            P(("shot", "slab"), "sub", "rep"),
-            P("rep", ("shot", "slab"), "sub", None),
-            P("shot", "rep", None),
-        ),
-        check_vma=False,
-    )
+    slabs, subs, reps = (mesh.shape[axis] for axis in ("slab", "sub", "rep"))
+
+    def step(courant, *rest):
+        deep, tall, _ = courant.shape
+        paired = all(size & (size - 1) == 0 for size in (slabs, subs, reps))
+        part_width = courant.shape[2] // reps
+        fits = deep * tall <= GRID_ROWS and part_width % 128 == 0
+        return jax.shard_map(
+            whole_shards if paired and fits else halo_shards,
+            mesh=mesh,
+            in_specs=(
+                P("slab", "sub", None),
+                P(("shot", "slab"), "sub", "rep"),
+                P(("shot", "slab"), "sub", "rep"),
+                P(),
+                P("shot"),
+                P("shot"),
+                P("shot"),
+                P("rep"),
+                P(),
+                P(),
+                P(),
+            ),
+            out_specs=(
+                P(("shot", "slab"), "sub", "rep"),
+                P("rep", ("shot", "slab"), "sub", None),
+                P("shot", "rep", None),
+            ),
+            check_vma=False,
+        )(courant, *rest)
+
+    return step

time: 164 us -> 40.1 us (0.24)
  starting transfers between devices: 59.5 us -> 7.31 us
  blocking collectives: 26.8 us -> 0 us
  local copies, waits for them, and re-layouts: 25.4 us -> 1.81 us
  waiting for transfers between devices: 35.4 us -> 17.4 us
  other arithmetic: 14.7 us -> 1.2 us
  Pallas kernels: 0 us -> 11.3 us
    ppermute x32 -> x5, starting transfers between devices: 59.5 us -> 7.31 us  [swapped(): return lax.ppermute(array, axis, [(i, i ^ distance) for i in range(size)])]
    add x4 -> x0, local copies, waits for them, and re-layouts: 18.7 us -> none  [shards(): 2.0 * wave_now - wave_prev + speed_square * laplace(wave_padded)]
    ppermute x32 -> x5, waiting for transfers between devices: 35.4 us -> 17.4 us  [swapped(): return lax.ppermute(array, axis, [(i, i ^ distance) for i in range(size)])]
    psum x1 -> x0, blocking collectives: 15.9 us -> none  [shards(): picked = lax.psum(picked, ('slab', 'sub'))]
    pallas_call x0 -> x1, Pallas kernels: none -> 11.3 us  [whole_shards(): pl.pallas_call(whole_kernel, out_shape=(jax.ShapeDtypeStruct((deep_count,...]
    all_gather x2 -> x0, blocking collectives: 10.9 us -> none  [the longest x1 5.89 us: shards(): lax.all_gather(incident_now, 'rep', axis=2, tiled=True)]
    gather x4 -> x0, local copies, waits for them, and re-layouts: 5.42 us -> none  [sample(): picked = field[:, clip_z, clip_y, where_x]]
    add x10 -> x0, other arithmetic: 4.17 us -> none  [the longest x4 2.49 us: shards(): whole_next = 2.0 * whole_now - whole_prev + speed_square * laplace(padded)]
  transfers between devices with their start and end apart: 32 -> 5, of which waited for: 14 -> 4; matrix products, arithmetic and copies ran while one was open for 17% -> 0% of each run, Pallas kernels for 0% -> 0%
where the time goes in v1:
time: 40.1 us; the launch traced here: 39.8 us
  waiting for transfers between devices  17.4 us (43%)
  Pallas kernels  11.3 us (28%)
  starting transfers between devices  7.31 us (18%)
  local copies, waits for them, and re-layouts  1.81 us (5%)
  other arithmetic  1.2 us (3%)
  between operations  0.77 us (2%)
    ppermute x5, waiting for transfers between devices, swapped(): return lax.ppermute(array, axis, [(i, i ^ distance) for i in range(size)])  17.4 us
    pallas_call x1, Pallas kernels, whole_shards(): pl.pallas_call(whole_kernel, out_shape=(jax.ShapeDtypeStruct((deep_count,...  11.3 us
    ppermute x5, starting transfers between devices, swapped(): return lax.ppermute(array, axis, [(i, i ^ distance) for i in range(size)])  7.31 us
    unnamed x22, local copies, waits for them, and re-layouts  1.81 us
  transfers between devices with their start and end apart: 5, of which 4 were waited for; matrix products, arithmetic and copies ran while one was open for 0% of the time, Pallas kernels for 0%

profile of v1, /device:TPU:0, one launch (start us, length us, event | category | flops | bytes accessed | tf_op | source)
XLA Modules:
  0.0 39.8 jit_solution(15608281678198597907)
XLA Ops:
  0.6 0.0 copy-start
  0.7 0.8 %copy-done = f32[4,16,256]{2,1,0:T(8,128)S(1)} copy-done((f32[4,16,256]{2,1,0:T(8,128)S(1)}, f32[4,16,256]{2,1,0:T(8,128)}, u32[]{:S(2)}) %copy-start) | copy-done | bytes 65560
  1.5 0.8 %fusion = (f32[1,12,16,128]{3,2,1,0:T(8,128)S(1)}, f32[12,16,128]{2,1,0:T(8,128)S(1)}) fusion(f32[4,16,128]{2,1,0:T(8,128)S(1)} %constant_dynamic-slice_fusion, f32[4,16,128]{2,1,0:T(8,128)} %param.14, f32[4,16,128]{2,1,0:T(8,128)} %param.15), kind=kLoop, calls=%fused_computation.8 | loop fusion | flops 49152 | bytes 294912 | tf_op jit(solution)/shard_map/stack | solution.py:304
  2.3 3.1 %collective-permute-start = (f32[12,16,128]{2,1,0:T(8,128)S(1)}, f32[12,16,128]{2,1,0:T(8,128)S(1)}, u32[]{:S(2)}, u32[]{:S(2)}) collective-permute-start(f32[12,16,128]{2,1,0:T(8,128)S(1)} %get-tuple-element.14), channel_id=1, source_target_pairs={{0,4},{4,0},{8,12},{12,8},{1,5},{5,1},{9,13},{13,9},{2,6},{6,2},{1... | collective-permute-start | bytes 294920 | tf_op jit(solution)/shard_map/ppermute | solution.py:174
  5.4 2.6 %collective-permute-start.1 = (f32[12,16,128]{2,1,0:T(8,128)S(1)}, f32[12,16,128]{2,1,0:T(8,128)S(1)}, u32[]{:S(2)}, u32[]{:S(2)}) collective-permute-start(f32[12,16,128]{2,1,0:T(8,128)S(1)} %get-tuple-element.14), channel_id=1, source_target_pairs={{0,8},{4,12},{8,0},{12,4},{1,9},{5,13},{9,1},{13,5},{2,10},{6,14},... | collective-permute-start | bytes 294920 | tf_op jit(solution)/shard_map/ppermute | solution.py:174
  7.9 0.0 collective-permute-start.2
  8.0 0.2 collective-permute-done
  8.2 7.6 %collective-permute-done.1 = f32[12,16,128]{2,1,0:T(8,128)S(1)} collective-permute-done((f32[12,16,128]{2,1,0:T(8,128)S(1)}, f32[12,16,128]{2,1,0:T(8,128)S(1)}, u32[]{:S(2)}, u32[]{:S(2)}) %collective-permute-start.1) | collective-permute-done | bytes 98336 | tf_op jit(solution)/shard_map/ppermute | solution.py:174
  15.8 0.0 collective-permute-done.2
  15.8 0.0 copy-start.5
  15.8 0.0 copy-start.6
  15.8 0.0 copy-start.7
  15.8 0.0 copy-start.8
  15.8 0.0 copy-start.9
  15.8 0.0 copy-start.10
  15.8 0.1 fusion.2
  15.9 1.6 %collective-permute-start.3 = (f32[4,12,16,128]{3,2,1,0:T(8,128)S(1)}, f32[4,12,16,128]{3,2,1,0:T(8,128)S(1)}, u32[]{:S(2)}, u32[]{:S(2)}) collective-permute-start(f32[4,12,16,128]{3,2,1,0:T(8,128)S(1)} %get-tuple-element.12), channel_id=1, source_target_pairs={{0,2},{2,0},{1,3},{3,1},{4,6},{6,4},{5,7},{7,5},{8,10},{10,8},{9,1... | collective-permute-start | bytes 1179656 | tf_op jit(solution)/shard_map/ppermute | solution.py:174
  17.4 7.5 %collective-permute-done.3 = f32[4,12,16,128]{3,2,1,0:T(8,128)S(1)} collective-permute-done((f32[4,12,16,128]{3,2,1,0:T(8,128)S(1)}, f32[4,12,16,128]{3,2,1,0:T(8,128)S(1)}, u32[]{:S(2)}, u32[]{:S(2)}) %collective-permute-start.3) | collective-permute-done | bytes 393248 | tf_op jit(solution)/shard_map/ppermute | solution.py:174
  24.9 0.2 fusion.1
  25.1 0.1 collective-permute-start.4
  25.2 0.1 pad_add_fusion.2.place_ref
  25.2 0.0 copy-done.5
  25.3 0.0 copy-done.6
  25.3 0.0 copy-done.7
  25.3 0.0 copy-done.8
  25.3 0.0 copy-done.9
  25.3 0.0 copy-done.10
  25.3 2.1 %collective-permute-done.4 = f32[2,4,12,16,128]{4,3,2,1,0:T(8,128)S(1)} collective-permute-done((f32[2,4,12,16,128]{4,3,2,1,0:T(8,128)S(1)}, f32[2,4,12,16,128]{4,3,2,1,0:T(8,128)S(1)}, u32[]{:S(2)}, u32[]{:S(2)}) %collective-permute-start.4) | collective-permute-done | bytes 786464 | tf_op jit(solution)/shard_map/ppermute | solution.py:174
  27.4 0.0 copy-start.1
  27.4 0.0 copy-start.2
  27.4 0.0 copy-start.3
  27.4 0.0 copy-start.4
  27.4 0.1 pad_maximum_fusion.blocks_ref
  27.6 0.9 %copy-done.1 = bf16[512,512]{1,0:T(8,128)(2,1)S(1)} copy-done((bf16[512,512]{1,0:T(8,128)(2,1)S(1)}, bf16[512,512]{1,0:T(8,128)(2,1)}, u32[]{:S(2)}) %copy-start.1) | copy-done | bytes 524312
  28.5 0.0 copy-done.2
  28.5 0.0 copy-done.3
  28.5 0.0 copy-done.4
  28.5 11.3 %shard_map.148 = (f32[4,16,128]{2,1,0:T(8,128)}, f32[2,4,16,256]{3,2,1,0:T(8,128)}, f32[8,32]{1,0:T(8,128)}) custom-call(s32[3]{0:T(128)S(1)} %pad_add_fusion.2.place_ref, f32[4,8]{1,0:T(4,128)S(1)} %copy-done.3, s32[3,8]{1,0:T(4,128)S(1)} %pad_add_fusion.source_ref, s32[2]{0:T(128)S(1)} %copy-done.4, s32[3,32]{1,0:T(4,128)S(1)} %pad_add_fusion.1.receiver_ref, ...), custom_call_target="tpu_custom_call" | custom-call | tf_op jit(solution)/shard_map/pallas_call | solution.py:311
  (3 shorter events, 0.0 us)
Async XLA Ops:
  0.6 0.8 %copy-start = (f32[4,16,256]{2,1,0:T(8,128)S(1)}, f32[4,16,256]{2,1,0:T(8,128)}, u32[]{:S(2)}) copy-start(f32[4,16,256]{2,1,0:T(8,128)} %param.13) | copy-start | bytes 196612
  2.3 5.9 %collective-permute-start = (f32[12,16,128]{2,1,0:T(8,128)S(1)}, f32[12,16,128]{2,1,0:T(8,128)S(1)}, u32[]{:S(2)}, u32[]{:S(2)}) collective-permute-start(f32[12,16,128]{2,1,0:T(8,128)S(1)} %get-tuple-element.14), channel_id=1, source_target_pairs={{0,4},{4,0},{8,12},{12,8},{1,5},{5,1},{9,13},{13,9},{2,6},{6,2},{1... | collective-permute-start | bytes 294920 | tf_op jit(solution)/shard_map/ppermute | solution.py:174
  5.4 10.4 %collective-permute-start.1 = (f32[12,16,128]{2,1,0:T(8,128)S(1)}, f32[12,16,128]{2,1,0:T(8,128)S(1)}, u32[]{:S(2)}, u32[]{:S(2)}) collective-permute-start(f32[12,16,128]{2,1,0:T(8,128)S(1)} %get-tuple-element.14), channel_id=1, source_target_pairs={{0,8},{4,12},{8,0},{12,4},{1,9},{5,13},{9,1},{13,5},{2,10},{6,14},... | collective-permute-start | bytes 294920 | tf_op jit(solution)/shard_map/ppermute | solution.py:174
  7.9 7.8 %collective-permute-start.2 = (f32[12,16,128]{2,1,0:T(8,128)S(1)}, f32[12,16,128]{2,1,0:T(8,128)S(1)}, u32[]{:S(2)}, u32[]{:S(2)}) collective-permute-start(f32[12,16,128]{2,1,0:T(8,128)S(1)} %get-tuple-element.14), channel_id=1, source_target_pairs={{0,12},{4,8},{8,4},{12,0},{1,13},{5,9},{9,5},{13,1},{2,14},{6,10},... | collective-permute-start | bytes 294920 | tf_op jit(solution)/shard_map/ppermute | solution.py:174
  15.8 9.5 %copy-start.5 = (s32[8]{0:T(128)S(1)}, s32[8]{0:T(128)}, u32[]{:S(2)}) copy-start(s32[8]{0:T(128)} %param.19) | copy-start | bytes 100
  15.8 9.5 %copy-start.6 = (s32[8]{0:T(128)S(1)}, s32[8]{0:T(128)}, u32[]{:S(2)}) copy-start(s32[8]{0:T(128)} %param.18) | copy-start | bytes 100
  15.8 9.5 %copy-start.7 = (s32[8]{0:T(128)S(1)}, s32[8]{0:T(128)}, u32[]{:S(2)}) copy-start(s32[8]{0:T(128)} %param.17) | copy-start | bytes 100
  15.8 9.5 %copy-start.8 = (s32[32]{0:T(128)S(1)}, s32[32]{0:T(128)}, u32[]{:S(2)}) copy-start(s32[32]{0:T(128)} %param.23) | copy-start | bytes 388
  15.8 9.5 %copy-start.9 = (s32[32]{0:T(128)S(1)}, s32[32]{0:T(128)}, u32[]{:S(2)}) copy-start(s32[32]{0:T(128)} %param.22) | copy-start | bytes 388
  15.8 9.5 %copy-start.10 = (s32[32]{0:T(128)S(1)}, s32[32]{0:T(128)}, u32[]{:S(2)}) copy-start(s32[32]{0:T(128)} %param.21) | copy-start | bytes 388
  15.9 9.0 %collective-permute-start.3 = (f32[4,12,16,128]{3,2,1,0:T(8,128)S(1)}, f32[4,12,16,128]{3,2,1,0:T(8,128)S(1)}, u32[]{:S(2)}, u32[]{:S(2)}) collective-permute-start(f32[4,12,16,128]{3,2,1,0:T(8,128)S(1)} %get-tuple-element.12), channel_id=1, source_target_pairs={{0,2},{2,0},{1,3},{3,1},{4,6},{6,4},{5,7},{7,5},{8,10},{10,8},{9,1... | collective-permute-start | bytes 1179656 | tf_op jit(solution)/shard_map/ppermute | solution.py:174
  25.1 2.4 %collective-permute-start.4 = (f32[2,4,12,16,128]{4,3,2,1,0:T(8,128)S(1)}, f32[2,4,12,16,128]{4,3,2,1,0:T(8,128)S(1)}, u32[]{:S(2)}, u32[]{:S(2)}) collective-permute-start(f32[2,4,12,16,128]{4,3,2,1,0:T(8,128)S(1)} %get-tuple-element.10), channel_id=1, source_target_pairs={{0,1},{1,0},{2,3},{3,2},{4,5},{5,4},{6,7},{7,6},{8,9},{9,8},{10,11... | collective-permute-start | bytes 2359304 | tf_op jit(solution)/shard_map/ppermute | solution.py:174
  27.4 1.0 %copy-start.1 = (bf16[512,512]{1,0:T(8,128)(2,1)S(1)}, bf16[512,512]{1,0:T(8,128)(2,1)}, u32[]{:S(2)}) copy-start(bf16[512,512]{1,0:T(8,128)(2,1)} %constant.21.clone.rows_op_ref) | copy-start | bytes 1572868
  27.4 1.1 %copy-start.2 = (bf16[256,256]{1,0:T(8,128)(2,1)S(1)}, bf16[256,256]{1,0:T(8,128)(2,1)}, u32[]{:S(2)}) copy-start(bf16[256,256]{1,0:T(8,128)(2,1)} %constant.22.clone.wide_op_ref) | copy-start | bytes 393220
  27.4 1.1 %copy-start.3 = (f32[4,8]{1,0:T(4,128)S(1)}, f32[4,8]{1,0:T(4,128)}, u32[]{:S(2)}) copy-start(f32[4,8]{1,0:T(4,128)} %wavelet_ref.1) | copy-start | bytes 388
  27.4 1.1 %copy-start.4 = (s32[2]{0:T(128)S(1)}, s32[2]{0:T(128)}, u32[]{:S(2)}) copy-start(s32[2]{0:T(128)} %seeds_ref.1) | copy-start | bytes 28

commit v2 on v0

--- a/solution.py
+++ b/solution.py
@@ -1,13 +1,21 @@
+import functools
+
 import jax
 import jax.numpy as jnp
+import numpy as np
 from jax import lax
+from jax.experimental import pallas as pl
+from jax.experimental.pallas import tpu as pltpu
 from jax.sharding import PartitionSpec as P
 
 STEPS = 4
+GRID_ROWS = 512
 
 
 stencil_coeffs = (-205.0 / 72.0, 8.0 / 5.0, -1.0 / 5.0, 8.0 / 315.0, -1.0 / 560.0)
 pert_scale = 0.2
+whole_coeffs = (-14350, 8064, -1008, 128, -9)
+coeff_scale = 5040.0
 
 
 def padded_2(array, sides, width):
@@ -94,7 +102,7 @@
     return jnp.where(inside[None, :], picked, jnp.zeros_like(picked))
 
 
-def shards(
+def halo_shards(
     courant,
     incident_prev,
     incident_now,
@@ -145,27 +153,424 @@
     return (incident_final, wave_now, traces)
 
 
+def band(apart):
+    value = jnp.zeros(apart.shape, jnp.float32)
+    for k in range(1, 5):
+        value = jnp.where(apart == k, float(whole_coeffs[k]), value)
+    return value
+
+
+def split3(value):
+    high = value.astype(jnp.bfloat16)
+    rest = value - high.astype(jnp.float32)
+    middle = rest.astype(jnp.bfloat16)
+    low = (rest - middle.astype(jnp.float32)).astype(jnp.bfloat16)
+    return high, middle, low
+
+
+def product(left, right):
+    return jnp.dot(left, right, preferred_element_type=jnp.float32)
+
+
+def across(row, column, tall):
+    far_z = jnp.abs(lax.div(row, tall) - lax.div(column, tall))
+    far_y = jnp.abs(lax.rem(row, tall) - lax.rem(column, tall))
+    return band(jnp.where(far_y == 0, far_z, jnp.where(far_z == 0, far_y, 0)))
+
+
+def seam(value, tall, run):
+    planes = value.shape[0] // tall
+    sums = {}
+    for z in range(planes):
+        for k in range(1, 5):
+            for other in (z - k, z + k):
+                if 0 <= other < planes and other // run != z // run:
+                    term = float(whole_coeffs[k]) * value[other * tall : (other + 1) * tall]
+                    sums[z] = sums[z] + term if z in sums else term
+    return sums
+
+
+def doubled_contrast(cell, seed):
+    hashed = cell + seed * 668265263
+    hashed = hashed ^ (hashed >> 15)
+    hashed = hashed * 1274126177
+    hashed = hashed ^ (hashed >> 13)
+    fraction = (hashed & 65535).astype(jnp.float32) / 65535.0
+    return 2.0 * (pert_scale * (2.0 * fraction - 1.0))
+
+
+def fetched(sources, targets, semaphores):
+    copies = [
+        pltpu.make_async_copy(source, target, semaphores.at[i])
+        for i, (source, target) in enumerate(zip(sources, targets, strict=True))
+    ]
+    for copy in copies:
+        copy.start()
+    return copies
+
+
+def pack_kernel(now_ref, prev_ref, courant_ref, own_ref, semaphores):
+    layers, _, part_width = now_ref.shape
+    rep = lax.axis_index("rep")
+    sources = [now_ref, prev_ref]
+    for x in range(2):
+        at_x = pl.multiple_of((rep ^ x) * part_width, part_width)
+        sources.append(courant_ref.at[:, :, pl.ds(at_x, part_width)])
+    targets = [own_ref.at[pl.ds(i * layers, layers)] for i in range(4)]
+    for copy in fetched(sources, targets, semaphores):
+        copy.wait()
+
+
+def prepare_kernel(own_shape, *refs):
+    place_ref, refs = refs[0], refs[1:]
+    given, outputs, held, semaphores = refs[:8], refs[8:16], refs[16:24], refs[24]
+    contrast_ref, force_ref, last_contrast_ref, last_force_ref = outputs[:4]
+    rows_ref, wide_ref, last_ref, mask_ref = outputs[4:]
+    wavelet_ref, source_z_ref, source_y_ref, source_x_ref = held[:4]
+    seeds_ref, receiver_z_ref, receiver_y_ref, receiver_x_ref = held[4:]
+    copies = fetched(given, held, semaphores)
+    deep, tall, wide = force_ref.shape[1:]
+    rows = deep * tall
+    runs, tops, block = rows_ref.shape[0], rows_ref.shape[1], rows_ref.shape[2] // 3
+    receivers = mask_ref.shape[0]
+    deep_count, tall_count = own_shape
+    own = deep_count * tall_count
+    replicas = seeds_ref.shape[0]
+    sources = range(source_z_ref.shape[0])
+    line = lax.broadcasted_iota(jnp.int32, (wide, wide), 0)
+    beside = band(jnp.abs(line - lax.broadcasted_iota(jnp.int32, (wide, wide), 1)))
+    for part in range(3):
+        wide_ref[part * wide : (part + 1) * wide, :] = beside.astype(jnp.bfloat16)
+    for copy in copies:
+        copy.wait()
+    z_of = lax.broadcasted_iota(jnp.int32, (deep, tall, wide), 0)
+    y_of = lax.broadcasted_iota(jnp.int32, (deep, tall, wide), 1)
+    x_of = lax.broadcasted_iota(jnp.int32, (deep, tall, wide), 2)
+    cell = z_of * 73856093 + y_of * 19349663 + x_of * 83492791
+    for r in range(replicas):
+        contrast_ref[r] = doubled_contrast(cell, seeds_ref[r])
+    lane = lax.broadcasted_iota(jnp.int32, (1, wide), 1)
+    force_ref[...] = jnp.zeros_like(force_ref)
+    for n in range(STEPS - 1):
+        for k in sources:
+            at = (n, source_z_ref[k], pl.ds(source_y_ref[k], 1), slice(None))
+            force_ref[at] += jnp.where(lane == source_x_ref[k], wavelet_ref[n, k], 0.0)
+    index = lax.broadcasted_iota(jnp.int32, (own + receivers, 1), 0)
+    row = (place_ref[0] * deep_count + lax.div(index, tall_count)) * tall
+    row += place_ref[1] * tall_count + lax.rem(index, tall_count)
+    for j in range(receivers):
+        row = jnp.where(index == own + j, receiver_z_ref[j] * tall + receiver_y_ref[j], row)
+        mask_ref[pl.ds(j, 1), :] = jnp.where(lane == receiver_x_ref[j], 1.0, 0.0)
+    cell = lax.div(row, tall) * 73856093 + lax.rem(row, tall) * 19349663 + lane * 83492791
+    for r in range(replicas):
+        last_contrast_ref[r] = doubled_contrast(cell, seeds_ref[r])
+    force = jnp.zeros((own + receivers, wide), jnp.float32)
+    for k in sources:
+        here = (row == source_z_ref[k] * tall + source_y_ref[k]) & (lane == source_x_ref[k])
+        force += jnp.where(here, wavelet_ref[STEPS - 1, k], 0.0)
+    last_force_ref[...] = force
+    column = lax.broadcasted_iota(jnp.int32, (1, rows), 1)
+    taken = jnp.where(row[own:] == column, 1.0, 0.0)
+    last = jnp.concatenate([across(row, column, tall), taken], axis=0).astype(jnp.bfloat16)
+    line = lax.broadcasted_iota(jnp.int32, (block, 1), 0)
+    inner = across(line, column[:, :block], tall).astype(jnp.bfloat16)
+    for part in range(3):
+        last_ref[:, part * rows : (part + 1) * rows] = last
+        for run in range(runs):
+            here = (run, slice(0, block), slice(part * block, (part + 1) * block))
+            rows_ref[here] = inner
+            here = (run, slice(block, tops), slice(part * block, (part + 1) * block))
+            rows_ref[here] = taken[:, run * block : (run + 1) * block].astype(jnp.bfloat16)
+
+
+def step_kernel(
+    layout,
+    own_shape,
+    place_ref,
+    contrast_ref,
+    force_ref,
+    last_contrast_ref,
+    last_force_ref,
+    rows_ref,
+    wide_ref,
+    last_ref,
+    mask_ref,
+    *refs,
+):
+    blocks, refs = refs[:-8], refs[-8:]
+    incident_ref, scattered_ref, traces_ref, field_ref, speed_ref, drive_ref, wave_ref, slim_ref = refs
+    deep, tall, wide = speed_ref.shape
+    rows = deep * tall
+    shape, cube = (rows, wide), (deep, tall, wide)
+    deep_count, tall_count, part_width = own_shape
+    own = deep_count * tall_count
+    replicas = contrast_ref.shape[0]
+    receivers = mask_ref.shape[0]
+    runs, block = rows_ref.shape[0], rows_ref.shape[2] // 3
+    run = block // tall
+    slab, sub, rep = place_ref[0], place_ref[1], place_ref[2]
+
+    for number, layer, what, x, y, z in layout:
+        at = (
+            pl.ds(pl.multiple_of((slab ^ z) * deep_count, deep_count), deep_count),
+            pl.ds(pl.multiple_of((sub ^ y) * tall_count, tall_count), tall_count),
+        )
+        at += (pl.ds(pl.multiple_of((rep ^ x) * part_width, part_width), part_width),)
+        piece = blocks[number][layer : layer + deep_count]
+        if what == "courant":
+            speed_ref[at] = piece * piece * (1.0 / coeff_scale)
+        else:
+            field_ref[(("now", "prev").index(what),) + at] = piece
+
+    def applied(value):
+        parts = split3(value)
+        total = (3.0 * whole_coeffs[0]) * value
+        total += product(jnp.concatenate(parts, axis=1), wide_ref[...])
+        down, taken = [], None
+        for number in range(runs):
+            here = slice(number * block, (number + 1) * block)
+            result = product(rows_ref[number], jnp.concatenate([part[here] for part in parts], axis=0))
+            down.append(result[:block])
+            taken = result[block:] if taken is None else taken + result[block:]
+        total += jnp.concatenate(down, axis=0)
+        sums = seam(value, tall, run)
+        pieces = []
+        for z in range(deep):
+            piece = total[z * tall : (z + 1) * tall]
+            pieces.append(piece + sums[z] if z in sums else piece)
+        return jnp.concatenate(pieces, axis=0), taken
+
+    def flat(ref, *index):
+        return ref[index].reshape(shape)
+
+    at_z = pl.multiple_of(slab * deep_count, deep_count)
+    at_y = pl.multiple_of(sub * tall_count, tall_count)
+    at_x = pl.multiple_of(rep * part_width, part_width)
+
+    def owned(ref, *index):
+        here = index + (pl.ds(at_z, deep_count), pl.ds(at_y, tall_count), slice(None))
+        return ref[here].reshape(own, wide)
+
+    samples = [[None] * replicas for _ in range(STEPS)]
+    speed = flat(speed_ref)
+
+    now = flat(field_ref, 0)
+    drive_ref[...] = speed * applied(now)[0] + flat(force_ref, 0)
+    field_ref[1] = (2.0 * now - flat(field_ref, 1) + drive_ref[...]).reshape(cube)
+    for r in range(replicas):
+        wave = flat(contrast_ref, r) * drive_ref[...]
+        wave_ref[0, r] = wave.reshape(cube)
+        result, samples[0][r] = applied(wave)
+        wave_ref[1, r] = (2.0 * wave + speed * result).reshape(cube)
+
+    now = flat(field_ref, 1)
+    drive_ref[...] = speed * applied(now)[0] + flat(force_ref, 1)
+    field_ref[0] = (2.0 * now - flat(field_ref, 0) + drive_ref[...]).reshape(cube)
+    for r in range(replicas):
+        wave_ref[1, r] += (flat(contrast_ref, r) * drive_ref[...]).reshape(cube)
+
+    now = flat(field_ref, 0)
+    drive_ref[...] = speed * applied(now)[0] + flat(force_ref, 2)
+    field_ref[1] = (2.0 * now - flat(field_ref, 1) + drive_ref[...]).reshape(cube)
+    for r in range(replicas):
+        wave = flat(wave_ref, 1, r)
+        result, samples[1][r] = applied(wave)
+        source = flat(contrast_ref, r) * drive_ref[...]
+        wave_ref[0, r] = (
+            2.0 * wave - flat(wave_ref, 0, r) + speed * result + source
+        ).reshape(cube)
+
+    taken = product(last_ref[own + receivers :], jnp.concatenate(split3(speed), axis=0))
+    speed = jnp.concatenate([owned(speed_ref), taken], axis=0)
+
+    def last_applied(value, mine):
+        result = product(last_ref[...], jnp.concatenate(split3(value), axis=0))
+        here = jnp.concatenate([mine, result[own + receivers :]], axis=0)
+        total = (3.0 * whole_coeffs[0]) * here + result[: own + receivers]
+        return total + product(jnp.concatenate(split3(here), axis=1), wide_ref[...]), here
+
+    result, now = last_applied(flat(field_ref, 1), owned(field_ref, 1))
+    drive = speed * result + last_force_ref[...]
+    slim_ref[...] = 2.0 * now[:own] - owned(field_ref, 0) + drive[:own]
+    incident_ref[...] = slim_ref[:, pl.ds(at_x, part_width)].reshape(incident_ref.shape)
+    for r in range(replicas):
+        result, wave = last_applied(flat(wave_ref, 0, r), owned(wave_ref, 0, r))
+        samples[2][r] = wave[own:]
+        before = jnp.concatenate([owned(wave_ref, 1, r), samples[1][r]], axis=0)
+        following = 2.0 * wave - before + speed * result + last_contrast_ref[r] * drive
+        scattered_ref[r] = following[:own].reshape(scattered_ref.shape[1:])
+        samples[3][r] = following[own:]
+    column = lax.broadcasted_iota(jnp.int32, (receivers, 128), 1)
+    gathered = jnp.zeros((receivers, 128), jnp.float32)
+    mask = mask_ref[...]
+    for n in range(STEPS):
+        for r in range(replicas):
+            summed = jnp.sum(samples[n][r] * mask, axis=1, keepdims=True)
+            gathered += jnp.where(column == n * replicas + r, summed, 0.0)
+    traces_ref[...] = jnp.transpose(gathered)[: STEPS * replicas, :]
+
+
+def swapped(array, axis, distance):
+    size = lax.axis_size(axis)
+    return lax.ppermute(array, axis, [(i, i ^ distance) for i in range(size)])
+
+
+def exchanged(own, deep_count, prepared):
+    sent = own[: 3 * deep_count]
+    beyond = {m: swapped(sent, "slab", m) for m in (1, 2, 3)}
+    near = jnp.concatenate([own[: 2 * deep_count], beyond[1]], axis=0)
+    far = jnp.concatenate([beyond[2], beyond[3]], axis=0)
+    far, prepared = lax.optimization_barrier((far, prepared))
+    near_two, far_two = swapped(near, "rep", 1), swapped(far, "rep", 1)
+    near_line = jnp.concatenate([near, near_two, own[2 * deep_count :]], axis=0)
+    blocks = [near_line, far, far_two]
+    blocks += [swapped(block, "sub", 1) for block in blocks]
+    names = ("now", "prev", "courant")
+    near_layout = [(name, 0) for name in names[:2]] + [(name, 1) for name in names]
+    near_layout = [(name, x, z) for x in range(2) for name, z in near_layout]
+    near_layout += [("courant", x, 0) for x in range(2)]
+    far_layout = [(name, m) for m in (2, 3) for name in names]
+    layout = []
+    for y in range(2):
+        for i, (name, x, z) in enumerate(near_layout):
+            layout.append((3 * y, i * deep_count, name, x, y, z))
+        for x in range(2):
+            for i, (name, z) in enumerate(far_layout):
+                layout.append((3 * y + 1 + x, i * deep_count, name, x, y, z))
+    return blocks, tuple(layout), prepared
+
+
+def whole_shards(
+    courant,
+    incident_prev,
+    incident_now,
+    wavelet,
+    source_z,
+    source_y,
+    source_x,
+    replica_seeds,
+    receiver_z,
+    receiver_y,
+    receiver_x,
+):
+    deep_count, tall_count, part_width = incident_now.shape
+    wide = courant.shape[2]
+    slab, sub, rep = (lax.axis_index(axis) for axis in ("slab", "sub", "rep"))
+    deep, tall = lax.axis_size("slab") * deep_count, lax.axis_size("sub") * tall_count
+    rows = deep * tall
+    replicas, receivers = replica_seeds.shape[0], receiver_z.shape[0]
+    own_shape = (deep_count, tall_count, part_width)
+    cube = (deep, tall, wide)
+    last_rows = deep_count * tall_count + receivers
+    block = min(rows, 256)
+    smem = pl.BlockSpec(memory_space=pltpu.SMEM)
+    vmem = pl.BlockSpec(memory_space=pltpu.VMEM)
+    anywhere = pl.BlockSpec(memory_space=pltpu.HBM)
+
+    def held(*shape, dtype=jnp.float32):
+        return jax.ShapeDtypeStruct(shape, dtype)
+
+    def call(kernel, out_shape, scalars, distant, arrays, scratch):
+        return pl.pallas_call(
+            kernel,
+            out_shape=out_shape,
+            in_specs=[smem] * len(scalars) + [anywhere] * len(distant) + [vmem] * len(arrays),
+            out_specs=tuple(vmem for _ in out_shape),
+            scratch_shapes=list(scratch),
+            compiler_params=pltpu.CompilerParams(vmem_limit_bytes=24 * 2**20),
+        )(*scalars, *(pltpu.with_memory_space_constraint(a, pltpu.HBM) for a in distant), *arrays)
+
+    place = jnp.stack([slab, sub, rep]).astype(jnp.int32)
+    given = (
+        wavelet,
+        source_z,
+        source_y,
+        source_x,
+        replica_seeds,
+        receiver_z,
+        receiver_y,
+        receiver_x,
+    )
+    prepared = call(
+        functools.partial(prepare_kernel, own_shape[:2]),
+        (
+            held(replicas, *cube),
+            held(STEPS - 1, *cube),
+            held(replicas, last_rows, wide),
+            held(last_rows, wide),
+            held(rows // block, block + receivers, 3 * block, dtype=jnp.bfloat16),
+            held(3 * wide, wide, dtype=jnp.bfloat16),
+            held(last_rows + receivers, 3 * rows, dtype=jnp.bfloat16),
+            held(receivers, wide),
+        ),
+        (place,),
+        given,
+        (),
+        (
+            *(pltpu.SMEM(array.shape, array.dtype) for array in given),
+            pltpu.SemaphoreType.DMA((len(given),)),
+        ),
+    )
+    own = call(
+        pack_kernel,
+        (held(4 * deep_count, tall_count, part_width),),
+        (),
+        (incident_now, incident_prev, courant),
+        (),
+        (pltpu.SemaphoreType.DMA((4,)),),
+    )[0]
+    blocks, layout, prepared = exchanged(own, deep_count, prepared)
+    incident_final, scattered_final, traces = call(
+        functools.partial(step_kernel, layout, own_shape),
+        (
+            held(*own_shape),
+            held(replicas, deep_count, tall_count, wide),
+            held(STEPS * replicas, receivers),
+        ),
+        (place,),
+        (),
+        (*prepared, *blocks),
+        (
+            pltpu.VMEM((2,) + cube, jnp.float32),
+            pltpu.VMEM(cube, jnp.float32),
+            pltpu.VMEM((rows, wide), jnp.float32),
+            pltpu.VMEM((2, replicas) + cube, jnp.float32),
+            pltpu.VMEM((deep_count * tall_count, wide), jnp.float32),
+        ),
+    )
+    return incident_final, scattered_final, traces.reshape(STEPS, replicas, receivers)
+
+
 def solution(mesh):
-    return jax.shard_map(
-        shards,
-        mesh=mesh,
-        in_specs=(
-            P("slab", "sub", None),
-            P(("shot", "slab"), "sub", "rep"),
-            P(("shot", "slab"), "sub", "rep"),
-            P(),
-            P("shot"),
-            P("shot"),
-            P("shot"),
-            P("rep"),
-            P(),
-            P(),
-            P(),
-        ),
-        out_specs=(
-            P(("shot", "slab"), "sub", "rep"),
-            P("rep", ("shot", "slab"), "sub", None),
-            P("shot", "rep", None),
-        ),
-        check_vma=False,
-    )
+    slabs, subs, reps = (mesh.shape[axis] for axis in ("slab", "sub", "rep"))
+
+    def step(courant, *rest):
+        deep, tall, _ = courant.shape
+        paired = (slabs, subs, reps, mesh.shape["shot"]) == (4, 2, 2, 2)
+        part_width = courant.shape[2] // reps
+        fits = deep * tall <= GRID_ROWS and part_width % 128 == 0
+        return jax.shard_map(
+            whole_shards if paired and fits else halo_shards,
+            mesh=mesh,
+            in_specs=(
+                P("slab", "sub", None),
+                P(("shot", "slab"), "sub", "rep"),
+                P(("shot", "slab"), "sub", "rep"),
+                P(),
+                P("shot"),
+                P("shot"),
+                P("shot"),
+                P("rep"),
+                P(),
+                P(),
+                P(),
+            ),
+            out_specs=(
+                P(("shot", "slab"), "sub", "rep"),
+                P("rep", ("shot", "slab"), "sub", None),
+                P("shot", "rep", None),
+            ),
+            check_vma=False,
+        )(courant, *rest)
+
+    return step

time: 164 us -> 31.5 us (0.19)
  starting transfers between devices: 59.5 us -> 9.61 us
  blocking collectives: 26.8 us -> 0 us
  waiting for transfers between devices: 35.4 us -> 9.7 us
  local copies, waits for them, and re-layouts: 25.4 us -> 0.02 us
  other arithmetic: 14.7 us -> 0.13 us
  Pallas kernels: 0 us -> 11.1 us
    ppermute x32 -> x8, starting transfers between devices: 59.5 us -> 9.61 us  [swapped(): return lax.ppermute(array, axis, [(i, i ^ distance) for i in range(size)])]
    ppermute x32 -> x8, waiting for transfers between devices: 35.4 us -> 9.7 us  [swapped(): return lax.ppermute(array, axis, [(i, i ^ distance) for i in range(size)])]
    add x4 -> x0, local copies, waits for them, and re-layouts: 18.7 us -> none  [shards(): 2.0 * wave_now - wave_prev + speed_square * laplace(wave_padded)]
    psum x1 -> x0, blocking collectives: 15.9 us -> none  [shards(): picked = lax.psum(picked, ('slab', 'sub'))]
    pallas_call x0 -> x3, Pallas kernels: none -> 11.1 us  [call(): pl.pallas_call(kernel, out_shape=out_shape, in_specs=[smem] * len(scalars...]
    all_gather x2 -> x0, blocking collectives: 10.9 us -> none  [the longest x1 5.89 us: shards(): lax.all_gather(incident_now, 'rep', axis=2, tiled=True)]
    gather x4 -> x0, local copies, waits for them, and re-layouts: 5.42 us -> none  [sample(): picked = field[:, clip_z, clip_y, where_x]]
    add x10 -> x0, other arithmetic: 4.17 us -> none  [the longest x4 2.49 us: shards(): whole_next = 2.0 * whole_now - whole_prev + speed_square * laplace(padded)]
  transfers between devices with their start and end apart: 32 -> 8, of which waited for: 14 -> 5; matrix products, arithmetic and copies ran while one was open for 17% -> 0% of each run, Pallas kernels for 0% -> 9%
where the time goes in v2:
time: 31.5 us; the launch traced here: 31.3 us
  Pallas kernels  11.1 us (35%)
  waiting for transfers between devices  9.7 us (31%)
  starting transfers between devices  9.61 us (31%)
  between operations  0.69 us (2%)
    pallas_call x3, Pallas kernels, call(): pl.pallas_call(kernel, out_shape=out_shape, in_specs=[smem] * len(scalars...  11.1 us
    ppermute x8, waiting for transfers between devices, swapped(): return lax.ppermute(array, axis, [(i, i ^ distance) for i in range(size)])  9.7 us
    ppermute x8, starting transfers between devices, swapped(): return lax.ppermute(array, axis, [(i, i ^ distance) for i in range(size)])  9.61 us
  transfers between devices with their start and end apart: 8, of which 5 were waited for; matrix products, arithmetic and copies ran while one was open for 0% of the time, Pallas kernels for 9%

profile of v2, /device:TPU:0, one launch (start us, length us, event | category | flops | bytes accessed | tf_op | source)
XLA Modules:
  0.0 31.3 jit_solution(7386527825215065768)
XLA Ops:
  0.6 0.8 %shard_map.130 = f32[16,16,128]{2,1,0:T(8,128)S(1)} custom-call(f32[4,16,128]{2,1,0:T(8,128)} %now_ref.1, f32[4,16,128]{2,1,0:T(8,128)} %prev_ref.1, f32[4,16,256]{2,1,0:T(8,128)} %courant_ref.1), custom_call_target="tpu_custom_call" | custom-call | tf_op jit(solution)/shard_map/pallas_call | solution.py:474
  1.5 3.1 %collective-permute-start.2 = (f32[12,16,128]{2,1,0:T(8,128)S(1)}, f32[12,16,128]{2,1,0:T(8,128)S(1)}, u32[]{:S(2)}, u32[]{:S(2)}) collective-permute-start(f32[12,16,128]{2,1,0:T(8,128)S(1)} %slice.12), channel_id=1, source_target_pairs={{0,4},{4,0},{8,12},{12,8},{1,5},{5,1},{9,13},{13,9},{2,6},{6,2},{1... | collective-permute-start | bytes 294920 | tf_op jit(solution)/shard_map/ppermute | solution.py:415
  4.6 2.5 %collective-permute-start.1 = (f32[12,16,128]{2,1,0:T(8,128)S(1)}, f32[12,16,128]{2,1,0:T(8,128)S(1)}, u32[]{:S(2)}, u32[]{:S(2)}) collective-permute-start(f32[12,16,128]{2,1,0:T(8,128)S(1)} %slice.12), channel_id=1, source_target_pairs={{0,12},{4,8},{8,4},{12,0},{1,13},{5,9},{9,5},{13,1},{2,14},{6,10},... | collective-permute-start | bytes 294920 | tf_op jit(solution)/shard_map/ppermute | solution.py:415
  7.1 0.1 collective-permute-start
  7.2 0.2 collective-permute-done.2
  7.4 1.8 %collective-permute-start.3 = (f32[20,16,128]{2,1,0:T(8,128)S(1)}, f32[20,16,128]{2,1,0:T(8,128)S(1)}, u32[]{:S(2)}, u32[]{:S(2)}) collective-permute-start(f32[20,16,128]{2,1,0:T(8,128)S(1)} %pad_maximum_fusion.2), channel_id=1, source_target_pairs={{0,2},{2,0},{1,3},{3,1},{4,6},{6,4},{5,7},{7,5},{8,10},{10,8},{9,1... | collective-permute-start | bytes 491528 | tf_op jit(solution)/shard_map/ppermute | solution.py:415
  9.2 0.1 pad_add_fusion.refs_0_.place_ref
  9.3 2.9 %shard_map.131 = (f32[2,16,32,256]{3,2,1,0:T(8,128)S(1)}, f32[3,16,32,256]{3,2,1,0:T(8,128)S(1)}, f32[2,96,256]{2,1,0:T(8,128)S(1)}, f32[96,256]{1,0:T(8,128)S(1...) custom-call(s32[3]{0:T(128)S(1)} %pad_add_fusion.refs_0_.place_ref, ...), custom_call_target="tpu_custom_call" | custom-call | tf_op jit(solution)/shard_map/pallas_call | solution.py:474
  12.2 0.5 %collective-permute-done.1 = f32[12,16,128]{2,1,0:T(8,128)S(1)} collective-permute-done((f32[12,16,128]{2,1,0:T(8,128)S(1)}, f32[12,16,128]{2,1,0:T(8,128)S(1)}, u32[]{:S(2)}, u32[]{:S(2)}) %collective-permute-start.1) | collective-permute-done | bytes 98336 | tf_op jit(solution)/shard_map/ppermute | solution.py:415
  12.7 3.3 %collective-permute-done = f32[12,16,128]{2,1,0:T(8,128)S(1)} collective-permute-done((f32[12,16,128]{2,1,0:T(8,128)S(1)}, f32[12,16,128]{2,1,0:T(8,128)S(1)}, u32[]{:S(2)}, u32[]{:S(2)}) %collective-permute-start) | collective-permute-done | bytes 98336 | tf_op jit(solution)/shard_map/ppermute | solution.py:415
  16.0 1.6 %collective-permute-start.4 = (f32[24,16,128]{2,1,0:T(8,128)S(1)}, f32[24,16,128]{2,1,0:T(8,128)S(1)}, u32[]{:S(2)}, u32[]{:S(2)}) collective-permute-start(f32[24,16,128]{2,1,0:T(8,128)S(1)} %pad_maximum_fusion.1.refs_1_), channel_id=1, source_target_pairs={{0,2},{2,0},{1,3},{3,1},{4,6},{6,4},{5,7},{7,5},{8,10},{10,8},{9,1... | collective-permute-start | bytes 589832 | tf_op jit(solution)/shard_map/ppermute | solution.py:415
  17.6 0.0 collective-permute-done.3
  17.6 0.1 collective-permute-start.5
  17.7 0.5 %collective-permute-start.6 = (f32[24,16,128]{2,1,0:T(8,128)S(1)}, f32[24,16,128]{2,1,0:T(8,128)S(1)}, u32[]{:S(2)}, u32[]{:S(2)}) collective-permute-start(f32[24,16,128]{2,1,0:T(8,128)S(1)} %pad_maximum_fusion.1.refs_1_), channel_id=1, source_target_pairs={{0,1},{1,0},{2,3},{3,2},{4,5},{5,4},{6,7},{7,6},{8,9},{9,8},{10,11... | collective-permute-start | bytes 589832 | tf_op jit(solution)/shard_map/ppermute | solution.py:415
  18.2 4.3 %collective-permute-done.4.refs_2_ = f32[24,16,128]{2,1,0:T(8,128)S(1)} collective-permute-done((f32[24,16,128]{2,1,0:T(8,128)S(1)}, f32[24,16,128]{2,1,0:T(8,128)S(1)}, u32[]{:S(2)}, u32[]{:S(2)}) %collective-permute-start.4) | collective-permute-done | bytes 196640 | tf_op jit(solution)/shard_map/ppermute | solution.py:415
  22.5 0.0 collective-permute-start.7
  22.5 0.0 collective-permute-done.6.refs_4_
  22.5 1.4 %collective-permute-done.7.refs_5_ = f32[24,16,128]{2,1,0:T(8,128)S(1)} collective-permute-done((f32[24,16,128]{2,1,0:T(8,128)S(1)}, f32[24,16,128]{2,1,0:T(8,128)S(1)}, u32[]{:S(2)}, u32[]{:S(2)}) %collective-permute-start.7) | collective-permute-done | bytes 196640 | tf_op jit(solution)/shard_map/ppermute | solution.py:415
  23.9 0.0 collective-permute-done.5.refs_3_
  23.9 7.3 %shard_map.132 = (f32[4,16,128]{2,1,0:T(8,128)}, f32[2,4,16,256]{3,2,1,0:T(8,128)}, f32[8,32]{1,0:T(8,128)}) custom-call(s32[3]{0:T(128)S(1)} %pad_add_fusion.refs_0_.place_ref, f32[2,16,32,256]{3,2,1,0:T(8,128)S(1)} %get-tuple-element.31.contrast_ref, f32[3,16,32,256]{3,2,1,0:T(8,128)S(1)} %get-tuple-element.32.force_ref, ...), custom_call_target="tpu_custom_call" | custom-call | tf_op jit(solution)/shard_map/pallas_call | solution.py:474
  (5 shorter events, 0.1 us)
Async XLA Ops:
  1.5 5.9 %collective-permute-start.2 = (f32[12,16,128]{2,1,0:T(8,128)S(1)}, f32[12,16,128]{2,1,0:T(8,128)S(1)}, u32[]{:S(2)}, u32[]{:S(2)}) collective-permute-start(f32[12,16,128]{2,1,0:T(8,128)S(1)} %slice.12), channel_id=1, source_target_pairs={{0,4},{4,0},{8,12},{12,8},{1,5},{5,1},{9,13},{13,9},{2,6},{6,2},{1... | collective-permute-start | bytes 294920 | tf_op jit(solution)/shard_map/ppermute | solution.py:415
  4.6 8.2 %collective-permute-start.1 = (f32[12,16,128]{2,1,0:T(8,128)S(1)}, f32[12,16,128]{2,1,0:T(8,128)S(1)}, u32[]{:S(2)}, u32[]{:S(2)}) collective-permute-start(f32[12,16,128]{2,1,0:T(8,128)S(1)} %slice.12), channel_id=1, source_target_pairs={{0,12},{4,8},{8,4},{12,0},{1,13},{5,9},{9,5},{13,1},{2,14},{6,10},... | collective-permute-start | bytes 294920 | tf_op jit(solution)/shard_map/ppermute | solution.py:415
  7.1 8.9 %collective-permute-start = (f32[12,16,128]{2,1,0:T(8,128)S(1)}, f32[12,16,128]{2,1,0:T(8,128)S(1)}, u32[]{:S(2)}, u32[]{:S(2)}) collective-permute-start(f32[12,16,128]{2,1,0:T(8,128)S(1)} %slice.12), channel_id=1, source_target_pairs={{0,8},{4,12},{8,0},{12,4},{1,9},{5,13},{9,1},{13,5},{2,10},{6,14},... | collective-permute-start | bytes 294920 | tf_op jit(solution)/shard_map/ppermute | solution.py:415
  7.4 10.2 %collective-permute-start.3 = (f32[20,16,128]{2,1,0:T(8,128)S(1)}, f32[20,16,128]{2,1,0:T(8,128)S(1)}, u32[]{:S(2)}, u32[]{:S(2)}) collective-permute-start(f32[20,16,128]{2,1,0:T(8,128)S(1)} %pad_maximum_fusion.2), channel_id=1, source_target_pairs={{0,2},{2,0},{1,3},{3,1},{4,6},{6,4},{5,7},{7,5},{8,10},{10,8},{9,1... | collective-permute-start | bytes 491528 | tf_op jit(solution)/shard_map/ppermute | solution.py:415
  16.0 6.5 %collective-permute-start.4 = (f32[24,16,128]{2,1,0:T(8,128)S(1)}, f32[24,16,128]{2,1,0:T(8,128)S(1)}, u32[]{:S(2)}, u32[]{:S(2)}) collective-permute-start(f32[24,16,128]{2,1,0:T(8,128)S(1)} %pad_maximum_fusion.1.refs_1_), channel_id=1, source_target_pairs={{0,2},{2,0},{1,3},{3,1},{4,6},{6,4},{5,7},{7,5},{8,10},{10,8},{9,1... | collective-permute-start | bytes 589832 | tf_op jit(solution)/shard_map/ppermute | solution.py:415
  17.6 6.3 %collective-permute-start.5 = (f32[48,16,128]{2,1,0:T(8,128)S(1)}, f32[48,16,128]{2,1,0:T(8,128)S(1)}, u32[]{:S(2)}, u32[]{:S(2)}) collective-permute-start(f32[48,16,128]{2,1,0:T(8,128)S(1)} %pad_maximum_fusion.refs_0_), channel_id=1, source_target_pairs={{0,1},{1,0},{2,3},{3,2},{4,5},{5,4},{6,7},{7,6},{8,9},{9,8},{10,11... | collective-permute-start | bytes 1179656 | tf_op jit(solution)/shard_map/ppermute | solution.py:415
  17.7 4.8 %collective-permute-start.6 = (f32[24,16,128]{2,1,0:T(8,128)S(1)}, f32[24,16,128]{2,1,0:T(8,128)S(1)}, u32[]{:S(2)}, u32[]{:S(2)}) collective-permute-start(f32[24,16,128]{2,1,0:T(8,128)S(1)} %pad_maximum_fusion.1.refs_1_), channel_id=1, source_target_pairs={{0,1},{1,0},{2,3},{3,2},{4,5},{5,4},{6,7},{7,6},{8,9},{9,8},{10,11... | collective-permute-start | bytes 589832 | tf_op jit(solution)/shard_map/ppermute | solution.py:415
  22.5 1.4 %collective-permute-start.7 = (f32[24,16,128]{2,1,0:T(8,128)S(1)}, f32[24,16,128]{2,1,0:T(8,128)S(1)}, u32[]{:S(2)}, u32[]{:S(2)}) collective-permute-start(f32[24,16,128]{2,1,0:T(8,128)S(1)} %collective-permute-done.4.refs_2_), channel_id=1, source_target_pairs={{0,1},{1,0},{2,3},{3,2},{4,5},{5,4},{6,7},{7,6},{8,9},{9,8},{10,11... | collective-permute-start | bytes 589832 | tf_op jit(solution)/shard_map/ppermute | solution.py:415

commit v3 on v2

--- a/solution.py
+++ b/solution.py
@@ -10,6 +10,8 @@
 
 STEPS = 4
 GRID_ROWS = 512
+CHUNK = 2
+WAVE_PARTS = 2
 
 
 stencil_coeffs = (-205.0 / 72.0, 8.0 / 5.0, -1.0 / 5.0, 8.0 / 315.0, -1.0 / 560.0)
@@ -160,12 +162,13 @@
     return value
 
 
-def split3(value):
-    high = value.astype(jnp.bfloat16)
-    rest = value - high.astype(jnp.float32)
-    middle = rest.astype(jnp.bfloat16)
-    low = (rest - middle.astype(jnp.float32)).astype(jnp.bfloat16)
-    return high, middle, low
+def split(value, count):
+    parts = []
+    for part in range(count):
+        parts.append(value.astype(jnp.bfloat16))
+        if part < count - 1:
+            value = value - parts[-1].astype(jnp.float32)
+    return parts
 
 
 def product(left, right):
@@ -176,18 +179,6 @@
     far_z = jnp.abs(lax.div(row, tall) - lax.div(column, tall))
     far_y = jnp.abs(lax.rem(row, tall) - lax.rem(column, tall))
     return band(jnp.where(far_y == 0, far_z, jnp.where(far_z == 0, far_y, 0)))
-
-
-def seam(value, tall, run):
-    planes = value.shape[0] // tall
-    sums = {}
-    for z in range(planes):
-        for k in range(1, 5):
-            for other in (z - k, z + k):
-                if 0 <= other < planes and other // run != z // run:
-                    term = float(whole_coeffs[k]) * value[other * tall : (other + 1) * tall]
-                    sums[z] = sums[z] + term if z in sums else term
-    return sums
 
 
 def doubled_contrast(cell, seed):
@@ -275,8 +266,9 @@
     line = lax.broadcasted_iota(jnp.int32, (block, 1), 0)
     inner = across(line, column[:, :block], tall).astype(jnp.bfloat16)
     for part in range(3):
-        last_ref[:, part * rows : (part + 1) * rows] = last
         for run in range(runs):
+            start = (3 * run + part) * block
+            last_ref[:, start : start + block] = last[:, run * block : (run + 1) * block]
             here = (run, slice(0, block), slice(part * block, (part + 1) * block))
             rows_ref[here] = inner
             here = (run, slice(block, tops), slice(part * block, (part + 1) * block))
@@ -297,51 +289,101 @@
     mask_ref,
     *refs,
 ):
-    blocks, refs = refs[:-8], refs[-8:]
-    incident_ref, scattered_ref, traces_ref, field_ref, speed_ref, drive_ref, wave_ref, slim_ref = refs
+    blocks, refs = refs[:-11], refs[-11:]
+    incident_ref, scattered_ref, traces_ref = refs[:3]
+    field_ref, speed_ref, drive_ref, wave_ref, parts_ref, product_ref, taken_ref, slim_ref = refs[3:]
     deep, tall, wide = speed_ref.shape
-    rows = deep * tall
-    shape, cube = (rows, wide), (deep, tall, wide)
     deep_count, tall_count, part_width = own_shape
     own = deep_count * tall_count
     replicas = contrast_ref.shape[0]
     receivers = mask_ref.shape[0]
     runs, block = rows_ref.shape[0], rows_ref.shape[2] // 3
     run = block // tall
-    slab, sub, rep = place_ref[0], place_ref[1], place_ref[2]
+    group = min(run, CHUNK)
+    slab, sub, rep = (place_ref[i] for i in range(3))
 
     for number, layer, what, x, y, z in layout:
+        half = rep ^ x
         at = (
             pl.ds(pl.multiple_of((slab ^ z) * deep_count, deep_count), deep_count),
             pl.ds(pl.multiple_of((sub ^ y) * tall_count, tall_count), tall_count),
+            pl.ds(pl.multiple_of(half * part_width, part_width), part_width),
         )
-        at += (pl.ds(pl.multiple_of((rep ^ x) * part_width, part_width), part_width),)
         piece = blocks[number][layer : layer + deep_count]
         if what == "courant":
             speed_ref[at] = piece * piece * (1.0 / coeff_scale)
         else:
-            field_ref[(("now", "prev").index(what),) + at] = piece
-
-    def applied(value):
-        parts = split3(value)
-        total = (3.0 * whole_coeffs[0]) * value
-        total += product(jnp.concatenate(parts, axis=1), wide_ref[...])
-        down, taken = [], None
-        for number in range(runs):
-            here = slice(number * block, (number + 1) * block)
-            result = product(rows_ref[number], jnp.concatenate([part[here] for part in parts], axis=0))
-            down.append(result[:block])
-            taken = result[block:] if taken is None else taken + result[block:]
-        total += jnp.concatenate(down, axis=0)
-        sums = seam(value, tall, run)
+            field_ref[(("prev", "now").index(what),) + at] = piece
+
+    def groups(number):
+        for first in range(number * run, (number + 1) * run, group):
+            yield first, slice((first - number * run) * tall, (first - number * run + group) * tall)
+
+    def flat(ref, *index):
+        value = ref[index]
+        return value.reshape(-1, wide)
+
+    def near(ref, first, *index):
+        return flat(ref, *index, slice(first, first + group))
+
+    def put(ref, value, first, *index):
+        ref[index + (slice(first, first + group),)] = value.reshape(group, tall, wide)
+
+    def cut(slot, number, rows, value, count):
+        for part, piece in enumerate(split(value, count)):
+            parts_ref[slot, number, part * block + rows.start : part * block + rows.stop] = piece
+
+    def multiply(slot, number, count, sampled):
+        held = parts_ref[slot, number, : count * block]
+        tops = rows_ref.shape[1] if sampled else block
+        beside = jnp.concatenate([held[part * block : (part + 1) * block] for part in range(count)], axis=1)
+        down = product(rows_ref[number, :tops, : count * block], held)
+        product_ref[slot, number] = down[:block] + product(beside, wide_ref[: count * wide])
+        if sampled:
+            taken_ref[slot, number] = down[block:]
+
+    def applied(slot, number, rows, first, ref, *index):
+        total = (3.0 * whole_coeffs[0]) * near(ref, first, *index) + product_ref[slot, number, rows]
         pieces = []
-        for z in range(deep):
-            piece = total[z * tall : (z + 1) * tall]
-            pieces.append(piece + sums[z] if z in sums else piece)
-        return jnp.concatenate(pieces, axis=0), taken
-
-    def flat(ref, *index):
-        return ref[index].reshape(shape)
+        for z in range(first, first + group):
+            piece = total[(z - first) * tall : (z - first + 1) * tall]
+            for k in range(1, 5):
+                for other in (z - k, z + k):
+                    if 0 <= other < deep and other // run != z // run:
+                        piece = piece + float(whole_coeffs[k]) * ref[index + (other,)]
+            pieces.append(piece)
+        return jnp.concatenate(pieces, axis=0) if len(pieces) > 1 else pieces[0]
+
+    def start_incident(number):
+        for first, rows in groups(number):
+            cut(0, number, rows, near(field_ref, first, 1), 3)
+
+    def step_incident(n, number):
+        before, now, after = n % 4, (n + 1) % 4, (n + 2) % 4
+        for first, rows in groups(number):
+            drive = near(speed_ref, first) * applied(0, number, rows, first, field_ref, now)
+            drive += near(force_ref, first, n)
+            put(drive_ref, drive, first)
+            following = 2.0 * near(field_ref, first, now) - near(field_ref, first, before) + drive
+            put(field_ref, following, first, after)
+            cut(0, number, rows, following, 3)
+            if n == 0:
+                for r in range(replicas):
+                    wave = near(contrast_ref, first, r) * drive
+                    put(wave_ref, wave, first, r, 0)
+                    cut(1 + r, number, rows, wave, WAVE_PARTS)
+
+    def step_wave(n, r, number):
+        for first, rows in groups(number):
+            following = (
+                2.0 * near(wave_ref, first, r, n - 1)
+                + near(speed_ref, first) * applied(1 + r, number, rows, first, wave_ref, r, n - 1)
+                + near(contrast_ref, first, r) * near(drive_ref, first)
+            )
+            if n > 1:
+                following -= near(wave_ref, first, r, n - 2)
+            put(wave_ref, following, first, r, n)
+            cut(1 + r, number, rows, following, WAVE_PARTS)
 
     at_z = pl.multiple_of(slab * deep_count, deep_count)
     at_y = pl.multiple_of(sub * tall_count, tall_count)
@@ -351,52 +393,59 @@
         here = index + (pl.ds(at_z, deep_count), pl.ds(at_y, tall_count), slice(None))
         return ref[here].reshape(own, wide)
 
+    def chosen(slot, rows, count):
+        total = None
+        for number in range(runs):
+            start = number * 3 * block
+            held = parts_ref[slot, number, : count * block]
+            term = product(last_ref[rows, start : start + count * block], held)
+            total = term if total is None else total + term
+        return total
+
     samples = [[None] * replicas for _ in range(STEPS)]
-    speed = flat(speed_ref)
-
-    now = flat(field_ref, 0)
-    drive_ref[...] = speed * applied(now)[0] + flat(force_ref, 0)
-    field_ref[1] = (2.0 * now - flat(field_ref, 1) + drive_ref[...]).reshape(cube)
-    for r in range(replicas):
-        wave = flat(contrast_ref, r) * drive_ref[...]
-        wave_ref[0, r] = wave.reshape(cube)
-        result, samples[0][r] = applied(wave)
-        wave_ref[1, r] = (2.0 * wave + speed * result).reshape(cube)
-
-    now = flat(field_ref, 1)
-    drive_ref[...] = speed * applied(now)[0] + flat(force_ref, 1)
-    field_ref[0] = (2.0 * now - flat(field_ref, 0) + drive_ref[...]).reshape(cube)
-    for r in range(replicas):
-        wave_ref[1, r] += (flat(contrast_ref, r) * drive_ref[...]).reshape(cube)
-
-    now = flat(field_ref, 0)
-    drive_ref[...] = speed * applied(now)[0] + flat(force_ref, 2)
-    field_ref[1] = (2.0 * now - flat(field_ref, 1) + drive_ref[...]).reshape(cube)
-    for r in range(replicas):
-        wave = flat(wave_ref, 1, r)
-        result, samples[1][r] = applied(wave)
-        source = flat(contrast_ref, r) * drive_ref[...]
-        wave_ref[0, r] = (
-            2.0 * wave - flat(wave_ref, 0, r) + speed * result + source
-        ).reshape(cube)
-
-    taken = product(last_ref[own + receivers :], jnp.concatenate(split3(speed), axis=0))
-    speed = jnp.concatenate([owned(speed_ref), taken], axis=0)
-
-    def last_applied(value, mine):
-        result = product(last_ref[...], jnp.concatenate(split3(value), axis=0))
+    each = range(runs)
+
+    for number in each:
+        start_incident(number)
+    for number in each:
+        multiply(0, number, 3, False)
+    for number in each:
+        for first, rows in groups(number):
+            cut(1 + replicas, number, rows, near(speed_ref, first), 3)
+    for number in each:
+        step_incident(0, number)
+    for n in (1, 2):
+        work = [(multiply, (0, number, 3, False)) for number in each]
+        after = [(step_incident, (n, number)) for number in each]
+        for r in range(replicas):
+            work += [(multiply, (1 + r, number, WAVE_PARTS, True)) for number in each]
+            after += [(step_wave, (n, r, number)) for number in each]
+        for i in range(len(work) + runs):
+            if i < len(work):
+                work[i][0](*work[i][1])
+            if i >= runs:
+                after[i - runs][0](*after[i - runs][1])
+        for r in range(replicas):
+            samples[n - 1][r] = sum(taken_ref[1 + r, number] for number in each)
+
+    receiver_rows = slice(own + receivers, own + 2 * receivers)
+    speed = jnp.concatenate([owned(speed_ref), chosen(1 + replicas, receiver_rows, 3)], axis=0)
+
+    def last_applied(slot, mine, count):
+        result = chosen(slot, slice(None), count)
         here = jnp.concatenate([mine, result[own + receivers :]], axis=0)
         total = (3.0 * whole_coeffs[0]) * here + result[: own + receivers]
-        return total + product(jnp.concatenate(split3(here), axis=1), wide_ref[...]), here
-
-    result, now = last_applied(flat(field_ref, 1), owned(field_ref, 1))
+        beside = jnp.concatenate(split(here, count), axis=1)
+        return total + product(beside, wide_ref[: count * wide]), here
+
+    result, now = last_applied(0, owned(field_ref, 0), 3)
     drive = speed * result + last_force_ref[...]
-    slim_ref[...] = 2.0 * now[:own] - owned(field_ref, 0) + drive[:own]
+    slim_ref[...] = 2.0 * now[:own] - owned(field_ref, 3) + drive[:own]
     incident_ref[...] = slim_ref[:, pl.ds(at_x, part_width)].reshape(incident_ref.shape)
     for r in range(replicas):
-        result, wave = last_applied(flat(wave_ref, 0, r), owned(wave_ref, 0, r))
+        result, wave = last_applied(1 + r, owned(wave_ref, r, 2), WAVE_PARTS)
         samples[2][r] = wave[own:]
-        before = jnp.concatenate([owned(wave_ref, 1, r), samples[1][r]], axis=0)
+        before = jnp.concatenate([owned(wave_ref, r, 1), samples[1][r]], axis=0)
         following = 2.0 * wave - before + speed * result + last_contrast_ref[r] * drive
         scattered_ref[r] = following[:own].reshape(scattered_ref.shape[1:])
         samples[3][r] = following[own:]
@@ -419,7 +468,7 @@
     sent = own[: 3 * deep_count]
     beyond = {m: swapped(sent, "slab", m) for m in (1, 2, 3)}
     near = jnp.concatenate([own[: 2 * deep_count], beyond[1]], axis=0)
-    far = jnp.concatenate([beyond[2], beyond[3]], axis=0)
+    far = jnp.concatenate([beyond[3], beyond[2]], axis=0)
     far, prepared = lax.optimization_barrier((far, prepared))
     near_two, far_two = swapped(near, "rep", 1), swapped(far, "rep", 1)
     near_line = jnp.concatenate([near, near_two, own[2 * deep_count :]], axis=0)
@@ -429,7 +478,7 @@
     near_layout = [(name, 0) for name in names[:2]] + [(name, 1) for name in names]
     near_layout = [(name, x, z) for x in range(2) for name, z in near_layout]
     near_layout += [("courant", x, 0) for x in range(2)]
-    far_layout = [(name, m) for m in (2, 3) for name in names]
+    far_layout = [(name, m) for m in (3, 2) for name in names]
     layout = []
     for y in range(2):
         for i, (name, x, z) in enumerate(near_layout):
@@ -531,10 +580,13 @@
         (),
         (*prepared, *blocks),
         (
-            pltpu.VMEM((2,) + cube, jnp.float32),
+            pltpu.VMEM((4,) + cube, jnp.float32),
             pltpu.VMEM(cube, jnp.float32),
-            pltpu.VMEM((rows, wide), jnp.float32),
-            pltpu.VMEM((2, replicas) + cube, jnp.float32),
+            pltpu.VMEM(cube, jnp.float32),
+            pltpu.VMEM((replicas, 3) + cube, jnp.float32),
+            pltpu.VMEM((2 + replicas, rows // block, 3 * block, wide), jnp.bfloat16),
+            pltpu.VMEM((1 + replicas, rows // block, block, wide), jnp.float32),
+            pltpu.VMEM((1 + replicas, rows // block, receivers, wide), jnp.float32),
             pltpu.VMEM((deep_count * tall_count, wide), jnp.float32),
         ),
     )

time: 31.5 us -> 28.6 us (0.908)
  waiting for transfers between devices: 9.7 us -> 7.98 us
  Pallas kernels: 11.1 us -> 9.95 us
    ppermute x8, waiting for transfers between devices: 9.7 us -> 7.98 us  [swapped(): return lax.ppermute(array, axis, [(i, i ^ distance) for i in range(size)])]
    pallas_call x3, Pallas kernels: 11.1 us -> 9.95 us  [call(): pl.pallas_call(kernel, out_shape=out_shape, in_specs=[smem] * len(scalars...]
  transfers between devices with their start and end apart: 8 -> 8, of which waited for: 5 -> 4; matrix products, arithmetic and copies ran while one was open for 0% -> 0% of each run, Pallas kernels for 9% -> 10%
where the time goes in v3:
time: 28.6 us; the launch traced here: 28.4 us
  Pallas kernels  9.95 us (35%)
  starting transfers between devices  9.61 us (34%)
  waiting for transfers between devices  7.98 us (28%)
  between operations  0.69 us (2%)
    pallas_call x3, Pallas kernels, call(): pl.pallas_call(kernel, out_shape=out_shape, in_specs=[smem] * len(scalars...  9.95 us
    ppermute x8, starting transfers between devices, swapped(): return lax.ppermute(array, axis, [(i, i ^ distance) for i in range(size)])  9.61 us
    ppermute x8, waiting for transfers between devices, swapped(): return lax.ppermute(array, axis, [(i, i ^ distance) for i in range(size)])  7.98 us
  transfers between devices with their start and end apart: 8, of which 4 were waited for; matrix products, arithmetic and copies ran while one was open for 0% of the time, Pallas kernels for 10%

profile of v3, /device:TPU:0, one launch (start us, length us, event | category | flops | bytes accessed | tf_op | source)
XLA Modules:
  0.0 28.4 jit_solution(7696939579247858231)
XLA Ops:
  0.6 0.8 %shard_map.130 = f32[16,16,128]{2,1,0:T(8,128)S(1)} custom-call(f32[4,16,128]{2,1,0:T(8,128)} %now_ref.1, f32[4,16,128]{2,1,0:T(8,128)} %prev_ref.1, f32[4,16,256]{2,1,0:T(8,128)} %courant_ref.1), custom_call_target="tpu_custom_call" | custom-call | tf_op jit(solution)/shard_map/pallas_call | solution.py:523
  1.5 3.1 %collective-permute-start.2 = (f32[12,16,128]{2,1,0:T(8,128)S(1)}, f32[12,16,128]{2,1,0:T(8,128)S(1)}, u32[]{:S(2)}, u32[]{:S(2)}) collective-permute-start(f32[12,16,128]{2,1,0:T(8,128)S(1)} %slice.12), channel_id=1, source_target_pairs={{0,4},{4,0},{8,12},{12,8},{1,5},{5,1},{9,13},{13,9},{2,6},{6,2},{1... | collective-permute-start | bytes 294920 | tf_op jit(solution)/shard_map/ppermute | solution.py:464
  4.6 2.6 %collective-permute-start.1 = (f32[12,16,128]{2,1,0:T(8,128)S(1)}, f32[12,16,128]{2,1,0:T(8,128)S(1)}, u32[]{:S(2)}, u32[]{:S(2)}) collective-permute-start(f32[12,16,128]{2,1,0:T(8,128)S(1)} %slice.12), channel_id=1, source_target_pairs={{0,8},{4,12},{8,0},{12,4},{1,9},{5,13},{9,1},{13,5},{2,10},{6,14},... | collective-permute-start | bytes 294920 | tf_op jit(solution)/shard_map/ppermute | solution.py:464
  7.2 0.0 collective-permute-start
  7.2 0.2 collective-permute-done.2
  7.4 1.8 %collective-permute-start.3 = (f32[20,16,128]{2,1,0:T(8,128)S(1)}, f32[20,16,128]{2,1,0:T(8,128)S(1)}, u32[]{:S(2)}, u32[]{:S(2)}) collective-permute-start(f32[20,16,128]{2,1,0:T(8,128)S(1)} %pad_maximum_fusion.2), channel_id=1, source_target_pairs={{0,2},{2,0},{1,3},{3,1},{4,6},{6,4},{5,7},{7,5},{8,10},{10,8},{9,1... | collective-permute-start | bytes 491528 | tf_op jit(solution)/shard_map/ppermute | solution.py:464
  9.2 0.1 pad_add_fusion.refs_0_.place_ref
  9.3 2.9 %shard_map.131 = (f32[2,16,32,256]{3,2,1,0:T(8,128)S(1)}, f32[3,16,32,256]{3,2,1,0:T(8,128)S(1)}, f32[2,96,256]{2,1,0:T(8,128)S(1)}, f32[96,256]{1,0:T(8,128)S(1...) custom-call(s32[3]{0:T(128)S(1)} %pad_add_fusion.refs_0_.place_ref, ...), custom_call_target="tpu_custom_call" | custom-call | tf_op jit(solution)/shard_map/pallas_call | solution.py:523
  12.2 2.8 %collective-permute-done.1 = f32[12,16,128]{2,1,0:T(8,128)S(1)} collective-permute-done((f32[12,16,128]{2,1,0:T(8,128)S(1)}, f32[12,16,128]{2,1,0:T(8,128)S(1)}, u32[]{:S(2)}, u32[]{:S(2)}) %collective-permute-start.1) | collective-permute-done | bytes 98336 | tf_op jit(solution)/shard_map/ppermute | solution.py:464
  15.0 0.0 collective-permute-done
  15.0 1.6 %collective-permute-start.4 = (f32[24,16,128]{2,1,0:T(8,128)S(1)}, f32[24,16,128]{2,1,0:T(8,128)S(1)}, u32[]{:S(2)}, u32[]{:S(2)}) collective-permute-start(f32[24,16,128]{2,1,0:T(8,128)S(1)} %pad_maximum_fusion.1.refs_1_), channel_id=1, source_target_pairs={{0,2},{2,0},{1,3},{3,1},{4,6},{6,4},{5,7},{7,5},{8,10},{10,8},{9,1... | collective-permute-start | bytes 589832 | tf_op jit(solution)/shard_map/ppermute | solution.py:464
  16.6 0.0 collective-permute-done.3
  16.6 0.1 collective-permute-start.5
  16.7 0.5 %collective-permute-start.6 = (f32[24,16,128]{2,1,0:T(8,128)S(1)}, f32[24,16,128]{2,1,0:T(8,128)S(1)}, u32[]{:S(2)}, u32[]{:S(2)}) collective-permute-start(f32[24,16,128]{2,1,0:T(8,128)S(1)} %pad_maximum_fusion.1.refs_1_), channel_id=1, source_target_pairs={{0,1},{1,0},{2,3},{3,2},{4,5},{5,4},{6,7},{7,6},{8,9},{9,8},{10,11... | collective-permute-start | bytes 589832 | tf_op jit(solution)/shard_map/ppermute | solution.py:464
  17.2 3.6 %collective-permute-done.4.refs_2_ = f32[24,16,128]{2,1,0:T(8,128)S(1)} collective-permute-done((f32[24,16,128]{2,1,0:T(8,128)S(1)}, f32[24,16,128]{2,1,0:T(8,128)S(1)}, u32[]{:S(2)}, u32[]{:S(2)}) %collective-permute-start.4) | collective-permute-done | bytes 196640 | tf_op jit(solution)/shard_map/ppermute | solution.py:464
  20.8 0.0 collective-permute-start.7
  20.8 0.0 collective-permute-done.6.refs_4_
  20.8 1.4 %collective-permute-done.7.refs_5_ = f32[24,16,128]{2,1,0:T(8,128)S(1)} collective-permute-done((f32[24,16,128]{2,1,0:T(8,128)S(1)}, f32[24,16,128]{2,1,0:T(8,128)S(1)}, u32[]{:S(2)}, u32[]{:S(2)}) %collective-permute-start.7) | collective-permute-done | bytes 196640 | tf_op jit(solution)/shard_map/ppermute | solution.py:464
  22.2 0.0 collective-permute-done.5.refs_3_
  22.2 6.2 %shard_map.132 = (f32[4,16,128]{2,1,0:T(8,128)}, f32[2,4,16,256]{3,2,1,0:T(8,128)}, f32[8,32]{1,0:T(8,128)}) custom-call(s32[3]{0:T(128)S(1)} %pad_add_fusion.refs_0_.place_ref, f32[2,16,32,256]{3,2,1,0:T(8,128)S(1)} %get-tuple-element.31.contrast_ref, f32[3,16,32,256]{3,2,1,0:T(8,128)S(1)} %get-tuple-element.32.force_ref, ...), custom_call_target="tpu_custom_call" | custom-call | tf_op jit(solution)/shard_map/pallas_call | solution.py:523
  (5 shorter events, 0.1 us)
Async XLA Ops:
  1.5 5.9 %collective-permute-start.2 = (f32[12,16,128]{2,1,0:T(8,128)S(1)}, f32[12,16,128]{2,1,0:T(8,128)S(1)}, u32[]{:S(2)}, u32[]{:S(2)}) collective-permute-start(f32[12,16,128]{2,1,0:T(8,128)S(1)} %slice.12), channel_id=1, source_target_pairs={{0,4},{4,0},{8,12},{12,8},{1,5},{5,1},{9,13},{13,9},{2,6},{6,2},{1... | collective-permute-start | bytes 294920 | tf_op jit(solution)/shard_map/ppermute | solution.py:464
  4.6 10.4 %collective-permute-start.1 = (f32[12,16,128]{2,1,0:T(8,128)S(1)}, f32[12,16,128]{2,1,0:T(8,128)S(1)}, u32[]{:S(2)}, u32[]{:S(2)}) collective-permute-start(f32[12,16,128]{2,1,0:T(8,128)S(1)} %slice.12), channel_id=1, source_target_pairs={{0,8},{4,12},{8,0},{12,4},{1,9},{5,13},{9,1},{13,5},{2,10},{6,14},... | collective-permute-start | bytes 294920 | tf_op jit(solution)/shard_map/ppermute | solution.py:464
  7.2 7.8 %collective-permute-start = (f32[12,16,128]{2,1,0:T(8,128)S(1)}, f32[12,16,128]{2,1,0:T(8,128)S(1)}, u32[]{:S(2)}, u32[]{:S(2)}) collective-permute-start(f32[12,16,128]{2,1,0:T(8,128)S(1)} %slice.12), channel_id=1, source_target_pairs={{0,12},{4,8},{8,4},{12,0},{1,13},{5,9},{9,5},{13,1},{2,14},{6,10},... | collective-permute-start | bytes 294920 | tf_op jit(solution)/shard_map/ppermute | solution.py:464
  7.4 9.2 %collective-permute-start.3 = (f32[20,16,128]{2,1,0:T(8,128)S(1)}, f32[20,16,128]{2,1,0:T(8,128)S(1)}, u32[]{:S(2)}, u32[]{:S(2)}) collective-permute-start(f32[20,16,128]{2,1,0:T(8,128)S(1)} %pad_maximum_fusion.2), channel_id=1, source_target_pairs={{0,2},{2,0},{1,3},{3,1},{4,6},{6,4},{5,7},{7,5},{8,10},{10,8},{9,1... | collective-permute-start | bytes 491528 | tf_op jit(solution)/shard_map/ppermute | solution.py:464
  15.0 5.7 %collective-permute-start.4 = (f32[24,16,128]{2,1,0:T(8,128)S(1)}, f32[24,16,128]{2,1,0:T(8,128)S(1)}, u32[]{:S(2)}, u32[]{:S(2)}) collective-permute-start(f32[24,16,128]{2,1,0:T(8,128)S(1)} %pad_maximum_fusion.1.refs_1_), channel_id=1, source_target_pairs={{0,2},{2,0},{1,3},{3,1},{4,6},{6,4},{5,7},{7,5},{8,10},{10,8},{9,1... | collective-permute-start | bytes 589832 | tf_op jit(solution)/shard_map/ppermute | solution.py:464
  16.6 5.6 %collective-permute-start.5 = (f32[48,16,128]{2,1,0:T(8,128)S(1)}, f32[48,16,128]{2,1,0:T(8,128)S(1)}, u32[]{:S(2)}, u32[]{:S(2)}) collective-permute-start(f32[48,16,128]{2,1,0:T(8,128)S(1)} %pad_maximum_fusion.refs_0_), channel_id=1, source_target_pairs={{0,1},{1,0},{2,3},{3,2},{4,5},{5,4},{6,7},{7,6},{8,9},{9,8},{10,11... | collective-permute-start | bytes 1179656 | tf_op jit(solution)/shard_map/ppermute | solution.py:464
  16.7 4.1 %collective-permute-start.6 = (f32[24,16,128]{2,1,0:T(8,128)S(1)}, f32[24,16,128]{2,1,0:T(8,128)S(1)}, u32[]{:S(2)}, u32[]{:S(2)}) collective-permute-start(f32[24,16,128]{2,1,0:T(8,128)S(1)} %pad_maximum_fusion.1.refs_1_), channel_id=1, source_target_pairs={{0,1},{1,0},{2,3},{3,2},{4,5},{5,4},{6,7},{7,6},{8,9},{9,8},{10,11... | collective-permute-start | bytes 589832 | tf_op jit(solution)/shard_map/ppermute | solution.py:464
  20.8 1.4 %collective-permute-start.7 = (f32[24,16,128]{2,1,0:T(8,128)S(1)}, f32[24,16,128]{2,1,0:T(8,128)S(1)}, u32[]{:S(2)}, u32[]{:S(2)}) collective-permute-start(f32[24,16,128]{2,1,0:T(8,128)S(1)} %collective-permute-done.4.refs_2_), channel_id=1, source_target_pairs={{0,1},{1,0},{2,3},{3,2},{4,5},{5,4},{6,7},{7,6},{8,9},{9,8},{10,11... | collective-permute-start | bytes 589832 | tf_op jit(solution)/shard_map/ppermute | solution.py:464

commit v4 on v3

--- a/solution.py
+++ b/solution.py
@@ -212,11 +212,19 @@
         copy.wait()
 
 
+def beside_kernel(wide_ref):
+    wide = wide_ref.shape[1]
+    line = lax.broadcasted_iota(jnp.int32, (wide, wide), 0)
+    beside = band(jnp.abs(line - lax.broadcasted_iota(jnp.int32, (wide, wide), 1)))
+    for part in range(3):
+        wide_ref[part * wide : (part + 1) * wide, :] = beside.astype(jnp.bfloat16)
+
+
 def prepare_kernel(own_shape, *refs):
     place_ref, refs = refs[0], refs[1:]
-    given, outputs, held, semaphores = refs[:8], refs[8:16], refs[16:24], refs[24]
+    given, outputs, held, semaphores = refs[:8], refs[8:15], refs[15:23], refs[23]
     contrast_ref, force_ref, last_contrast_ref, last_force_ref = outputs[:4]
-    rows_ref, wide_ref, last_ref, mask_ref = outputs[4:]
+    rows_ref, last_ref, mask_ref = outputs[4:]
     wavelet_ref, source_z_ref, source_y_ref, source_x_ref = held[:4]
     seeds_ref, receiver_z_ref, receiver_y_ref, receiver_x_ref = held[4:]
     copies = fetched(given, held, semaphores)
@@ -228,10 +236,6 @@
     own = deep_count * tall_count
     replicas = seeds_ref.shape[0]
     sources = range(source_z_ref.shape[0])
-    line = lax.broadcasted_iota(jnp.int32, (wide, wide), 0)
-    beside = band(jnp.abs(line - lax.broadcasted_iota(jnp.int32, (wide, wide), 1)))
-    for part in range(3):
-        wide_ref[part * wide : (part + 1) * wide, :] = beside.astype(jnp.bfloat16)
     for copy in copies:
         copy.wait()
     z_of = lax.broadcasted_iota(jnp.int32, (deep, tall, wide), 0)
@@ -284,9 +288,9 @@
     last_contrast_ref,
     last_force_ref,
     rows_ref,
-    wide_ref,
     last_ref,
     mask_ref,
+    wide_ref,
     *refs,
 ):
     blocks, refs = refs[:-11], refs[-11:]
@@ -464,29 +468,33 @@
     return lax.ppermute(array, axis, [(i, i ^ distance) for i in range(size)])
 
 
-def exchanged(own, deep_count, prepared):
+def exchanged(own, deep_count, matrices, prepared):
     sent = own[: 3 * deep_count]
-    beyond = {m: swapped(sent, "slab", m) for m in (1, 2, 3)}
+    beyond = {m: swapped(sent, "slab", m) for m in (1, 2)}
+    late, matrices = lax.optimization_barrier((sent, matrices))
+    beyond[3] = swapped(late, "slab", 3)
     near = jnp.concatenate([own[: 2 * deep_count], beyond[1]], axis=0)
-    far = jnp.concatenate([beyond[3], beyond[2]], axis=0)
-    far, prepared = lax.optimization_barrier((far, prepared))
-    near_two, far_two = swapped(near, "rep", 1), swapped(far, "rep", 1)
-    near_line = jnp.concatenate([near, near_two, own[2 * deep_count :]], axis=0)
-    blocks = [near_line, far, far_two]
+    near_two, two_two = swapped(near, "rep", 1), swapped(beyond[2], "rep", 1)
+    near_two, prepared = lax.optimization_barrier((near_two, prepared))
+    three_two = swapped(beyond[3], "rep", 1)
+    blocks = [
+        jnp.concatenate([near, near_two, own[2 * deep_count :]], axis=0),
+        jnp.concatenate([beyond[2], two_two], axis=0),
+        jnp.concatenate([beyond[3], three_two], axis=0),
+    ]
     blocks += [swapped(block, "sub", 1) for block in blocks]
     names = ("now", "prev", "courant")
     near_layout = [(name, 0) for name in names[:2]] + [(name, 1) for name in names]
-    near_layout = [(name, x, z) for x in range(2) for name, z in near_layout]
-    near_layout += [("courant", x, 0) for x in range(2)]
-    far_layout = [(name, m) for m in (3, 2) for name in names]
-    layout = []
-    for y in range(2):
-        for i, (name, x, z) in enumerate(near_layout):
-            layout.append((3 * y, i * deep_count, name, x, y, z))
-        for x in range(2):
-            for i, (name, z) in enumerate(far_layout):
-                layout.append((3 * y + 1 + x, i * deep_count, name, x, y, z))
-    return blocks, tuple(layout), prepared
+    layouts = [[(name, x, z) for x in range(2) for name, z in near_layout]]
+    layouts[0] += [("courant", x, 0) for x in range(2)]
+    layouts += [[(name, x, z) for x in range(2) for name in names] for z in (2, 3)]
+    layout = [
+        (len(layouts) * y + number, i * deep_count, name, x, y, z)
+        for y in range(2)
+        for number, parts in enumerate(layouts)
+        for i, (name, x, z) in enumerate(parts)
+    ]
+    return blocks, tuple(layout), (*prepared, *matrices)
 
 
 def whole_shards(
@@ -548,7 +556,6 @@
             held(replicas, last_rows, wide),
             held(last_rows, wide),
             held(rows // block, block + receivers, 3 * block, dtype=jnp.bfloat16),
-            held(3 * wide, wide, dtype=jnp.bfloat16),
             held(last_rows + receivers, 3 * rows, dtype=jnp.bfloat16),
             held(receivers, wide),
         ),
@@ -560,6 +567,7 @@
             pltpu.SemaphoreType.DMA((len(given),)),
         ),
     )
+    matrices = call(beside_kernel, (held(3 * wide, wide, dtype=jnp.bfloat16),), (), (), (), ())
     own = call(
         pack_kernel,
         (held(4 * deep_count, tall_count, part_width),),
@@ -568,7 +576,7 @@
         (),
         (pltpu.SemaphoreType.DMA((4,)),),
     )[0]
-    blocks, layout, prepared = exchanged(own, deep_count, prepared)
+    blocks, layout, prepared = exchanged(own, deep_count, matrices, prepared)
     incident_final, scattered_final, traces = call(
         functools.partial(step_kernel, layout, own_shape),
         (

time: 28.6 us -> 27.8 us (0.972)
  waiting for transfers between devices: 7.98 us -> 7.21 us
    ppermute x8 -> x9, waiting for transfers between devices: 7.98 us -> 7.21 us  [swapped(): return lax.ppermute(array, axis, [(i, i ^ distance) for i in range(size)])]
    pallas_call x3 -> x4, Pallas kernels: 9.95 us -> 9.89 us  [call(): pl.pallas_call(kernel, out_shape=out_shape, in_specs=[smem] * len(scalars...]
    ppermute x8 -> x9, starting transfers between devices: 9.61 us -> 9.64 us  [swapped(): return lax.ppermute(array, axis, [(i, i ^ distance) for i in range(size)])]
  transfers between devices with their start and end apart: 8 -> 9, of which waited for: 4 -> 7; matrix products, arithmetic and copies ran while one was open for 0% -> 1% of each run, Pallas kernels for 10% -> 11%
where the time goes in v4:
time: 27.8 us; the launch traced here: 27.6 us
  Pallas kernels  9.89 us (36%)
  starting transfers between devices  9.64 us (35%)
  waiting for transfers between devices  7.21 us (26%)
  between operations  0.73 us (3%)
    pallas_call x4, Pallas kernels, call(): pl.pallas_call(kernel, out_shape=out_shape, in_specs=[smem] * len(scalars...  9.89 us
    ppermute x9, starting transfers between devices, swapped(): return lax.ppermute(array, axis, [(i, i ^ distance) for i in range(size)])  9.64 us
    ppermute x9, waiting for transfers between devices, swapped(): return lax.ppermute(array, axis, [(i, i ^ distance) for i in range(size)])  7.21 us
  transfers between devices with their start and end apart: 9, of which 7 were waited for; matrix products, arithmetic and copies ran while one was open for 1% of the time, Pallas kernels for 11%

profile of v4, /device:TPU:0, one launch (start us, length us, event | category | flops | bytes accessed | tf_op | source)
XLA Modules:
  0.0 27.6 jit_solution(5807062187740535204)
XLA Ops:
  0.6 0.8 %shard_map.130 = f32[16,16,128]{2,1,0:T(8,128)S(1)} custom-call(f32[4,16,128]{2,1,0:T(8,128)} %now_ref.1, f32[4,16,128]{2,1,0:T(8,128)} %prev_ref.1, f32[4,16,256]{2,1,0:T(8,128)} %courant_ref.1), custom_call_target="tpu_custom_call" | custom-call | tf_op jit(solution)/shard_map/pallas_call | solution.py:531
  1.5 4.1 %collective-permute-start.2 = (f32[12,16,128]{2,1,0:T(8,128)S(1)}, f32[12,16,128]{2,1,0:T(8,128)S(1)}, u32[]{:S(2)}, u32[]{:S(2)}) collective-permute-start(f32[12,16,128]{2,1,0:T(8,128)S(1)} %slice.13), channel_id=1, source_target_pairs={{0,8},{4,12},{8,0},{12,4},{1,9},{5,13},{9,1},{13,5},{2,10},{6,14},... | collective-permute-start | bytes 294920 | tf_op jit(solution)/shard_map/ppermute | solution.py:468
  5.6 1.6 %collective-permute-start = (f32[12,16,128]{2,1,0:T(8,128)S(1)}, f32[12,16,128]{2,1,0:T(8,128)S(1)}, u32[]{:S(2)}, u32[]{:S(2)}) collective-permute-start(f32[12,16,128]{2,1,0:T(8,128)S(1)} %slice.13), channel_id=1, source_target_pairs={{0,4},{4,0},{8,12},{12,8},{1,5},{5,1},{9,13},{13,9},{2,6},{6,2},{1... | collective-permute-start | bytes 294920 | tf_op jit(solution)/shard_map/ppermute | solution.py:468
  7.2 0.1 shard_map.132.wide_ref
  7.2 0.1 collective-permute-start.4
  7.4 0.1 pad_add_fusion.refs_0_.place_ref
  7.4 2.9 %shard_map.131 = (f32[2,16,32,256]{3,2,1,0:T(8,128)S(1)}, f32[3,16,32,256]{3,2,1,0:T(8,128)S(1)}, f32[2,96,256]{2,1,0:T(8,128)S(1)}, f32[96,256]{1,0:T(8,128)S(1...) custom-call(s32[3]{0:T(128)S(1)} %pad_add_fusion.refs_0_.place_ref, ...), custom_call_target="tpu_custom_call" | custom-call | tf_op jit(solution)/shard_map/pallas_call | solution.py:531
  10.4 0.4 %collective-permute-done = f32[12,16,128]{2,1,0:T(8,128)S(1)} collective-permute-done((f32[12,16,128]{2,1,0:T(8,128)S(1)}, f32[12,16,128]{2,1,0:T(8,128)S(1)}, u32[]{:S(2)}, u32[]{:S(2)}) %collective-permute-start) | collective-permute-done | bytes 98336 | tf_op jit(solution)/shard_map/ppermute | solution.py:468
  10.7 1.6 %collective-permute-start.1 = (f32[20,16,128]{2,1,0:T(8,128)S(1)}, f32[20,16,128]{2,1,0:T(8,128)S(1)}, u32[]{:S(2)}, u32[]{:S(2)}) collective-permute-start(f32[20,16,128]{2,1,0:T(8,128)S(1)} %pad_maximum_fusion.1), channel_id=1, source_target_pairs={{0,2},{2,0},{1,3},{3,1},{4,6},{6,4},{5,7},{7,5},{8,10},{10,8},{9,1... | collective-permute-start | bytes 491528 | tf_op jit(solution)/shard_map/ppermute | solution.py:468
  12.3 0.0 collective-permute-done.2
  12.3 0.7 %collective-permute-start.3 = (f32[12,16,128]{2,1,0:T(8,128)S(1)}, f32[12,16,128]{2,1,0:T(8,128)S(1)}, u32[]{:S(2)}, u32[]{:S(2)}) collective-permute-start(f32[12,16,128]{2,1,0:T(8,128)S(1)} %collective-permute-done.2), channel_id=1, source_target_pairs={{0,2},{2,0},{1,3},{3,1},{4,6},{6,4},{5,7},{7,5},{8,10},{10,8},{9,1... | collective-permute-start | bytes 294920 | tf_op jit(solution)/shard_map/ppermute | solution.py:468
  13.0 0.8 %collective-permute-done.4 = f32[12,16,128]{2,1,0:T(8,128)S(1)} collective-permute-done((f32[12,16,128]{2,1,0:T(8,128)S(1)}, f32[12,16,128]{2,1,0:T(8,128)S(1)}, u32[]{:S(2)}, u32[]{:S(2)}) %collective-permute-start.4) | collective-permute-done | bytes 98336 | tf_op jit(solution)/shard_map/ppermute | solution.py:468
  13.8 1.5 %collective-permute-start.5 = (f32[12,16,128]{2,1,0:T(8,128)S(1)}, f32[12,16,128]{2,1,0:T(8,128)S(1)}, u32[]{:S(2)}, u32[]{:S(2)}) collective-permute-start(f32[12,16,128]{2,1,0:T(8,128)S(1)} %collective-permute-done.4), channel_id=1, source_target_pairs={{0,2},{2,0},{1,3},{3,1},{4,6},{6,4},{5,7},{7,5},{8,10},{10,8},{9,1... | collective-permute-start | bytes 294920 | tf_op jit(solution)/shard_map/ppermute | solution.py:468
  15.3 2.7 %collective-permute-done.1 = f32[20,16,128]{2,1,0:T(8,128)S(1)} collective-permute-done((f32[20,16,128]{2,1,0:T(8,128)S(1)}, f32[20,16,128]{2,1,0:T(8,128)S(1)}, u32[]{:S(2)}, u32[]{:S(2)}) %collective-permute-start.1) | collective-permute-done | bytes 163872 | tf_op jit(solution)/shard_map/ppermute | solution.py:468
  18.0 0.1 collective-permute-start.6
  18.1 1.0 %collective-permute-done.3 = f32[12,16,128]{2,1,0:T(8,128)S(1)} collective-permute-done((f32[12,16,128]{2,1,0:T(8,128)S(1)}, f32[12,16,128]{2,1,0:T(8,128)S(1)}, u32[]{:S(2)}, u32[]{:S(2)}) %collective-permute-start.3) | collective-permute-done | bytes 98336 | tf_op jit(solution)/shard_map/ppermute | solution.py:468
  19.0 0.1 collective-permute-start.7
  19.1 1.0 %collective-permute-done.5 = f32[12,16,128]{2,1,0:T(8,128)S(1)} collective-permute-done((f32[12,16,128]{2,1,0:T(8,128)S(1)}, f32[12,16,128]{2,1,0:T(8,128)S(1)}, u32[]{:S(2)}, u32[]{:S(2)}) %collective-permute-start.5) | collective-permute-done | bytes 98336 | tf_op jit(solution)/shard_map/ppermute | solution.py:468
  20.1 0.1 collective-permute-start.8
  20.2 0.4 %collective-permute-done.7.refs_4_ = f32[24,16,128]{2,1,0:T(8,128)S(1)} collective-permute-done((f32[24,16,128]{2,1,0:T(8,128)S(1)}, f32[24,16,128]{2,1,0:T(8,128)S(1)}, u32[]{:S(2)}, u32[]{:S(2)}) %collective-permute-start.7) | collective-permute-done | bytes 196640 | tf_op jit(solution)/shard_map/ppermute | solution.py:468
  20.5 1.1 %collective-permute-done.8.refs_5_ = f32[24,16,128]{2,1,0:T(8,128)S(1)} collective-permute-done((f32[24,16,128]{2,1,0:T(8,128)S(1)}, f32[24,16,128]{2,1,0:T(8,128)S(1)}, u32[]{:S(2)}, u32[]{:S(2)}) %collective-permute-start.8) | collective-permute-done | bytes 196640 | tf_op jit(solution)/shard_map/ppermute | solution.py:468
  21.6 0.0 collective-permute-done.6.refs_3_
  21.6 6.0 %shard_map.133 = (f32[4,16,128]{2,1,0:T(8,128)}, f32[2,4,16,256]{3,2,1,0:T(8,128)}, f32[8,32]{1,0:T(8,128)}) custom-call(s32[3]{0:T(128)S(1)} %pad_add_fusion.refs_0_.place_ref, f32[2,16,32,256]{3,2,1,0:T(8,128)S(1)} %get-tuple-element.30.contrast_ref, f32[3,16,32,256]{3,2,1,0:T(8,128)S(1)} %get-tuple-element.31.force_ref, ...), custom_call_target="tpu_custom_call" | custom-call | tf_op jit(solution)/shard_map/pallas_call | solution.py:531
  (8 shorter events, 0.1 us)
Async XLA Ops:
  1.5 10.8 %collective-permute-start.2 = (f32[12,16,128]{2,1,0:T(8,128)S(1)}, f32[12,16,128]{2,1,0:T(8,128)S(1)}, u32[]{:S(2)}, u32[]{:S(2)}) collective-permute-start(f32[12,16,128]{2,1,0:T(8,128)S(1)} %slice.13), channel_id=1, source_target_pairs={{0,8},{4,12},{8,0},{12,4},{1,9},{5,13},{9,1},{13,5},{2,10},{6,14},... | collective-permute-start | bytes 294920 | tf_op jit(solution)/shard_map/ppermute | solution.py:468
  5.6 5.1 %collective-permute-start = (f32[12,16,128]{2,1,0:T(8,128)S(1)}, f32[12,16,128]{2,1,0:T(8,128)S(1)}, u32[]{:S(2)}, u32[]{:S(2)}) collective-permute-start(f32[12,16,128]{2,1,0:T(8,128)S(1)} %slice.13), channel_id=1, source_target_pairs={{0,4},{4,0},{8,12},{12,8},{1,5},{5,1},{9,13},{13,9},{2,6},{6,2},{1... | collective-permute-start | bytes 294920 | tf_op jit(solution)/shard_map/ppermute | solution.py:468
  7.2 6.6 %collective-permute-start.4 = (f32[12,16,128]{2,1,0:T(8,128)S(1)}, f32[12,16,128]{2,1,0:T(8,128)S(1)}, u32[]{:S(2)}, u32[]{:S(2)}) collective-permute-start(f32[12,16,128]{2,1,0:T(8,128)S(1)} %slice.13), channel_id=1, source_target_pairs={{0,12},{4,8},{8,4},{12,0},{1,13},{5,9},{9,5},{13,1},{2,14},{6,10},... | collective-permute-start | bytes 294920 | tf_op jit(solution)/shard_map/ppermute | solution.py:468
  10.7 7.2 %collective-permute-start.1 = (f32[20,16,128]{2,1,0:T(8,128)S(1)}, f32[20,16,128]{2,1,0:T(8,128)S(1)}, u32[]{:S(2)}, u32[]{:S(2)}) collective-permute-start(f32[20,16,128]{2,1,0:T(8,128)S(1)} %pad_maximum_fusion.1), channel_id=1, source_target_pairs={{0,2},{2,0},{1,3},{3,1},{4,6},{6,4},{5,7},{7,5},{8,10},{10,8},{9,1... | collective-permute-start | bytes 491528 | tf_op jit(solution)/shard_map/ppermute | solution.py:468
  12.3 6.7 %collective-permute-start.3 = (f32[12,16,128]{2,1,0:T(8,128)S(1)}, f32[12,16,128]{2,1,0:T(8,128)S(1)}, u32[]{:S(2)}, u32[]{:S(2)}) collective-permute-start(f32[12,16,128]{2,1,0:T(8,128)S(1)} %collective-permute-done.2), channel_id=1, source_target_pairs={{0,2},{2,0},{1,3},{3,1},{4,6},{6,4},{5,7},{7,5},{8,10},{10,8},{9,1... | collective-permute-start | bytes 294920 | tf_op jit(solution)/shard_map/ppermute | solution.py:468
  13.8 6.2 %collective-permute-start.5 = (f32[12,16,128]{2,1,0:T(8,128)S(1)}, f32[12,16,128]{2,1,0:T(8,128)S(1)}, u32[]{:S(2)}, u32[]{:S(2)}) collective-permute-start(f32[12,16,128]{2,1,0:T(8,128)S(1)} %collective-permute-done.4), channel_id=1, source_target_pairs={{0,2},{2,0},{1,3},{3,1},{4,6},{6,4},{5,7},{7,5},{8,10},{10,8},{9,1... | collective-permute-start | bytes 294920 | tf_op jit(solution)/shard_map/ppermute | solution.py:468
  18.0 3.6 %collective-permute-start.6 = (f32[48,16,128]{2,1,0:T(8,128)S(1)}, f32[48,16,128]{2,1,0:T(8,128)S(1)}, u32[]{:S(2)}, u32[]{:S(2)}) collective-permute-start(f32[48,16,128]{2,1,0:T(8,128)S(1)} %pad_maximum_fusion.refs_0_), channel_id=1, source_target_pairs={{0,1},{1,0},{2,3},{3,2},{4,5},{5,4},{6,7},{7,6},{8,9},{9,8},{10,11... | collective-permute-start | bytes 1179656 | tf_op jit(solution)/shard_map/ppermute | solution.py:468
  19.0 1.5 %collective-permute-start.7 = (f32[24,16,128]{2,1,0:T(8,128)S(1)}, f32[24,16,128]{2,1,0:T(8,128)S(1)}, u32[]{:S(2)}, u32[]{:S(2)}) collective-permute-start(f32[24,16,128]{2,1,0:T(8,128)S(1)} %constant_dynamic-update-slice_fusion.refs_1_), channel_id=1, source_target_pairs={{0,1},{1,0},{2,3},{3,2},{4,5},{5,4},{6,7},{7,6},{8,9},{9,8},{10,11... | collective-permute-start | bytes 589832 | tf_op jit(solution)/shard_map/ppermute | solution.py:468
  20.1 1.5 %collective-permute-start.8 = (f32[24,16,128]{2,1,0:T(8,128)S(1)}, f32[24,16,128]{2,1,0:T(8,128)S(1)}, u32[]{:S(2)}, u32[]{:S(2)}) collective-permute-start(f32[24,16,128]{2,1,0:T(8,128)S(1)} %constant_dynamic-update-slice_fusion.2.refs_2_), channel_id=1, source_target_pairs={{0,1},{1,0},{2,3},{3,2},{4,5},{5,4},{6,7},{7,6},{8,9},{9,8},{10,11... | collective-permute-start | bytes 589832 | tf_op jit(solution)/shard_map/ppermute | solution.py:468

commit v5 on v4

--- a/solution.py
+++ b/solution.py
@@ -221,7 +221,6 @@
 
 
 def prepare_kernel(own_shape, *refs):
-    place_ref, refs = refs[0], refs[1:]
     given, outputs, held, semaphores = refs[:8], refs[8:15], refs[15:23], refs[23]
     contrast_ref, force_ref, last_contrast_ref, last_force_ref = outputs[:4]
     rows_ref, last_ref, mask_ref = outputs[4:]
@@ -251,8 +250,8 @@
             at = (n, source_z_ref[k], pl.ds(source_y_ref[k], 1), slice(None))
             force_ref[at] += jnp.where(lane == source_x_ref[k], wavelet_ref[n, k], 0.0)
     index = lax.broadcasted_iota(jnp.int32, (own + receivers, 1), 0)
-    row = (place_ref[0] * deep_count + lax.div(index, tall_count)) * tall
-    row += place_ref[1] * tall_count + lax.rem(index, tall_count)
+    row = (lax.axis_index("slab") * deep_count + lax.div(index, tall_count)) * tall
+    row += lax.axis_index("sub") * tall_count + lax.rem(index, tall_count)
     for j in range(receivers):
         row = jnp.where(index == own + j, receiver_z_ref[j] * tall + receiver_y_ref[j], row)
         mask_ref[pl.ds(j, 1), :] = jnp.where(lane == receiver_x_ref[j], 1.0, 0.0)
@@ -282,7 +281,6 @@
 def step_kernel(
     layout,
     own_shape,
-    place_ref,
     contrast_ref,
     force_ref,
     last_contrast_ref,
@@ -293,9 +291,16 @@
     wide_ref,
     *refs,
 ):
-    blocks, refs = refs[:-11], refs[-11:]
-    incident_ref, scattered_ref, traces_ref = refs[:3]
-    field_ref, speed_ref, drive_ref, wave_ref, parts_ref, product_ref, taken_ref, slim_ref = refs[3:]
+    blocks, refs = refs[:-15], refs[-15:]
+    outputs = refs[:3]
+    field_ref, speed_ref, drive_ref, wave_ref, parts_ref, product_ref, taken_ref, slim_ref = refs[3:11]
+    incident_ref, scattered_ref, traces_ref, semaphores = refs[11:]
+    copies = []
+
+    def send(source, target):
+        copies.append(pltpu.make_async_copy(source, target, semaphores.at[len(copies)]))
+        copies[-1].start()
+
     deep, tall, wide = speed_ref.shape
     deep_count, tall_count, part_width = own_shape
     own = deep_count * tall_count
@@ -304,7 +309,7 @@
     runs, block = rows_ref.shape[0], rows_ref.shape[2] // 3
     run = block // tall
     group = min(run, CHUNK)
-    slab, sub, rep = (place_ref[i] for i in range(3))
+    slab, sub, rep = (lax.axis_index(axis) for axis in ("slab", "sub", "rep"))
 
     for number, layer, what, x, y, z in layout:
         half = rep ^ x
@@ -427,40 +432,56 @@
         for i in range(len(work) + runs):
             if i < len(work):
                 work[i][0](*work[i][1])
+            if i == len(work) and n == STEPS - 2:
+                incident_result = chosen(0, slice(None), 3)
             if i >= runs:
                 after[i - runs][0](*after[i - runs][1])
         for r in range(replicas):
             samples[n - 1][r] = sum(taken_ref[1 + r, number] for number in each)
 
+    wave_results = [chosen(1 + r, slice(None), WAVE_PARTS) for r in range(replicas)]
     receiver_rows = slice(own + receivers, own + 2 * receivers)
     speed = jnp.concatenate([owned(speed_ref), chosen(1 + replicas, receiver_rows, 3)], axis=0)
 
-    def last_applied(slot, mine, count):
-        result = chosen(slot, slice(None), count)
-        here = jnp.concatenate([mine, result[own + receivers :]], axis=0)
+    def last_field(result, mine):
+        return jnp.concatenate([mine, result[own + receivers :]], axis=0)
+
+    def last_applied(result, here, count):
         total = (3.0 * whole_coeffs[0]) * here + result[: own + receivers]
-        beside = jnp.concatenate(split(here, count), axis=1)
-        return total + product(beside, wide_ref[: count * wide]), here
-
-    result, now = last_applied(0, owned(field_ref, 0), 3)
-    drive = speed * result + last_force_ref[...]
+        return total + product(jnp.concatenate(split(here, count), axis=1), wide_ref[: count * wide])
+
+    column = lax.broadcasted_iota(jnp.int32, (receivers, 128), 1)
+    mask = mask_ref[...]
+
+    def recorded(n):
+        total = jnp.zeros((receivers, 128), jnp.float32)
+        for r in range(replicas):
+            summed = jnp.sum(samples[n][r] * mask, axis=1, keepdims=True)
+            total += jnp.where(column == n * replicas + r, summed, 0.0)
+        return total
+
+    now = last_field(incident_result, owned(field_ref, 0))
+    waves = [last_field(wave_results[r], owned(wave_ref, r, 2)) for r in range(replicas)]
+    incident_result = last_applied(incident_result, now, 3)
+    wave_results = [last_applied(wave_results[r], waves[r], WAVE_PARTS) for r in range(replicas)]
+    for r in range(replicas):
+        samples[2][r] = waves[r][own:]
+    gathered = recorded(0) + recorded(1) + recorded(2)
+    drive = speed * incident_result + last_force_ref[...]
     slim_ref[...] = 2.0 * now[:own] - owned(field_ref, 3) + drive[:own]
     incident_ref[...] = slim_ref[:, pl.ds(at_x, part_width)].reshape(incident_ref.shape)
+    send(incident_ref, outputs[0])
     for r in range(replicas):
-        result, wave = last_applied(1 + r, owned(wave_ref, r, 2), WAVE_PARTS)
-        samples[2][r] = wave[own:]
         before = jnp.concatenate([owned(wave_ref, r, 1), samples[1][r]], axis=0)
-        following = 2.0 * wave - before + speed * result + last_contrast_ref[r] * drive
+        following = 2.0 * waves[r] - before + speed * wave_results[r] + last_contrast_ref[r] * drive
         scattered_ref[r] = following[:own].reshape(scattered_ref.shape[1:])
+        send(scattered_ref.at[r], outputs[1].at[r])
         samples[3][r] = following[own:]
-    column = lax.broadcasted_iota(jnp.int32, (receivers, 128), 1)
-    gathered = jnp.zeros((receivers, 128), jnp.float32)
-    mask = mask_ref[...]
-    for n in range(STEPS):
-        for r in range(replicas):
-            summed = jnp.sum(samples[n][r] * mask, axis=1, keepdims=True)
-            gathered += jnp.where(column == n * replicas + r, summed, 0.0)
+    gathered += recorded(3)
     traces_ref[...] = jnp.transpose(gathered)[: STEPS * replicas, :]
+    send(traces_ref, outputs[2])
+    for copy in copies:
+        copy.wait()
 
 
 def swapped(array, axis, distance):
@@ -512,7 +533,6 @@
 ):
     deep_count, tall_count, part_width = incident_now.shape
     wide = courant.shape[2]
-    slab, sub, rep = (lax.axis_index(axis) for axis in ("slab", "sub", "rep"))
     deep, tall = lax.axis_size("slab") * deep_count, lax.axis_size("sub") * tall_count
     rows = deep * tall
     replicas, receivers = replica_seeds.shape[0], receiver_z.shape[0]
@@ -520,24 +540,22 @@
     cube = (deep, tall, wide)
     last_rows = deep_count * tall_count + receivers
     block = min(rows, 256)
-    smem = pl.BlockSpec(memory_space=pltpu.SMEM)
     vmem = pl.BlockSpec(memory_space=pltpu.VMEM)
     anywhere = pl.BlockSpec(memory_space=pltpu.HBM)
 
     def held(*shape, dtype=jnp.float32):
         return jax.ShapeDtypeStruct(shape, dtype)
 
-    def call(kernel, out_shape, scalars, distant, arrays, scratch):
+    def call(kernel, out_shape, distant, arrays, scratch, out_space=vmem):
         return pl.pallas_call(
             kernel,
             out_shape=out_shape,
-            in_specs=[smem] * len(scalars) + [anywhere] * len(distant) + [vmem] * len(arrays),
-            out_specs=tuple(vmem for _ in out_shape),
+            in_specs=[anywhere] * len(distant) + [vmem] * len(arrays),
+            out_specs=tuple(out_space for _ in out_shape),
             scratch_shapes=list(scratch),
             compiler_params=pltpu.CompilerParams(vmem_limit_bytes=24 * 2**20),
-        )(*scalars, *(pltpu.with_memory_space_constraint(a, pltpu.HBM) for a in distant), *arrays)
-
-    place = jnp.stack([slab, sub, rep]).astype(jnp.int32)
+        )(*(pltpu.with_memory_space_constraint(a, pltpu.HBM) for a in distant), *arrays)
+
     given = (
         wavelet,
         source_z,
@@ -559,7 +577,6 @@
             held(last_rows + receivers, 3 * rows, dtype=jnp.bfloat16),
             held(receivers, wide),
         ),
-        (place,),
         given,
         (),
         (
@@ -567,11 +584,10 @@
             pltpu.SemaphoreType.DMA((len(given),)),
         ),
     )
-    matrices = call(beside_kernel, (held(3 * wide, wide, dtype=jnp.bfloat16),), (), (), (), ())
+    matrices = call(beside_kernel, (held(3 * wide, wide, dtype=jnp.bfloat16),), (), (), ())
     own = call(
         pack_kernel,
         (held(4 * deep_count, tall_count, part_width),),
-        (),
         (incident_now, incident_prev, courant),
         (),
         (pltpu.SemaphoreType.DMA((4,)),),
@@ -584,7 +600,6 @@
             held(replicas, deep_count, tall_count, wide),
             held(STEPS * replicas, receivers),
         ),
-        (place,),
         (),
         (*prepared, *blocks),
         (
@@ -596,7 +611,12 @@
             pltpu.VMEM((1 + replicas, rows // block, block, wide), jnp.float32),
             pltpu.VMEM((1 + replicas, rows // block, receivers, wide), jnp.float32),
             pltpu.VMEM((deep_count * tall_count, wide), jnp.float32),
+            pltpu.VMEM(own_shape, jnp.float32),
+            pltpu.VMEM((replicas, deep_count, tall_count, wide), jnp.float32),
+            pltpu.VMEM((STEPS * replicas, receivers), jnp.float32),
+            pltpu.SemaphoreType.DMA((2 + replicas,)),
         ),
+        anywhere,
     )
     return incident_final, scattered_final, traces.reshape(STEPS, replicas, receivers)
 

time: 27.8 us -> 26.3 us (0.946)
  Pallas kernels: 9.89 us -> 8.3 us
    pallas_call x4, Pallas kernels: 9.89 us -> 8.3 us  [call(): pl.pallas_call(kernel, out_shape=out_shape, in_specs=[anywhere] * len(dis...]
  transfers between devices with their start and end apart: 9 -> 9, of which waited for: 7 -> 7; matrix products, arithmetic and copies ran while one was open for 1% -> 0% of each run, Pallas kernels for 11% -> 9%
where the time goes in v5:
time: 26.3 us; the launch traced here: 26.1 us
  starting transfers between devices  9.64 us (37%)
  Pallas kernels  8.3 us (32%)
  waiting for transfers between devices  7.37 us (28%)
  between operations  0.72 us (3%)
    ppermute x9, starting transfers between devices, swapped(): return lax.ppermute(array, axis, [(i, i ^ distance) for i in range(size)])  9.64 us
    pallas_call x4, Pallas kernels, call(): pl.pallas_call(kernel, out_shape=out_shape, in_specs=[anywhere] * len(dis...  8.3 us
    ppermute x9, waiting for transfers between devices, swapped(): return lax.ppermute(array, axis, [(i, i ^ distance) for i in range(size)])  7.37 us
  transfers between devices with their start and end apart: 9, of which 7 were waited for; matrix products, arithmetic and copies ran while one was open for 0% of the time, Pallas kernels for 9%

profile of v5, /device:TPU:0, one launch (start us, length us, event | category | flops | bytes accessed | tf_op | source)
XLA Modules:
  0.0 26.1 jit_solution(10598036991486937162)
XLA Ops:
  0.6 0.8 %shard_map.130 = f32[16,16,128]{2,1,0:T(8,128)S(1)} custom-call(f32[4,16,128]{2,1,0:T(8,128)} %now_ref.1, f32[4,16,128]{2,1,0:T(8,128)} %prev_ref.1, f32[4,16,256]{2,1,0:T(8,128)} %courant_ref.1), custom_call_target="tpu_custom_call" | custom-call | tf_op jit(solution)/shard_map/pallas_call | solution.py:550
  1.5 4.1 %collective-permute-start.2 = (f32[12,16,128]{2,1,0:T(8,128)S(1)}, f32[12,16,128]{2,1,0:T(8,128)S(1)}, u32[]{:S(2)}, u32[]{:S(2)}) collective-permute-start(f32[12,16,128]{2,1,0:T(8,128)S(1)} %slice.13), channel_id=1, source_target_pairs={{0,8},{4,12},{8,0},{12,4},{1,9},{5,13},{9,1},{13,5},{2,10},{6,14},... | collective-permute-start | bytes 294920 | tf_op jit(solution)/shard_map/ppermute | solution.py:489
  5.6 1.6 %collective-permute-start = (f32[12,16,128]{2,1,0:T(8,128)S(1)}, f32[12,16,128]{2,1,0:T(8,128)S(1)}, u32[]{:S(2)}, u32[]{:S(2)}) collective-permute-start(f32[12,16,128]{2,1,0:T(8,128)S(1)} %slice.13), channel_id=1, source_target_pairs={{0,4},{4,0},{8,12},{12,8},{1,5},{5,1},{9,13},{13,9},{2,6},{6,2},{1... | collective-permute-start | bytes 294920 | tf_op jit(solution)/shard_map/ppermute | solution.py:489
  7.2 0.1 shard_map.132.wide_ref
  7.2 0.1 collective-permute-start.4
  7.3 2.4 %shard_map.131 = (f32[2,16,32,256]{3,2,1,0:T(8,128)S(1)}, f32[3,16,32,256]{3,2,1,0:T(8,128)S(1)}, f32[2,96,256]{2,1,0:T(8,128)S(1)}, f32[96,256]{1,0:T(8,128)S(1...) custom-call(f32[4,8]{1,0:T(4,128)} %refs_0_.1, s32[8]{0:T(128)} %refs_1_.1, ...), custom_call_target="tpu_custom_call" | custom-call | tf_op jit(solution)/shard_map/pallas_call | solution.py:550
  9.8 1.0 %collective-permute-done = f32[12,16,128]{2,1,0:T(8,128)S(1)} collective-permute-done((f32[12,16,128]{2,1,0:T(8,128)S(1)}, f32[12,16,128]{2,1,0:T(8,128)S(1)}, u32[]{:S(2)}, u32[]{:S(2)}) %collective-permute-start) | collective-permute-done | bytes 98336 | tf_op jit(solution)/shard_map/ppermute | solution.py:489
  10.7 1.6 %collective-permute-start.1 = (f32[20,16,128]{2,1,0:T(8,128)S(1)}, f32[20,16,128]{2,1,0:T(8,128)S(1)}, u32[]{:S(2)}, u32[]{:S(2)}) collective-permute-start(f32[20,16,128]{2,1,0:T(8,128)S(1)} %pad_maximum_fusion.1), channel_id=1, source_target_pairs={{0,2},{2,0},{1,3},{3,1},{4,6},{6,4},{5,7},{7,5},{8,10},{10,8},{9,1... | collective-permute-start | bytes 491528 | tf_op jit(solution)/shard_map/ppermute | solution.py:489
  12.3 0.0 collective-permute-done.2
  12.3 0.7 %collective-permute-start.3 = (f32[12,16,128]{2,1,0:T(8,128)S(1)}, f32[12,16,128]{2,1,0:T(8,128)S(1)}, u32[]{:S(2)}, u32[]{:S(2)}) collective-permute-start(f32[12,16,128]{2,1,0:T(8,128)S(1)} %collective-permute-done.2), channel_id=1, source_target_pairs={{0,2},{2,0},{1,3},{3,1},{4,6},{6,4},{5,7},{7,5},{8,10},{10,8},{9,1... | collective-permute-start | bytes 294920 | tf_op jit(solution)/shard_map/ppermute | solution.py:489
  13.0 0.8 %collective-permute-done.4 = f32[12,16,128]{2,1,0:T(8,128)S(1)} collective-permute-done((f32[12,16,128]{2,1,0:T(8,128)S(1)}, f32[12,16,128]{2,1,0:T(8,128)S(1)}, u32[]{:S(2)}, u32[]{:S(2)}) %collective-permute-start.4) | collective-permute-done | bytes 98336 | tf_op jit(solution)/shard_map/ppermute | solution.py:489
  13.8 1.5 %collective-permute-start.5 = (f32[12,16,128]{2,1,0:T(8,128)S(1)}, f32[12,16,128]{2,1,0:T(8,128)S(1)}, u32[]{:S(2)}, u32[]{:S(2)}) collective-permute-start(f32[12,16,128]{2,1,0:T(8,128)S(1)} %collective-permute-done.4), channel_id=1, source_target_pairs={{0,2},{2,0},{1,3},{3,1},{4,6},{6,4},{5,7},{7,5},{8,10},{10,8},{9,1... | collective-permute-start | bytes 294920 | tf_op jit(solution)/shard_map/ppermute | solution.py:489
  15.3 2.2 %collective-permute-done.1 = f32[20,16,128]{2,1,0:T(8,128)S(1)} collective-permute-done((f32[20,16,128]{2,1,0:T(8,128)S(1)}, f32[20,16,128]{2,1,0:T(8,128)S(1)}, u32[]{:S(2)}, u32[]{:S(2)}) %collective-permute-start.1) | collective-permute-done | bytes 163872 | tf_op jit(solution)/shard_map/ppermute | solution.py:489
  17.5 0.1 collective-permute-start.6
  17.6 0.9 %collective-permute-done.3 = f32[12,16,128]{2,1,0:T(8,128)S(1)} collective-permute-done((f32[12,16,128]{2,1,0:T(8,128)S(1)}, f32[12,16,128]{2,1,0:T(8,128)S(1)}, u32[]{:S(2)}, u32[]{:S(2)}) %collective-permute-start.3) | collective-permute-done | bytes 98336 | tf_op jit(solution)/shard_map/ppermute | solution.py:489
  18.6 0.1 collective-permute-start.7
  18.6 1.0 %collective-permute-done.5 = f32[12,16,128]{2,1,0:T(8,128)S(1)} collective-permute-done((f32[12,16,128]{2,1,0:T(8,128)S(1)}, f32[12,16,128]{2,1,0:T(8,128)S(1)}, u32[]{:S(2)}, u32[]{:S(2)}) %collective-permute-start.5) | collective-permute-done | bytes 98336 | tf_op jit(solution)/shard_map/ppermute | solution.py:489
  19.6 0.1 collective-permute-start.8
  19.7 0.4 %collective-permute-done.7.refs_4_ = f32[24,16,128]{2,1,0:T(8,128)S(1)} collective-permute-done((f32[24,16,128]{2,1,0:T(8,128)S(1)}, f32[24,16,128]{2,1,0:T(8,128)S(1)}, u32[]{:S(2)}, u32[]{:S(2)}) %collective-permute-start.7) | collective-permute-done | bytes 196640 | tf_op jit(solution)/shard_map/ppermute | solution.py:489
  20.1 1.1 %collective-permute-done.8.refs_5_ = f32[24,16,128]{2,1,0:T(8,128)S(1)} collective-permute-done((f32[24,16,128]{2,1,0:T(8,128)S(1)}, f32[24,16,128]{2,1,0:T(8,128)S(1)}, u32[]{:S(2)}, u32[]{:S(2)}) %collective-permute-start.8) | collective-permute-done | bytes 196640 | tf_op jit(solution)/shard_map/ppermute | solution.py:489
  21.1 0.0 collective-permute-done.6.refs_3_
  21.1 5.0 %shard_map.133 = (f32[4,16,128]{2,1,0:T(8,128)}, f32[2,4,16,256]{3,2,1,0:T(8,128)}, f32[8,32]{1,0:T(8,128)}) custom-call(f32[2,16,32,256]{3,2,1,0:T(8,128)S(1)} %get-tuple-element.30.contrast_ref, f32[3,16,32,256]{3,2,1,0:T(8,128)S(1)} %get-tuple-element.31.force_ref, f32[2,96,256]{2,1,0:T(8,128)S(1)} %get-tuple-element.32.last_contrast_ref, ...), custom_call_target="tpu_custom_call" | custom-call | tf_op jit(solution)/shard_map/pallas_call | solution.py:550
  (8 shorter events, 0.1 us)
Async XLA Ops:
  1.5 10.8 %collective-permute-start.2 = (f32[12,16,128]{2,1,0:T(8,128)S(1)}, f32[12,16,128]{2,1,0:T(8,128)S(1)}, u32[]{:S(2)}, u32[]{:S(2)}) collective-permute-start(f32[12,16,128]{2,1,0:T(8,128)S(1)} %slice.13), channel_id=1, source_target_pairs={{0,8},{4,12},{8,0},{12,4},{1,9},{5,13},{9,1},{13,5},{2,10},{6,14},... | collective-permute-start | bytes 294920 | tf_op jit(solution)/shard_map/ppermute | solution.py:489
  5.6 5.1 %collective-permute-start = (f32[12,16,128]{2,1,0:T(8,128)S(1)}, f32[12,16,128]{2,1,0:T(8,128)S(1)}, u32[]{:S(2)}, u32[]{:S(2)}) collective-permute-start(f32[12,16,128]{2,1,0:T(8,128)S(1)} %slice.13), channel_id=1, source_target_pairs={{0,4},{4,0},{8,12},{12,8},{1,5},{5,1},{9,13},{13,9},{2,6},{6,2},{1... | collective-permute-start | bytes 294920 | tf_op jit(solution)/shard_map/ppermute | solution.py:489
  7.2 6.6 %collective-permute-start.4 = (f32[12,16,128]{2,1,0:T(8,128)S(1)}, f32[12,16,128]{2,1,0:T(8,128)S(1)}, u32[]{:S(2)}, u32[]{:S(2)}) collective-permute-start(f32[12,16,128]{2,1,0:T(8,128)S(1)} %slice.13), channel_id=1, source_target_pairs={{0,12},{4,8},{8,4},{12,0},{1,13},{5,9},{9,5},{13,1},{2,14},{6,10},... | collective-permute-start | bytes 294920 | tf_op jit(solution)/shard_map/ppermute | solution.py:489
  10.7 6.8 %collective-permute-start.1 = (f32[20,16,128]{2,1,0:T(8,128)S(1)}, f32[20,16,128]{2,1,0:T(8,128)S(1)}, u32[]{:S(2)}, u32[]{:S(2)}) collective-permute-start(f32[20,16,128]{2,1,0:T(8,128)S(1)} %pad_maximum_fusion.1), channel_id=1, source_target_pairs={{0,2},{2,0},{1,3},{3,1},{4,6},{6,4},{5,7},{7,5},{8,10},{10,8},{9,1... | collective-permute-start | bytes 491528 | tf_op jit(solution)/shard_map/ppermute | solution.py:489
  12.3 6.2 %collective-permute-start.3 = (f32[12,16,128]{2,1,0:T(8,128)S(1)}, f32[12,16,128]{2,1,0:T(8,128)S(1)}, u32[]{:S(2)}, u32[]{:S(2)}) collective-permute-start(f32[12,16,128]{2,1,0:T(8,128)S(1)} %collective-permute-done.2), channel_id=1, source_target_pairs={{0,2},{2,0},{1,3},{3,1},{4,6},{6,4},{5,7},{7,5},{8,10},{10,8},{9,1... | collective-permute-start | bytes 294920 | tf_op jit(solution)/shard_map/ppermute | solution.py:489
  13.8 5.8 %collective-permute-start.5 = (f32[12,16,128]{2,1,0:T(8,128)S(1)}, f32[12,16,128]{2,1,0:T(8,128)S(1)}, u32[]{:S(2)}, u32[]{:S(2)}) collective-permute-start(f32[12,16,128]{2,1,0:T(8,128)S(1)} %collective-permute-done.4), channel_id=1, source_target_pairs={{0,2},{2,0},{1,3},{3,1},{4,6},{6,4},{5,7},{7,5},{8,10},{10,8},{9,1... | collective-permute-start | bytes 294920 | tf_op jit(solution)/shard_map/ppermute | solution.py:489
  17.5 3.6 %collective-permute-start.6 = (f32[48,16,128]{2,1,0:T(8,128)S(1)}, f32[48,16,128]{2,1,0:T(8,128)S(1)}, u32[]{:S(2)}, u32[]{:S(2)}) collective-permute-start(f32[48,16,128]{2,1,0:T(8,128)S(1)} %pad_maximum_fusion.refs_0_), channel_id=1, source_target_pairs={{0,1},{1,0},{2,3},{3,2},{4,5},{5,4},{6,7},{7,6},{8,9},{9,8},{10,11... | collective-permute-start | bytes 1179656 | tf_op jit(solution)/shard_map/ppermute | solution.py:489
  18.6 1.5 %collective-permute-start.7 = (f32[24,16,128]{2,1,0:T(8,128)S(1)}, f32[24,16,128]{2,1,0:T(8,128)S(1)}, u32[]{:S(2)}, u32[]{:S(2)}) collective-permute-start(f32[24,16,128]{2,1,0:T(8,128)S(1)} %constant_dynamic-update-slice_fusion.refs_1_), channel_id=1, source_target_pairs={{0,1},{1,0},{2,3},{3,2},{4,5},{5,4},{6,7},{7,6},{8,9},{9,8},{10,11... | collective-permute-start | bytes 589832 | tf_op jit(solution)/shard_map/ppermute | solution.py:489
  19.6 1.5 %collective-permute-start.8 = (f32[24,16,128]{2,1,0:T(8,128)S(1)}, f32[24,16,128]{2,1,0:T(8,128)S(1)}, u32[]{:S(2)}, u32[]{:S(2)}) collective-permute-start(f32[24,16,128]{2,1,0:T(8,128)S(1)} %constant_dynamic-update-slice_fusion.2.refs_2_), channel_id=1, source_target_pairs={{0,1},{1,0},{2,3},{3,2},{4,5},{5,4},{6,7},{7,6},{8,9},{9,8},{10,11... | collective-permute-start | bytes 589832 | tf_op jit(solution)/shard_map/ppermute | solution.py:489

commit v6 on v5

--- a/solution.py
+++ b/solution.py
@@ -496,19 +496,21 @@
     beyond[3] = swapped(late, "slab", 3)
     near = jnp.concatenate([own[: 2 * deep_count], beyond[1]], axis=0)
     near_two, two_two = swapped(near, "rep", 1), swapped(beyond[2], "rep", 1)
-    near_two, prepared = lax.optimization_barrier((near_two, prepared))
+    line = jnp.concatenate([own[2 * deep_count :], near, near_two], axis=0)
+    line, prepared = lax.optimization_barrier((line, prepared))
     three_two = swapped(beyond[3], "rep", 1)
     blocks = [
-        jnp.concatenate([near, near_two, own[2 * deep_count :]], axis=0),
+        line,
         jnp.concatenate([beyond[2], two_two], axis=0),
-        jnp.concatenate([beyond[3], three_two], axis=0),
+        jnp.concatenate([three_two, beyond[3]], axis=0),
     ]
     blocks += [swapped(block, "sub", 1) for block in blocks]
     names = ("now", "prev", "courant")
     near_layout = [(name, 0) for name in names[:2]] + [(name, 1) for name in names]
-    layouts = [[(name, x, z) for x in range(2) for name, z in near_layout]]
-    layouts[0] += [("courant", x, 0) for x in range(2)]
-    layouts += [[(name, x, z) for x in range(2) for name in names] for z in (2, 3)]
+    layouts = [[("courant", x, 0) for x in range(2)]]
+    layouts[0] += [(name, x, z) for x in range(2) for name, z in near_layout]
+    layouts += [[(name, x, 2) for x in (0, 1) for name in names]]
+    layouts += [[(name, x, 3) for x in (1, 0) for name in names]]
     layout = [
         (len(layouts) * y + number, i * deep_count, name, x, y, z)
         for y in range(2)

time: 26.3 us -> 26.3 us (level)
  waiting for transfers between devices: 7.37 us -> 6.89 us
  starting transfers between devices: 9.64 us -> 10.1 us
    ppermute x9, starting transfers between devices: 9.64 us -> 10.1 us  [swapped(): return lax.ppermute(array, axis, [(i, i ^ distance) for i in range(size)])]
    ppermute x9, waiting for transfers between devices: 7.37 us -> 6.89 us  [swapped(): return lax.ppermute(array, axis, [(i, i ^ distance) for i in range(size)])]
  transfers between devices with their start and end apart: 9 -> 9, of which waited for: 7 -> 6; matrix products, arithmetic and copies ran while one was open for 0% -> 0% of each run, Pallas kernels for 9% -> 9%
where the time goes in v6:
time: 26.3 us; the launch traced here: 26.1 us
  starting transfers between devices  10.1 us (38%)
  Pallas kernels  8.3 us (32%)
  waiting for transfers between devices  6.89 us (26%)
  between operations  0.73 us (3%)
    ppermute x9, starting transfers between devices, swapped(): return lax.ppermute(array, axis, [(i, i ^ distance) for i in range(size)])  10.1 us
    pallas_call x4, Pallas kernels, call(): pl.pallas_call(kernel, out_shape=out_shape, in_specs=[anywhere] * len(dis...  8.3 us
    ppermute x9, waiting for transfers between devices, swapped(): return lax.ppermute(array, axis, [(i, i ^ distance) for i in range(size)])  6.89 us
  transfers between devices with their start and end apart: 9, of which 6 were waited for; matrix products, arithmetic and copies ran while one was open for 0% of the time, Pallas kernels for 9%

profile of v6, /device:TPU:0, one launch (start us, length us, event | category | flops | bytes accessed | tf_op | source)
XLA Modules:
  0.0 26.1 jit_solution(5551804171016576006)
XLA Ops:
  0.6 0.8 %shard_map.130 = f32[16,16,128]{2,1,0:T(8,128)S(1)} custom-call(f32[4,16,128]{2,1,0:T(8,128)} %now_ref.1, f32[4,16,128]{2,1,0:T(8,128)} %prev_ref.1, f32[4,16,256]{2,1,0:T(8,128)} %courant_ref.1), custom_call_target="tpu_custom_call" | custom-call | tf_op jit(solution)/shard_map/pallas_call | solution.py:552
  1.5 4.1 %collective-permute-start.2 = (f32[12,16,128]{2,1,0:T(8,128)S(1)}, f32[12,16,128]{2,1,0:T(8,128)S(1)}, u32[]{:S(2)}, u32[]{:S(2)}) collective-permute-start(f32[12,16,128]{2,1,0:T(8,128)S(1)} %slice.14), channel_id=1, source_target_pairs={{0,8},{4,12},{8,0},{12,4},{1,9},{5,13},{9,1},{13,5},{2,10},{6,14},... | collective-permute-start | bytes 294920 | tf_op jit(solution)/shard_map/ppermute | solution.py:489
  5.6 1.6 %collective-permute-start = (f32[12,16,128]{2,1,0:T(8,128)S(1)}, f32[12,16,128]{2,1,0:T(8,128)S(1)}, u32[]{:S(2)}, u32[]{:S(2)}) collective-permute-start(f32[12,16,128]{2,1,0:T(8,128)S(1)} %slice.14), channel_id=1, source_target_pairs={{0,4},{4,0},{8,12},{12,8},{1,5},{5,1},{9,13},{13,9},{2,6},{6,2},{1... | collective-permute-start | bytes 294920 | tf_op jit(solution)/shard_map/ppermute | solution.py:489
  7.2 0.1 shard_map.132.wide_ref
  7.2 0.1 collective-permute-start.4
  7.3 2.4 %shard_map.131 = (f32[2,16,32,256]{3,2,1,0:T(8,128)S(1)}, f32[3,16,32,256]{3,2,1,0:T(8,128)S(1)}, f32[2,96,256]{2,1,0:T(8,128)S(1)}, f32[96,256]{1,0:T(8,128)S(1...) custom-call(f32[4,8]{1,0:T(4,128)} %refs_0_.1, s32[8]{0:T(128)} %refs_1_.1, ...), custom_call_target="tpu_custom_call" | custom-call | tf_op jit(solution)/shard_map/pallas_call | solution.py:552
  9.8 1.0 %collective-permute-done = f32[12,16,128]{2,1,0:T(8,128)S(1)} collective-permute-done((f32[12,16,128]{2,1,0:T(8,128)S(1)}, f32[12,16,128]{2,1,0:T(8,128)S(1)}, u32[]{:S(2)}, u32[]{:S(2)}) %collective-permute-start) | collective-permute-done | bytes 98336 | tf_op jit(solution)/shard_map/ppermute | solution.py:489
  10.7 1.6 %collective-permute-start.1 = (f32[20,16,128]{2,1,0:T(8,128)S(1)}, f32[20,16,128]{2,1,0:T(8,128)S(1)}, u32[]{:S(2)}, u32[]{:S(2)}) collective-permute-start(f32[20,16,128]{2,1,0:T(8,128)S(1)} %pad_maximum_fusion.1), channel_id=1, source_target_pairs={{0,2},{2,0},{1,3},{3,1},{4,6},{6,4},{5,7},{7,5},{8,10},{10,8},{9,1... | collective-permute-start | bytes 491528 | tf_op jit(solution)/shard_map/ppermute | solution.py:489
  12.3 0.0 collective-permute-done.2
  12.3 0.7 %collective-permute-start.3 = (f32[12,16,128]{2,1,0:T(8,128)S(1)}, f32[12,16,128]{2,1,0:T(8,128)S(1)}, u32[]{:S(2)}, u32[]{:S(2)}) collective-permute-start(f32[12,16,128]{2,1,0:T(8,128)S(1)} %collective-permute-done.2), channel_id=1, source_target_pairs={{0,2},{2,0},{1,3},{3,1},{4,6},{6,4},{5,7},{7,5},{8,10},{10,8},{9,1... | collective-permute-start | bytes 294920 | tf_op jit(solution)/shard_map/ppermute | solution.py:489
  13.0 0.8 %collective-permute-done.4 = f32[12,16,128]{2,1,0:T(8,128)S(1)} collective-permute-done((f32[12,16,128]{2,1,0:T(8,128)S(1)}, f32[12,16,128]{2,1,0:T(8,128)S(1)}, u32[]{:S(2)}, u32[]{:S(2)}) %collective-permute-start.4) | collective-permute-done | bytes 98336 | tf_op jit(solution)/shard_map/ppermute | solution.py:489
  13.8 1.5 %collective-permute-start.5 = (f32[12,16,128]{2,1,0:T(8,128)S(1)}, f32[12,16,128]{2,1,0:T(8,128)S(1)}, u32[]{:S(2)}, u32[]{:S(2)}) collective-permute-start(f32[12,16,128]{2,1,0:T(8,128)S(1)} %collective-permute-done.4), channel_id=1, source_target_pairs={{0,2},{2,0},{1,3},{3,1},{4,6},{6,4},{5,7},{7,5},{8,10},{10,8},{9,1... | collective-permute-start | bytes 294920 | tf_op jit(solution)/shard_map/ppermute | solution.py:489
  15.3 3.3 %collective-permute-done.3 = f32[12,16,128]{2,1,0:T(8,128)S(1)} collective-permute-done((f32[12,16,128]{2,1,0:T(8,128)S(1)}, f32[12,16,128]{2,1,0:T(8,128)S(1)}, u32[]{:S(2)}, u32[]{:S(2)}) %collective-permute-start.3) | collective-permute-done | bytes 98336 | tf_op jit(solution)/shard_map/ppermute | solution.py:489
  18.6 0.1 collective-permute-start.7
  18.6 0.0 collective-permute-done.1
  18.7 0.5 %collective-permute-start.6 = (f32[48,16,128]{2,1,0:T(8,128)S(1)}, f32[48,16,128]{2,1,0:T(8,128)S(1)}, u32[]{:S(2)}, u32[]{:S(2)}) collective-permute-start(f32[48,16,128]{2,1,0:T(8,128)S(1)} %pad_maximum_fusion.refs_0_), channel_id=1, source_target_pairs={{0,1},{1,0},{2,3},{3,2},{4,5},{5,4},{6,7},{7,6},{8,9},{9,8},{10,11... | collective-permute-start | bytes 1179656 | tf_op jit(solution)/shard_map/ppermute | solution.py:489
  19.2 0.4 %collective-permute-done.5 = f32[12,16,128]{2,1,0:T(8,128)S(1)} collective-permute-done((f32[12,16,128]{2,1,0:T(8,128)S(1)}, f32[12,16,128]{2,1,0:T(8,128)S(1)}, u32[]{:S(2)}, u32[]{:S(2)}) %collective-permute-start.5) | collective-permute-done | bytes 98336 | tf_op jit(solution)/shard_map/ppermute | solution.py:489
  19.6 0.1 collective-permute-start.8
  19.7 0.4 %collective-permute-done.7.refs_4_ = f32[24,16,128]{2,1,0:T(8,128)S(1)} collective-permute-done((f32[24,16,128]{2,1,0:T(8,128)S(1)}, f32[24,16,128]{2,1,0:T(8,128)S(1)}, u32[]{:S(2)}, u32[]{:S(2)}) %collective-permute-start.7) | collective-permute-done | bytes 196640 | tf_op jit(solution)/shard_map/ppermute | solution.py:489
  20.1 1.1 %collective-permute-done.8.refs_5_ = f32[24,16,128]{2,1,0:T(8,128)S(1)} collective-permute-done((f32[24,16,128]{2,1,0:T(8,128)S(1)}, f32[24,16,128]{2,1,0:T(8,128)S(1)}, u32[]{:S(2)}, u32[]{:S(2)}) %collective-permute-start.8) | collective-permute-done | bytes 196640 | tf_op jit(solution)/shard_map/ppermute | solution.py:489
  21.1 0.0 collective-permute-done.6.refs_3_
  21.1 5.0 %shard_map.133 = (f32[4,16,128]{2,1,0:T(8,128)}, f32[2,4,16,256]{3,2,1,0:T(8,128)}, f32[8,32]{1,0:T(8,128)}) custom-call(f32[2,16,32,256]{3,2,1,0:T(8,128)S(1)} %get-tuple-element.30.contrast_ref, f32[3,16,32,256]{3,2,1,0:T(8,128)S(1)} %get-tuple-element.31.force_ref, f32[2,96,256]{2,1,0:T(8,128)S(1)} %get-tuple-element.32.last_contrast_ref, ...), custom_call_target="tpu_custom_call" | custom-call | tf_op jit(solution)/shard_map/pallas_call | solution.py:552
  (8 shorter events, 0.1 us)
Async XLA Ops:
  1.5 10.8 %collective-permute-start.2 = (f32[12,16,128]{2,1,0:T(8,128)S(1)}, f32[12,16,128]{2,1,0:T(8,128)S(1)}, u32[]{:S(2)}, u32[]{:S(2)}) collective-permute-start(f32[12,16,128]{2,1,0:T(8,128)S(1)} %slice.14), channel_id=1, source_target_pairs={{0,8},{4,12},{8,0},{12,4},{1,9},{5,13},{9,1},{13,5},{2,10},{6,14},... | collective-permute-start | bytes 294920 | tf_op jit(solution)/shard_map/ppermute | solution.py:489
  5.6 5.1 %collective-permute-start = (f32[12,16,128]{2,1,0:T(8,128)S(1)}, f32[12,16,128]{2,1,0:T(8,128)S(1)}, u32[]{:S(2)}, u32[]{:S(2)}) collective-permute-start(f32[12,16,128]{2,1,0:T(8,128)S(1)} %slice.14), channel_id=1, source_target_pairs={{0,4},{4,0},{8,12},{12,8},{1,5},{5,1},{9,13},{13,9},{2,6},{6,2},{1... | collective-permute-start | bytes 294920 | tf_op jit(solution)/shard_map/ppermute | solution.py:489
  7.2 6.6 %collective-permute-start.4 = (f32[12,16,128]{2,1,0:T(8,128)S(1)}, f32[12,16,128]{2,1,0:T(8,128)S(1)}, u32[]{:S(2)}, u32[]{:S(2)}) collective-permute-start(f32[12,16,128]{2,1,0:T(8,128)S(1)} %slice.14), channel_id=1, source_target_pairs={{0,12},{4,8},{8,4},{12,0},{1,13},{5,9},{9,5},{13,1},{2,14},{6,10},... | collective-permute-start | bytes 294920 | tf_op jit(solution)/shard_map/ppermute | solution.py:489
  10.7 7.9 %collective-permute-start.1 = (f32[20,16,128]{2,1,0:T(8,128)S(1)}, f32[20,16,128]{2,1,0:T(8,128)S(1)}, u32[]{:S(2)}, u32[]{:S(2)}) collective-permute-start(f32[20,16,128]{2,1,0:T(8,128)S(1)} %pad_maximum_fusion.1), channel_id=1, source_target_pairs={{0,2},{2,0},{1,3},{3,1},{4,6},{6,4},{5,7},{7,5},{8,10},{10,8},{9,1... | collective-permute-start | bytes 491528 | tf_op jit(solution)/shard_map/ppermute | solution.py:489
  12.3 6.2 %collective-permute-start.3 = (f32[12,16,128]{2,1,0:T(8,128)S(1)}, f32[12,16,128]{2,1,0:T(8,128)S(1)}, u32[]{:S(2)}, u32[]{:S(2)}) collective-permute-start(f32[12,16,128]{2,1,0:T(8,128)S(1)} %collective-permute-done.2), channel_id=1, source_target_pairs={{0,2},{2,0},{1,3},{3,1},{4,6},{6,4},{5,7},{7,5},{8,10},{10,8},{9,1... | collective-permute-start | bytes 294920 | tf_op jit(solution)/shard_map/ppermute | solution.py:489
  13.8 5.8 %collective-permute-start.5 = (f32[12,16,128]{2,1,0:T(8,128)S(1)}, f32[12,16,128]{2,1,0:T(8,128)S(1)}, u32[]{:S(2)}, u32[]{:S(2)}) collective-permute-start(f32[12,16,128]{2,1,0:T(8,128)S(1)} %collective-permute-done.4), channel_id=1, source_target_pairs={{0,2},{2,0},{1,3},{3,1},{4,6},{6,4},{5,7},{7,5},{8,10},{10,8},{9,1... | collective-permute-start | bytes 294920 | tf_op jit(solution)/shard_map/ppermute | solution.py:489
  18.6 1.5 %collective-permute-start.7 = (f32[24,16,128]{2,1,0:T(8,128)S(1)}, f32[24,16,128]{2,1,0:T(8,128)S(1)}, u32[]{:S(2)}, u32[]{:S(2)}) collective-permute-start(f32[24,16,128]{2,1,0:T(8,128)S(1)} %constant_dynamic-update-slice_fusion.refs_1_), channel_id=1, source_target_pairs={{0,1},{1,0},{2,3},{3,2},{4,5},{5,4},{6,7},{7,6},{8,9},{9,8},{10,11... | collective-permute-start | bytes 589832 | tf_op jit(solution)/shard_map/ppermute | solution.py:489
  18.7 2.5 %collective-permute-start.6 = (f32[48,16,128]{2,1,0:T(8,128)S(1)}, f32[48,16,128]{2,1,0:T(8,128)S(1)}, u32[]{:S(2)}, u32[]{:S(2)}) collective-permute-start(f32[48,16,128]{2,1,0:T(8,128)S(1)} %pad_maximum_fusion.refs_0_), channel_id=1, source_target_pairs={{0,1},{1,0},{2,3},{3,2},{4,5},{5,4},{6,7},{7,6},{8,9},{9,8},{10,11... | collective-permute-start | bytes 1179656 | tf_op jit(solution)/shard_map/ppermute | solution.py:489
  19.6 1.5 %collective-permute-start.8 = (f32[24,16,128]{2,1,0:T(8,128)S(1)}, f32[24,16,128]{2,1,0:T(8,128)S(1)}, u32[]{:S(2)}, u32[]{:S(2)}) collective-permute-start(f32[24,16,128]{2,1,0:T(8,128)S(1)} %constant_dynamic-update-slice_fusion.2.refs_2_), channel_id=1, source_target_pairs={{0,1},{1,0},{2,3},{3,2},{4,5},{5,4},{6,7},{7,6},{8,9},{9,8},{10,11... | collective-permute-start | bytes 589832 | tf_op jit(solution)/shard_map/ppermute | solution.py:489
